TPU v7x, 256 devices: a whole 4x4x8 slice. The times are simulated.
256 devices in a mesh: lat: 16 (over z_lo, y), lon: 16 (over z_hi, x, core).
Axes of the slice: x: 4, y: 4, z: 8 (z_hi: 2, z_lo: 4; z = z_hi * 4 + z_lo), core: 2. Of those that a mesh axis runs over, the one named last changes fastest.
Arguments:
- cube_cells: bfloat16 [12288, 80, 128], P(('lat', 'lon')), may hold values from -6 to 6
- block_source: int32 [720, 16, 4], P('lat', 'lon'), may hold values from 0 to 767, as said below
- block_weight: bfloat16 [720, 16, 4, 90, 128], P('lat', 'lon'), may hold values from -0.25 to 0.25
- lift_in: bfloat16 [80, 256], replicated, may hold values from -0.625 to 0.625
- lift_out: bfloat16 [256, 256], replicated, may hold values from -0.375 to 0.375
- spectral: bfloat16 [384, 256, 256], P('lon'), may hold values from -1.5 to 1.5
Outputs:
- grid_field: bfloat16 [720, 1440, 256], P('lat', 'lon')
Inputs may be any that keep to these rules, and one draw needn't show every extreme that they name: `block_source`: for target row r in band i = r // 45 and longitude block J, every entry is a position among band i's 768 tiles lying cyclically within 24 positions below or above the positions J * 48 to (J + 1) * 48 - 1. In the first row of every band and block, the first entry is the lowest position of that range and the second the highest.
All inputs are finite; a program needn't handle non-finite values.
Results may differ from a plain program's by a relative error of at most 0.015.
Values may be sent and summed in bfloat16 or wider, within the bound.
No kernel may reach another device: no remote copies, remote signals or barrier semaphores. Data moves between devices by JAX's collectives and lax.ppermute only.
A program may use at most 192 MiB of HBM per device.

v0:
```python
import math

import jax
import jax.numpy as jnp
from jax import lax
from jax.sharding import PartitionSpec as P

NLAT = 720
NLON = 1440
L = 384
SRC_DEV = 48


unroll_steps = 16


def extended(cells, sides, width):
    for axis, dim in sides:
        count = lax.axis_size(axis)
        head = lax.slice_in_dim(cells, 0, width, axis=dim)
        tail = lax.slice_in_dim(cells, cells.shape[dim] - width, cells.shape[dim], axis=dim)
        cells = jnp.concatenate(
            [
                lax.ppermute(tail, axis, [(i, (i + 1) % count) for i in range(count)]),
                cells,
                lax.ppermute(head, axis, [((i + 1) % count, i) for i in range(count)]),
            ],
            axis=dim,
        )
    return cells


def legendre_setup(wave_orders):
    colatitude = (jnp.arange(NLAT, dtype=jnp.float32) + 0.5) * (math.pi / NLAT)
    cosine = jnp.cos(colatitude)[None, :]
    order_col = wave_orders.astype(jnp.float32)[:, None]
    log_scale = (
        0.5
        * (
            jnp.log(2.0 * order_col + 1.0)
            - math.log(4.0 * math.pi)
            + lax.lgamma(2.0 * order_col + 1.0)
            - 2.0 * lax.lgamma(order_col + 1.0)
            - order_col * math.log(4.0)
        )
        + order_col * jnp.log(jnp.sin(colatitude))[None, :]
    )
    initial = jnp.exp(jnp.minimum(log_scale + 80.0, 0.0))
    restore = jnp.exp(jnp.maximum(log_scale, -80.0))
    quadrature = jnp.sin(colatitude) * (math.pi / NLAT) * (2.0 * math.pi / NLON)
    return (cosine, order_col, initial, restore, quadrature)


def legendre_step(degree, current, earlier, cosine, order_col, initial):
    square = degree * degree
    rising = jnp.sqrt(
        jnp.maximum(4.0 * square - 1.0, 1.0) / jnp.maximum(square - order_col * order_col, 1.0)
    )
    shifted = (degree - 1.0) * (degree - 1.0)
    falling = jnp.sqrt(
        jnp.maximum(shifted - order_col * order_col, 0.0) / jnp.maximum(4.0 * shifted - 1.0, 1.0)
    )
    advanced = rising * (cosine * current - falling * earlier)
    return jnp.where(degree < order_col, 0.0, jnp.where(degree == order_col, initial, advanced))


def legendre_tables(wave_orders):
    cosine, order_col, initial, restore, quadrature = legendre_setup(wave_orders)

    def advance(carry, base_degree):
        current, earlier = carry
        stacked = []
        for offset in range(unroll_steps):
            latest = legendre_step(
                (base_degree + offset).astype(jnp.float32),
                current,
                earlier,
                cosine,
                order_col,
                initial,
            )
            earlier = current
            current = latest
            stacked.append(latest * restore)
        return ((current, earlier), jnp.stack(stacked))

    zeroed = jnp.zeros((wave_orders.shape[0], NLAT), jnp.float32)
    _, pieces = lax.scan(advance, (zeroed, zeroed), jnp.arange(0, L, unroll_steps, dtype=jnp.int32))
    table = pieces.reshape(L, wave_orders.shape[0], NLAT)
    return ((table * quadrature[None, None, :]).astype(jnp.bfloat16), table.astype(jnp.bfloat16))


def fourier_table(wave_orders):
    longitude = jnp.arange(NLON, dtype=jnp.int32)
    phase = longitude[:, None] * wave_orders[None, :] % NLON
    angle = phase.astype(jnp.float32) * (2.0 * math.pi / NLON)
    paired = jnp.stack([jnp.cos(angle), -jnp.sin(angle)], axis=2)
    return paired.reshape(NLON, 2 * wave_orders.shape[0])


def to_bands(values):
    return lax.all_to_all(values, "lat", split_axis=2, concat_axis=0, tiled=True)


def regroup(values):
    return lax.all_to_all(values, "lon", split_axis=3, concat_axis=1, tiled=True)


def analyse(table_part, data_part, first_block, block_width):
    order_count = table_part.shape[1]
    channel_count = data_part.shape[1]

    def fill_block(block_index, accumulated):
        table_block = lax.dynamic_slice_in_dim(
            table_part, block_index * block_width, block_width, 0
        )
        partial_value = jnp.einsum(
            "lmt,tcmp->mcpl", table_block, data_part, preferred_element_type=jnp.float32
        )
        return lax.dynamic_update_slice_in_dim(
            accumulated, partial_value, block_index * block_width, 3
        )

    zeroed = jnp.zeros((order_count, channel_count, 2, L), jnp.float32)
    return lax.fori_loop(first_block, L // block_width, fill_block, zeroed)


def synthesise(table_part, data_part, first_block, block_width):
    order_count = table_part.shape[1]
    channel_count = data_part.shape[3]

    def add_block(block_index, accumulated):
        table_block = lax.dynamic_slice_in_dim(
            table_part, block_index * block_width, block_width, 0
        )
        degree_rows = lax.dynamic_slice_in_dim(data_part, block_index * block_width, block_width, 1)
        return accumulated + jnp.einsum(
            "lmt,mlpd->mpdt", table_block, degree_rows, preferred_element_type=jnp.float32
        )

    zeroed = jnp.zeros((order_count, 2, channel_count, NLAT), jnp.float32)
    return lax.fori_loop(first_block, L // block_width, add_block, zeroed)


def shards(cube_cells, block_source, block_weight, lift_in, lift_out, spectral):
    lat_count = lax.axis_size("lat")
    lon_count = lax.axis_size("lon")
    lat_index = lax.axis_index("lat")
    lon_index = lax.axis_index("lon")
    block_width = min(128, L)
    rim_tiles = SRC_DEV // 2
    per_band = L // lat_count
    half_size = per_band // 2
    slot_index = jnp.arange(per_band, dtype=jnp.int32)[None, :]
    band_index = jnp.arange(lat_count, dtype=jnp.int32)[:, None]
    all_orders = band_index * per_band + slot_index
    column_orders = all_orders.reshape(lat_count * per_band)
    own_orders = lax.dynamic_index_in_dim(all_orders, lat_index, 0, keepdims=False)
    table_wide = fourier_table(column_orders)
    forward = table_wide.astype(jnp.bfloat16)
    widened = extended(cube_cells, (("lon", 0),), rim_tiles)
    band_tiles = lon_count * SRC_DEV
    offsets = (block_source[:, 0, :] - lon_index * SRC_DEV + rim_tiles) % band_tiles
    picked = widened[offsets]
    remapped = jnp.einsum(
        "rkts,rkcs->rtc", block_weight[:, 0], picked, preferred_element_type=jnp.float32
    ).astype(jnp.bfloat16)
    hidden = jax.nn.gelu(
        jnp.einsum("rtc,cd->rtd", remapped, lift_in, preferred_element_type=jnp.float32)
    ).astype(jnp.bfloat16)
    lifted = jnp.einsum("rtd,de->ret", hidden, lift_out, preferred_element_type=jnp.float32).astype(
        jnp.bfloat16
    )
    grid_rows = lax.all_to_all(lifted, "lon", split_axis=1, concat_axis=2, tiled=True)
    spectra = jnp.einsum(
        "rcl,lq->rcq", grid_rows, forward, preferred_element_type=jnp.float32
    ).astype(jnp.bfloat16)
    gathered = to_bands(spectra)
    channel_count = gathered.shape[1]
    gathered = gathered.reshape(NLAT, channel_count, per_band, 2)
    weighted, plain_table = legendre_tables(own_orders)
    sections = []
    for half_index in range(2):
        lowest = half_index * half_size
        first_block = own_orders[lowest] // block_width
        sections.append(
            analyse(
                weighted[:, lowest : lowest + half_size, :],
                gathered[:, :, lowest : lowest + half_size, :],
                first_block,
                block_width,
            )
        )
    analysis = jnp.concatenate(sections, axis=0).astype(jnp.bfloat16)
    by_degree = regroup(analysis)
    mixed_modes = jnp.einsum(
        "mcpl,lcd->mlpd", by_degree, spectral, preferred_element_type=jnp.float32
    ).astype(jnp.bfloat16)
    returned = regroup(mixed_modes)
    pieces = []
    for half_index in range(2):
        lowest = half_index * half_size
        first_block = own_orders[lowest] // block_width
        pieces.append(
            synthesise(
                plain_table[:, lowest : lowest + half_size, :],
                returned[lowest : lowest + half_size],
                first_block,
                block_width,
            )
        )
    synthesized = (
        jnp.concatenate(pieces, axis=0)
        .astype(jnp.bfloat16)
        .reshape(2 * per_band, channel_count, NLAT)
    )
    rows_back = to_bands(synthesized)
    factors = jnp.repeat(jnp.where(column_orders == 0, 1.0, 2.0), 2).astype(jnp.bfloat16)
    inverse = forward * factors[None, :]
    grid_field = jnp.einsum(
        "qcr,kq->rkc", rows_back, inverse, preferred_element_type=jnp.float32
    ).astype(jnp.bfloat16)
    return lax.all_to_all(grid_field, "lon", split_axis=1, concat_axis=2, tiled=True)


def solution(mesh):
    in_specs = (
        P(("lat", "lon"), None, None),
        P("lat", "lon", None),
        P("lat", "lon", None, None, None),
        P(),
        P(),
        P("lon", None, None),
    )
    out_specs = P("lat", "lon", None)
    return jax.shard_map(shards, mesh=mesh, in_specs=in_specs, out_specs=out_specs, check_vma=False)
```

profile of v0, /device:TPU:33, one launch (start us, length us, event | category | flops | bytes accessed | tf_op | source)
XLA Modules:
  0.0 1430.8 jit_solution(3272911625693670035)
XLA Ops:
  4.9 812.1 %while.65 = (s32[]{:T(128)}, f32[24,720]{1,0:T(8,128)S(1)}, f32[24,720]{1,0:T(8,128)S(1)}, f32[24,16,24,720]{3,2,1,0:T(8,128)}, s32[24]{0:T(128)S(1)}, /*index=5...) while((s32[]{:T(128)}, f32[24,720]{1,0:T(8,128)S(1)}, ...), condition=%wide.region_1.2_spmd.clone.clone.clone.clone, body=%wide.region_0.1_spmd.clone.clone.clone.clone.sunk | while | flops 6260049 | bytes 6709841 | solution.py:88
  824.2 27.2 %copy.130 = f32[384,24,720]{0,2,1:T(8,128)} copy(f32[384,24,720]{2,1,0:T(8,128)} %bitcast.435) | data formatting | bytes 53084160 | tf_op jit(solution)/shard_map/reshape | solution.py:89
  854.6 4.5 gather_fusion
  859.1 5.8 fusion.124
  865.0 4.3 convert_bitcast_fusion
  869.3 4.8 copy.133
  874.0 14.3 %all-to-all-start = ((bf16[45,256,90]{2,0,1:T(8,128)(2,1)}), bf16[45,256,90]{2,0,1:T(8,128)(2,1)}, u32[]{:S(2)}, u32[]{:S(2)}) async-start(bf16[45,256,90]{2,0,1:T(8,128)(2,1)} %copy.133), calls=%async_computation | async-start | bytes 6291456 | tf_op jit(solution)/shard_map/all_to_all | solution.py:174
  888.4 9.5 cosine_convert_fusion
  900.4 6.8 copy.136
  907.2 6.0 convert_element_type.277
  913.3 26.7 %fusion.160 = (bf16[384,24,720]{0,2,1:T(8,128)(2,1)}, bf16[384,24,720]{0,2,1:T(8,128)(2,1)}) fusion(f32[384,24,720]{0,2,1:T(8,128)} %copy.130, f32[720]{0:T(1024)S(1)} %fusion.137), kind=kLoop, calls=%fused_computation.267 | loop fusion | flops 19906560 | bytes 53087040 | tf_op jit(solution)/shard_map/convert_element_type | solution.py:90
  940.0 24.1 %all-to-all-done = bf16[45,256,90]{2,0,1:T(8,128)(2,1)} async-done(((bf16[45,256,90]{2,0,1:T(8,128)(2,1)}), bf16[45,256,90]{2,0,1:T(8,128)(2,1)}, u32[]{:S(2)}, u32[]{:S(2)}) %all-to-all-start) | async-done | bytes 2073632 | tf_op jit(solution)/shard_map/all_to_all | solution.py:174
  964.1 5.5 copy.135
  969.6 6.1 all_to_all.77
  975.7 5.2 fusion.121
  980.9 5.5 copy.138
  986.5 7.2 reshape.1473
  993.7 6.8 all-to-all-start.1
  1000.5 17.9 %fusion.161 = (bf16[384,12,720]{0,2,1:T(8,128)(2,1)}, bf16[384,12,720]{0,2,1:T(8,128)(2,1)}, bf16[384,12,720]{0,2,1:T(8,128)(2,1)}, bf16[384,12,720]{0,2,1:T(8,128)(2,1)}) fusion(bf16[384,24,720]{0,2,1:T(8,128)(2,1)} %get-tuple-element.651, bf16[384,24,720]{0,2,1:T(8,128)(2,1)} %get-tuple-element.652), kind=kLoop, calls=%fused_computation.268 | loop fusion | bytes 53084160 | tf_op jit(solution)/shard_map/slice | solution.py:206
  1018.4 7.7 all-to-all-done.1
  1026.1 10.2 reshape.1474
  1036.3 7.2 copy.184
  1043.5 5.6 reshape.1451
  1052.3 8.7 while.61
  1061.7 8.7 while.62
  1072.3 6.8 copy.140
  1079.1 6.5 reshape.1475
  1085.6 26.5 %all_to_all.102 = bf16[16,2,9216]{2,1,0:T(2,128)(2,1)} all-to-all(bf16[16,2,9216]{2,1,0:T(2,128)(2,1)} %reshape.1475), channel_id=1, replica_groups=mesh['lat'=16,'lon'=16] {'lon'}, dimensions={0} | all-to-all | bytes 1179648 | tf_op jit(solution)/shard_map/all_to_all | solution.py:106
  1112.1 7.0 reshape.1476
  1119.1 9.5 copy.141
  1128.6 6.9 all_to_all.84
  1138.1 7.1 copy.143
  1145.2 11.1 reshape.1477
  1156.3 19.9 %all_to_all.103 = bf16[16,2,9216]{2,1,0:T(2,128)(2,1)} all-to-all(bf16[16,2,9216]{2,1,0:T(2,128)(2,1)} %reshape.1477), channel_id=1, replica_groups=mesh['lat'=16,'lon'=16] {'lon'}, dimensions={0} | all-to-all | bytes 1179648 | tf_op jit(solution)/shard_map/all_to_all | solution.py:106
  1176.3 11.8 reshape.1478
  1188.1 12.6 copy.168
  1200.7 6.0 fusion.163
  1206.6 4.9 copy.145
  1216.2 11.7 while.63
  1216.2 3.9 fusion.193
  1220.1 3.9 fusion.193
  1224.0 3.9 fusion.193
  1230.1 4.9 copy.147
  1235.0 3.5 slice.58
  1239.6 11.7 while.64
  1239.6 3.9 fusion.196
  1243.5 3.9 fusion.196
  1247.4 3.9 fusion.196
  1254.8 6.2 copy.148
  1261.0 6.9 reshape.1479
  1268.0 7.8 all-to-all-start.4
  1275.8 6.8 copy.129
  1282.6 6.0 mul.1719
  1288.6 13.0 all-to-all-done.4
  1301.6 5.9 reshape.1480
  1307.4 4.2 copy.171
  1311.6 5.5 reshape.1471
  1317.1 5.4 fusion.104
  1322.5 8.3 copy.153
  1330.8 10.6 reshape.1481
  1341.4 61.9 %all_to_all.104 = bf16[16,2,32400]{2,1,0:T(2,128)(2,1)} all-to-all(bf16[16,2,32400]{2,1,0:T(2,128)(2,1)} %reshape.1481), channel_id=1, replica_groups=mesh['lat'=16,'lon'=16] {'lon'}, dimensions={0} | all-to-all | bytes 4147200 | tf_op jit(solution)/shard_map/all_to_all | solution.py:223
  1403.3 11.9 reshape.1482
  1415.2 10.6 copy.155
  1425.8 4.6 copy.156
  (1254 shorter events, 607.3 us)
Async XLA Ops:
  0.0 1135.5 %copy-start = (bf16[24,256,256]{2,1,0:T(8,128)(2,1)S(1)}, bf16[24,256,256]{2,1,0:T(8,128)(2,1)}, u32[]{:S(2)}) copy-start(bf16[24,256,256]{2,1,0:T(8,128)(2,1)} %param.21) | copy-start | bytes 9437188
  2.3 849.3 %collective-permute-start = (bf16[24,80,128]{2,1,0:T(8,128)(2,1)}, bf16[24,80,128]{2,1,0:T(8,128)(2,1)}, u32[]{:S(2)}, u32[]{:S(2)}) collective-permute-start(bf16[24,80,128]{2,1,0:T(8,128)(2,1)} %get-tuple-element.663), channel_id=1, source_target_pairs={{0,1},{1,2},{2,3},{3,4},{4,5},{5,6},{6,7},{7,8},{8,9},{9,10},{10,1... | collective-permute-start | bytes 1474568 | tf_op jit(solution)/shard_map/ppermute | solution.py:24
  4.1 847.5 %collective-permute-start.1 = (bf16[24,80,128]{2,1,0:T(8,128)(2,1)}, bf16[24,80,128]{2,1,0:T(8,128)(2,1)}, u32[]{:S(2)}, u32[]{:S(2)}) collective-permute-start(bf16[24,80,128]{2,1,0:T(8,128)(2,1)} %get-tuple-element.664), channel_id=1, source_target_pairs={{1,0},{2,1},{3,2},{4,3},{5,4},{6,5},{7,6},{8,7},{9,8},{10,9},{11,1... | collective-permute-start | bytes 1474568 | tf_op jit(solution)/shard_map/ppermute | solution.py:26
  4.9 11.6 copy-start.17
  4.9 12.4 copy-start.11
  4.9 17.8 %copy-start.5 = (f32[24,1]{0,1:T(1,128)}, f32[24,1]{0,1:T(1,128)S(1)}, u32[]{:S(2)}) copy-start(f32[24,1]{0,1:T(1,128)S(1)} %get-tuple-element.1060) | copy-start | bytes 292 | tf_op jit(solution)/shard_map/while
  38.7 11.6 copy-start.17
  38.7 12.4 copy-start.11
  38.7 17.8 %copy-start.5 = (f32[24,1]{0,1:T(1,128)}, f32[24,1]{0,1:T(1,128)S(1)}, u32[]{:S(2)}) copy-start(f32[24,1]{0,1:T(1,128)S(1)} %get-tuple-element.1060) | copy-start | bytes 292 | tf_op jit(solution)/shard_map/while
  72.6 11.6 copy-start.17
  72.6 12.4 copy-start.11
  72.6 17.8 %copy-start.5 = (f32[24,1]{0,1:T(1,128)}, f32[24,1]{0,1:T(1,128)S(1)}, u32[]{:S(2)}) copy-start(f32[24,1]{0,1:T(1,128)S(1)} %get-tuple-element.1060) | copy-start | bytes 292 | tf_op jit(solution)/shard_map/while
  106.4 11.6 copy-start.17
  106.4 12.4 copy-start.11
  106.4 17.8 %copy-start.5 = (f32[24,1]{0,1:T(1,128)}, f32[24,1]{0,1:T(1,128)S(1)}, u32[]{:S(2)}) copy-start(f32[24,1]{0,1:T(1,128)S(1)} %get-tuple-element.1060) | copy-start | bytes 292 | tf_op jit(solution)/shard_map/while
  140.2 11.6 copy-start.17
  140.2 12.4 copy-start.11
  140.2 17.8 %copy-start.5 = (f32[24,1]{0,1:T(1,128)}, f32[24,1]{0,1:T(1,128)S(1)}, u32[]{:S(2)}) copy-start(f32[24,1]{0,1:T(1,128)S(1)} %get-tuple-element.1060) | copy-start | bytes 292 | tf_op jit(solution)/shard_map/while
  174.0 11.6 copy-start.17
  174.1 12.4 copy-start.11
  174.1 17.8 %copy-start.5 = (f32[24,1]{0,1:T(1,128)}, f32[24,1]{0,1:T(1,128)S(1)}, u32[]{:S(2)}) copy-start(f32[24,1]{0,1:T(1,128)S(1)} %get-tuple-element.1060) | copy-start | bytes 292 | tf_op jit(solution)/shard_map/while
  207.8 11.6 copy-start.17
  207.9 12.4 copy-start.11
  207.9 17.8 %copy-start.5 = (f32[24,1]{0,1:T(1,128)}, f32[24,1]{0,1:T(1,128)S(1)}, u32[]{:S(2)}) copy-start(f32[24,1]{0,1:T(1,128)S(1)} %get-tuple-element.1060) | copy-start | bytes 292 | tf_op jit(solution)/shard_map/while
  241.8 12.4 copy-start.11
  241.8 17.8 %copy-start.5 = (f32[24,1]{0,1:T(1,128)}, f32[24,1]{0,1:T(1,128)S(1)}, u32[]{:S(2)}) copy-start(f32[24,1]{0,1:T(1,128)S(1)} %get-tuple-element.1060) | copy-start | bytes 292 | tf_op jit(solution)/shard_map/while
  275.6 12.4 copy-start.11
  275.6 17.8 %copy-start.5 = (f32[24,1]{0,1:T(1,128)}, f32[24,1]{0,1:T(1,128)S(1)}, u32[]{:S(2)}) copy-start(f32[24,1]{0,1:T(1,128)S(1)} %get-tuple-element.1060) | copy-start | bytes 292 | tf_op jit(solution)/shard_map/while
  309.4 11.6 copy-start.17
  309.4 12.4 copy-start.11
  309.4 17.8 %copy-start.5 = (f32[24,1]{0,1:T(1,128)}, f32[24,1]{0,1:T(1,128)S(1)}, u32[]{:S(2)}) copy-start(f32[24,1]{0,1:T(1,128)S(1)} %get-tuple-element.1060) | copy-start | bytes 292 | tf_op jit(solution)/shard_map/while
  343.2 12.4 copy-start.11
  343.2 17.8 %copy-start.5 = (f32[24,1]{0,1:T(1,128)}, f32[24,1]{0,1:T(1,128)S(1)}, u32[]{:S(2)}) copy-start(f32[24,1]{0,1:T(1,128)S(1)} %get-tuple-element.1060) | copy-start | bytes 292 | tf_op jit(solution)/shard_map/while
  377.1 12.4 copy-start.11
  377.1 17.8 %copy-start.5 = (f32[24,1]{0,1:T(1,128)}, f32[24,1]{0,1:T(1,128)S(1)}, u32[]{:S(2)}) copy-start(f32[24,1]{0,1:T(1,128)S(1)} %get-tuple-element.1060) | copy-start | bytes 292 | tf_op jit(solution)/shard_map/while
  411.0 12.4 copy-start.11
  411.0 17.8 %copy-start.5 = (f32[24,1]{0,1:T(1,128)}, f32[24,1]{0,1:T(1,128)S(1)}, u32[]{:S(2)}) copy-start(f32[24,1]{0,1:T(1,128)S(1)} %get-tuple-element.1060) | copy-start | bytes 292 | tf_op jit(solution)/shard_map/while
  444.8 12.4 copy-start.11
  444.8 17.8 %copy-start.5 = (f32[24,1]{0,1:T(1,128)}, f32[24,1]{0,1:T(1,128)S(1)}, u32[]{:S(2)}) copy-start(f32[24,1]{0,1:T(1,128)S(1)} %get-tuple-element.1060) | copy-start | bytes 292 | tf_op jit(solution)/shard_map/while
  478.6 12.4 copy-start.11
  478.6 17.8 %copy-start.5 = (f32[24,1]{0,1:T(1,128)}, f32[24,1]{0,1:T(1,128)S(1)}, u32[]{:S(2)}) copy-start(f32[24,1]{0,1:T(1,128)S(1)} %get-tuple-element.1060) | copy-start | bytes 292 | tf_op jit(solution)/shard_map/while
  512.4 12.4 copy-start.11
  512.5 17.8 %copy-start.5 = (f32[24,1]{0,1:T(1,128)}, f32[24,1]{0,1:T(1,128)S(1)}, u32[]{:S(2)}) copy-start(f32[24,1]{0,1:T(1,128)S(1)} %get-tuple-element.1060) | copy-start | bytes 292 | tf_op jit(solution)/shard_map/while
  546.3 12.4 copy-start.11
  546.3 17.8 %copy-start.5 = (f32[24,1]{0,1:T(1,128)}, f32[24,1]{0,1:T(1,128)S(1)}, u32[]{:S(2)}) copy-start(f32[24,1]{0,1:T(1,128)S(1)} %get-tuple-element.1060) | copy-start | bytes 292 | tf_op jit(solution)/shard_map/while
  580.1 12.4 copy-start.11
  580.1 17.8 %copy-start.5 = (f32[24,1]{0,1:T(1,128)}, f32[24,1]{0,1:T(1,128)S(1)}, u32[]{:S(2)}) copy-start(f32[24,1]{0,1:T(1,128)S(1)} %get-tuple-element.1060) | copy-start | bytes 292 | tf_op jit(solution)/shard_map/while
  613.9 12.4 copy-start.11
  613.9 17.8 %copy-start.5 = (f32[24,1]{0,1:T(1,128)}, f32[24,1]{0,1:T(1,128)S(1)}, u32[]{:S(2)}) copy-start(f32[24,1]{0,1:T(1,128)S(1)} %get-tuple-element.1060) | copy-start | bytes 292 | tf_op jit(solution)/shard_map/while
  647.7 11.6 copy-start.17
  647.7 12.4 copy-start.11
  647.7 17.8 %copy-start.5 = (f32[24,1]{0,1:T(1,128)}, f32[24,1]{0,1:T(1,128)S(1)}, u32[]{:S(2)}) copy-start(f32[24,1]{0,1:T(1,128)S(1)} %get-tuple-element.1060) | copy-start | bytes 292 | tf_op jit(solution)/shard_map/while
  681.6 12.4 copy-start.11
  681.6 17.8 %copy-start.5 = (f32[24,1]{0,1:T(1,128)}, f32[24,1]{0,1:T(1,128)S(1)}, u32[]{:S(2)}) copy-start(f32[24,1]{0,1:T(1,128)S(1)} %get-tuple-element.1060) | copy-start | bytes 292 | tf_op jit(solution)/shard_map/while
  715.5 12.4 copy-start.11
  715.5 17.8 %copy-start.5 = (f32[24,1]{0,1:T(1,128)}, f32[24,1]{0,1:T(1,128)S(1)}, u32[]{:S(2)}) copy-start(f32[24,1]{0,1:T(1,128)S(1)} %get-tuple-element.1060) | copy-start | bytes 292 | tf_op jit(solution)/shard_map/while
  749.4 12.4 copy-start.11
  749.4 17.8 %copy-start.5 = (f32[24,1]{0,1:T(1,128)}, f32[24,1]{0,1:T(1,128)S(1)}, u32[]{:S(2)}) copy-start(f32[24,1]{0,1:T(1,128)S(1)} %get-tuple-element.1060) | copy-start | bytes 292 | tf_op jit(solution)/shard_map/while
  783.2 12.4 copy-start.11
  783.2 17.8 %copy-start.5 = (f32[24,1]{0,1:T(1,128)}, f32[24,1]{0,1:T(1,128)S(1)}, u32[]{:S(2)}) copy-start(f32[24,1]{0,1:T(1,128)S(1)} %get-tuple-element.1060) | copy-start | bytes 292 | tf_op jit(solution)/shard_map/while
  824.2 27.2 %copy-start.14 = (s32[45,1,4]{0,2,1:T(4,128)S(1)}, s32[45,1,4]{0,2,1:T(4,128)}, u32[]{:S(2)}) copy-start(s32[45,1,4]{0,2,1:T(4,128)} %param.17) | copy-start | bytes 2164
  874.0 90.0 %all-to-all-start = ((bf16[45,256,90]{2,0,1:T(8,128)(2,1)}), bf16[45,256,90]{2,0,1:T(8,128)(2,1)}, u32[]{:S(2)}, u32[]{:S(2)}) async-start(bf16[45,256,90]{2,0,1:T(8,128)(2,1)} %copy.133), calls=%async_computation | async-start | bytes 6291456 | tf_op jit(solution)/shard_map/all_to_all | solution.py:174
  993.7 32.4 %all-to-all-start.1 = ((bf16[16,2,17280]{2,1,0:T(2,128)(2,1)}), bf16[16,2,17280]{2,1,0:T(2,128)(2,1)}, u32[]{:S(2)}, u32[]{:S(2)}) async-start(bf16[16,2,17280]{2,1,0:T(2,128)(2,1)} %reshape.1473), calls=%async_computation.1 | async-start | bytes 2211840 | tf_op jit(solution)/shard_map/all_to_all | solution.py:102
  1268.0 33.6 %all-to-all-start.4 = ((bf16[16,2,17280]{2,1,0:T(2,128)(2,1)}), bf16[16,2,17280]{2,1,0:T(2,128)(2,1)}, u32[]{:S(2)}, u32[]{:S(2)}) async-start(bf16[16,2,17280]{2,1,0:T(2,128)(2,1)} %reshape.1479), calls=%async_computation.4 | async-start | bytes 2211840 | tf_op jit(solution)/shard_map/all_to_all | solution.py:102
  (259 other events, 2173.1 us)
where the time goes:
time: 1450 us; the launch traced here: 1430 us
  other arithmetic  535 us (37%)
  local copies, waits for them, and re-layouts  388 us (27%)
  loops' own time  255 us (18%)
  blocking collectives  108 us (7%)
  matrix products  64.1 us (4%)
  waiting for transfers between devices  44.8 us (3%)
  starting transfers between devices  30.7 us (2%)
    while x360, other arithmetic  371 us
    another operation x1, loops' own time, legendre_tables(): lax.scan(advance, (zeroed, zeroed), jnp.arange(0, L, unroll_steps, dtype=...  255 us
    unnamed x22, local copies, waits for them, and re-layouts  89.6 us
    all_to_all x1, blocking collectives, shards(): lax.all_to_all(grid_field, 'lon', split_axis=1, concat_axis=2, tiled=True)  61.9 us
    sqrt x96, other arithmetic, legendre_step(): jnp.sqrt(jnp.maximum(4.0 * square - 1.0, 1.0) / jnp.maximum(square - orde...  59.3 us
    dynamic_update_slice x24, local copies, waits for them, and re-layouts, legendre_tables(): lax.scan(advance, (zeroed, zeroed), jnp.arange(0, L, unroll_steps, dtype=...  57.2 us
    all_to_all x2, blocking collectives, regroup(): lax.all_to_all(values, 'lon', split_axis=3, concat_axis=1, tiled=True)  46.5 us
    another operation x24, other arithmetic, advance(): return ((current, earlier), jnp.stack(stacked))  34.2 us
  transfers between devices with their start and end apart: 5, of which 3 were waited for; matrix products, arithmetic and copies ran while one was open for 47% of the time, Pallas kernels for 0%

commit v1 on v0

v1 whole, which is shorter than its diff:
```python
import math

import jax
import jax.numpy as jnp
from jax import lax
from jax.experimental import pallas as pl
from jax.experimental.pallas import tpu as pltpu
from jax.sharding import PartitionSpec as P

NLAT = 720
NLON = 1440
L = 384
CIN = 80
C = 256
TILE = 128
K = 4
SRC_DEV = 48
RIM = 24
LAT_DEV = 45
LON_DEV = 90
N_LAT = 16
N_LON = 16
N_DEV = N_LAT * N_LON

ROWS = 3
GROUPS = LAT_DEV // ROWS
LON_PAD = 96
LON_ALL = N_LON * LON_PAD
ITEMS = 3
PIECES = 18
SLOTS = 24
DEG = L // N_LON
LATS = ROWS * N_DEV
MIB = 1024 * 1024


def params(mib):
    return pltpu.CompilerParams(vmem_limit_bytes=mib * MIB)


def whole():
    return pl.BlockSpec(memory_space=pltpu.VMEM)


def dot(a, b, dims=((1,), (0,))):
    return lax.dot_general(a, b, (dims, ((), ())), preferred_element_type=jnp.float32)


def remap_kernel(offsets, left, own, right, weight, out, tiles):
    step = pl.program_id(0)

    @pl.when(step == 0)
    def _():
        tiles[0:RIM] = left[...]
        tiles[RIM : RIM + SRC_DEV] = own[...]
        tiles[RIM + SRC_DEV :] = right[...]

    @pl.when(step < GROUPS)
    def _():
        columns = []
        for row in range(ROWS):
            base = (step * ROWS + row) * K
            cells = jnp.concatenate([tiles[offsets[base + k]] for k in range(K)], axis=1)
            blocks = jnp.concatenate([weight[row, 0, k] for k in range(K)], axis=1)
            columns.append(dot(blocks, cells, ((1,), (1,))))
        columns.append(jnp.zeros((LON_DEV, C - ROWS * CIN), jnp.float32))
        packed = jnp.concatenate(columns, axis=1)
        packed = jnp.concatenate([packed, jnp.zeros((LON_PAD - LON_DEV, C), jnp.float32)], axis=0)
        out[0] = packed.astype(jnp.bfloat16)

    @pl.when(step >= GROUPS)
    def _():
        out[...] = jnp.zeros_like(out)


def remap(offsets, left, own, right, weight):
    return pl.pallas_call(
        remap_kernel,
        out_shape=jax.ShapeDtypeStruct((N_LON, LON_PAD, C), jnp.bfloat16),
        grid_spec=pltpu.PrefetchScalarGridSpec(
            num_scalar_prefetch=1,
            grid=(N_LON,),
            in_specs=[
                pl.BlockSpec((RIM, CIN, TILE), lambda g, o: (0, 0, 0)),
                pl.BlockSpec((SRC_DEV, CIN, TILE), lambda g, o: (0, 0, 0)),
                pl.BlockSpec((RIM, CIN, TILE), lambda g, o: (0, 0, 0)),
                pl.BlockSpec(
                    (ROWS, 1, K, LON_DEV, TILE),
                    lambda g, o: (jnp.minimum(g, GROUPS - 1), 0, 0, 0, 0),
                ),
            ],
            out_specs=pl.BlockSpec((1, LON_PAD, C), lambda g, o: (g, 0, 0)),
            scratch_shapes=[pltpu.VMEM((RIM + SRC_DEV + RIM, CIN, TILE), jnp.bfloat16)],
        ),
        compiler_params=params(40),
        name="remap",
    )(offsets, left, own, right, weight)


def lift_kernel(cols, lift_in, lift_out, forward, out, scratch):
    for row in range(ROWS):
        hidden = jax.nn.gelu(dot(cols[...], lift_in[row])).astype(jnp.bfloat16)
        lifted = dot(hidden, lift_out[...]).astype(jnp.bfloat16)
        spectra = dot(forward[...], lifted)
        for item in range(ITEMS):
            for half in range(2):
                place = (item * ROWS + row) * 2 + half
                scratch[pl.ds(place, N_DEV, stride=SLOTS), :] = spectra[
                    item * N_DEV : (item + 1) * N_DEV, half * 128 : (half + 1) * 128
                ]
    for place in range(PIECES, SLOTS):
        scratch[pl.ds(place, N_DEV, stride=SLOTS), :] = jnp.zeros((N_DEV, 128), jnp.float32)
    out[...] = scratch[...].reshape(N_DEV, SLOTS, 128).astype(jnp.bfloat16)


def lift(cols, lift_in, lift_out, forward):
    return pl.pallas_call(
        lift_kernel,
        out_shape=jax.ShapeDtypeStruct((N_DEV, SLOTS, 128), jnp.bfloat16),
        in_specs=[whole()] * 4,
        out_specs=whole(),
        scratch_shapes=[pltpu.VMEM((N_DEV * SLOTS, 128), jnp.float32)],
        compiler_params=params(48),
        name="lift",
    )(cols, lift_in, lift_out, forward)


def legendre_kernel(rise, fall, start, initial, restore, factor, cosine, quad, weighted, plain, table):
    tiles = LATS // 128
    cos = [cosine[:, t * 128 : (t + 1) * 128] for t in range(tiles)]
    init = [initial[:, t * 128 : (t + 1) * 128] for t in range(tiles)]

    def advance(block, carry):
        current, earlier = carry
        for step in range(8):
            degree = block * 8 + step
            up, down, on = rise[degree], fall[degree], start[degree]
            latest = []
            for t in range(tiles):
                value = up * (cos[t] * current[t] - down * earlier[t]) + on * init[t]
                table[t, pl.ds(pl.multiple_of(degree * 8, 8), 8), :] = value
                latest.append(value)
            current, earlier = tuple(latest), current
        return current, earlier

    zero = tuple(jnp.zeros((8, 128), jnp.float32) for _ in range(tiles))
    lax.fori_loop(0, L // 8, advance, (zero, zero))
    for item in range(ITEMS):
        for t in range(tiles):
            lanes = slice(t * 128, (t + 1) * 128)
            values = table[t, pl.ds(item, L, stride=8), :] * restore[item : item + 1, lanes]
            weighted[item, :, lanes] = (values * quad[0:1, lanes]).astype(jnp.bfloat16)
            values = values * factor[item : item + 1, lanes]
            plain[item, lanes, :] = values.T.astype(jnp.bfloat16)


def legendre(chip):
    lane = jnp.arange(LATS, dtype=jnp.int32)
    row, device = lane // N_DEV, lane % N_DEV
    band, group = device // N_LON, device % N_LON
    held = (group < GROUPS)[None, :]
    latitude = band * LAT_DEV + jnp.minimum(group, GROUPS - 1) * ROWS + row
    colatitude = (latitude.astype(jnp.float32) + 0.5) * (math.pi / NLAT)
    cosine = jnp.cos(colatitude)[None, :]
    sine = jnp.sin(colatitude)[None, :]
    slot = jnp.arange(8, dtype=jnp.int32)
    order = (jnp.minimum(slot, ITEMS - 1) * (L // ITEMS) + chip).astype(jnp.float32)
    order_col = order[:, None]
    log_scale = (
        0.5
        * (
            jnp.log(2.0 * order_col + 1.0)
            - math.log(4.0 * math.pi)
            + lax.lgamma(2.0 * order_col + 1.0)
            - 2.0 * lax.lgamma(order_col + 1.0)
            - order_col * math.log(4.0)
        )
        + order_col * jnp.log(sine)
    )
    initial = jnp.exp(jnp.minimum(log_scale + 80.0, 0.0))
    restore = jnp.where(held, jnp.exp(jnp.maximum(log_scale, -80.0)), 0.0)
    quad = jnp.broadcast_to(sine * (math.pi / NLAT) * (2.0 * math.pi / NLON), (8, LATS))
    factor = jnp.broadcast_to(jnp.where(order_col == 0.0, 1.0, 2.0), (8, LATS))
    degree = jnp.arange(L, dtype=jnp.int32).astype(jnp.float32)[:, None, None]
    order_row = order[None, :, None]
    square = degree * degree
    rising = jnp.sqrt(
        jnp.maximum(4.0 * square - 1.0, 1.0) / jnp.maximum(square - order_row * order_row, 1.0)
    )
    shifted = (degree - 1.0) * (degree - 1.0)
    falling = jnp.sqrt(
        jnp.maximum(shifted - order_row * order_row, 0.0) / jnp.maximum(4.0 * shifted - 1.0, 1.0)
    )
    start = jnp.where(degree == order_row, 1.0, 0.0)
    spread = lambda values: jnp.broadcast_to(values, (L, 8, 128))
    return pl.pallas_call(
        legendre_kernel,
        out_shape=(
            jax.ShapeDtypeStruct((ITEMS, L, LATS), jnp.bfloat16),
            jax.ShapeDtypeStruct((ITEMS, LATS, L), jnp.bfloat16),
        ),
        in_specs=[whole()] * 8,
        out_specs=(whole(), whole()),
        scratch_shapes=[pltpu.VMEM((LATS // 128, L * 8, 128), jnp.float32)],
        compiler_params=params(40),
        name="legendre",
    )(
        spread(rising),
        spread(falling),
        spread(start),
        initial,
        restore,
        factor,
        jnp.broadcast_to(cosine, (8, LATS)),
        quad,
    )


def analyse_kernel(pieces, weighted, out, scratch):
    scratch[...] = pieces[...].astype(jnp.float32).reshape(N_DEV * SLOTS, 128)
    for item in range(ITEMS):
        rows = []
        for row in range(ROWS):
            place = (item * ROWS + row) * 2
            halves = [scratch[pl.ds(place + h, N_DEV, stride=SLOTS), :] for h in range(2)]
            rows.append(jnp.concatenate(halves, axis=1).astype(jnp.bfloat16))
        spectra = jnp.concatenate(rows, axis=0)
        result = dot(weighted[item], spectra).reshape(N_LON, DEG, C)
        out[:, item * DEG : (item + 1) * DEG, :] = result.astype(jnp.bfloat16)


def analyse(pieces, weighted):
    return pl.pallas_call(
        analyse_kernel,
        out_shape=jax.ShapeDtypeStruct((N_LON, ITEMS * DEG, C), jnp.bfloat16),
        in_specs=[whole()] * 2,
        out_specs=whole(),
        scratch_shapes=[pltpu.VMEM((N_DEV * SLOTS, 128), jnp.float32)],
        compiler_params=params(40),
        name="analyse",
    )(pieces, weighted)


MIX_STEPS = 4
MIX_DEG = DEG // MIX_STEPS


def mix_kernel(pieces, spectral, out, source, result):
    step = pl.program_id(0)
    count = N_LON * ITEMS

    @pl.when(step == 0)
    def _():
        values = pieces[...].astype(jnp.float32).reshape(count * DEG, C)
        source[0] = values[:, :128]
        source[1] = values[:, 128:]

    for index in range(MIX_DEG):
        degree = step * MIX_DEG + index
        halves = [source[h, pl.ds(degree, count, stride=DEG), :] for h in range(2)]
        values = jnp.concatenate(halves, axis=1).astype(jnp.bfloat16)
        mixed = dot(values, spectral[index])
        for h in range(2):
            result[h, pl.ds(degree, count, stride=DEG), :] = mixed[:, h * 128 : (h + 1) * 128]

    @pl.when(step == MIX_STEPS - 1)
    def _():
        for h in range(2):
            values = result[h].reshape(N_LON, ITEMS * DEG, 128)
            out[:, :, h * 128 : (h + 1) * 128] = values.astype(jnp.bfloat16)


def mix(pieces, spectral):
    shape = (N_LON, ITEMS * DEG, C)
    return pl.pallas_call(
        mix_kernel,
        out_shape=jax.ShapeDtypeStruct(shape, jnp.bfloat16),
        grid=(MIX_STEPS,),
        in_specs=[
            pl.BlockSpec(shape, lambda g: (0, 0, 0)),
            pl.BlockSpec((MIX_DEG, C, C), lambda g: (g, 0, 0)),
        ],
        out_specs=pl.BlockSpec(shape, lambda g: (0, 0, 0)),
        scratch_shapes=[pltpu.VMEM((2, N_LON * ITEMS * DEG, 128), jnp.float32)] * 2,
        compiler_params=params(40),
        name="mix",
    )(pieces, spectral)


def synthesise_kernel(pieces, plain, out, scratch):
    for item in range(ITEMS):
        values = pieces[...].astype(jnp.float32)[:, item * DEG : (item + 1) * DEG, :]
        mixed = values.reshape(L, C).astype(jnp.bfloat16)
        result = dot(plain[item], mixed)
        for row in range(ROWS):
            for half in range(2):
                place = (item * ROWS + row) * 2 + half
                scratch[pl.ds(place, N_DEV, stride=SLOTS), :] = result[
                    row * N_DEV : (row + 1) * N_DEV, half * 128 : (half + 1) * 128
                ]
    for place in range(PIECES, SLOTS):
        scratch[pl.ds(place, N_DEV, stride=SLOTS), :] = jnp.zeros((N_DEV, 128), jnp.float32)
    out[...] = scratch[...].reshape(N_DEV, SLOTS, 128).astype(jnp.bfloat16)


def synthesise(pieces, plain):
    return pl.pallas_call(
        synthesise_kernel,
        out_shape=jax.ShapeDtypeStruct((N_DEV, SLOTS, 128), jnp.bfloat16),
        in_specs=[whole()] * 2,
        out_specs=whole(),
        scratch_shapes=[pltpu.VMEM((N_DEV * SLOTS, 128), jnp.float32)],
        compiler_params=params(40),
        name="synthesise",
    )(pieces, plain)


def inverse_kernel(pieces, inverse, out, scratch):
    scratch[...] = pieces[...].astype(jnp.float32).reshape(N_DEV * SLOTS, 128)
    for row in range(ROWS):
        items = []
        for item in range(ITEMS):
            place = (item * ROWS + row) * 2
            halves = [scratch[pl.ds(place + h, N_DEV, stride=SLOTS), :] for h in range(2)]
            items.append(jnp.concatenate(halves, axis=1).astype(jnp.bfloat16))
        spectra = jnp.concatenate(items, axis=0)
        field = dot(inverse[...], spectra).astype(jnp.bfloat16)
        out[:, row * C : (row + 1) * C] = field


def invert(pieces, inverse):
    return pl.pallas_call(
        inverse_kernel,
        out_shape=jax.ShapeDtypeStruct((LON_ALL, ROWS * C), jnp.bfloat16),
        in_specs=[whole()] * 2,
        out_specs=whole(),
        scratch_shapes=[pltpu.VMEM((N_DEV * SLOTS, 128), jnp.float32)],
        compiler_params=params(48),
        name="invert",
    )(pieces, inverse)


def unpack_kernel(pieces, out):
    for row in range(ROWS):
        out[row] = pieces[0, :LON_DEV, row * C : (row + 1) * C]


def unpack(pieces):
    return pl.pallas_call(
        unpack_kernel,
        out_shape=jax.ShapeDtypeStruct((LAT_DEV, LON_DEV, C), jnp.bfloat16),
        grid=(GROUPS,),
        in_specs=[pl.BlockSpec((1, LON_PAD, ROWS * C), lambda g: (g, 0, 0))],
        out_specs=pl.BlockSpec((ROWS, LON_DEV, C), lambda g: (g, 0, 0)),
        compiler_params=params(32),
        name="unpack",
    )(pieces)


def fourier(item_axis):
    shape = (ITEMS * N_DEV, 1) if item_axis == 0 else (1, ITEMS * N_DEV)
    index = lax.broadcasted_iota(jnp.int32, shape, item_axis)
    device = index % N_DEV
    order = (index // N_DEV) * (L // ITEMS) + device // 2
    part = device % 2
    lon = lax.broadcasted_iota(
        jnp.int32, (1, LON_ALL) if item_axis == 0 else (LON_ALL, 1), 1 - item_axis
    )
    column = lon % LON_PAD
    longitude = (lon // LON_PAD) * LON_DEV + column
    held = jnp.where(column < LON_DEV, 1.0, 0.0)
    phase = longitude.astype(jnp.float32) * order.astype(jnp.float32) + 360.0 * part.astype(
        jnp.float32
    )
    phase = phase - 1440.0 * jnp.round(phase * (1.0 / 1440.0))
    angle = (360.0 - jnp.abs(phase)) * (math.pi / 720.0)
    square = angle * angle
    total = -1.0 / 39916800.0
    for term in (1.0 / 362880.0, -1.0 / 5040.0, 1.0 / 120.0, -1.0 / 6.0, 1.0):
        total = total * square + term
    return (total * angle * held).astype(jnp.bfloat16)


def exchange(values, axes):
    return lax.all_to_all(values, axes, split_axis=0, concat_axis=0, tiled=True)


def shards(cube_cells, block_source, block_weight, lift_in, lift_out, spectral):
    lat_index = lax.axis_index("lat")
    lon_index = lax.axis_index("lon")
    chip = lat_index * (N_LON // 2) + lon_index // 2
    right_pairs = [(i, (i + 1) % N_LON) for i in range(N_LON)]
    left_pairs = [(j, i) for i, j in right_pairs]
    left = lax.ppermute(cube_cells[SRC_DEV - RIM :], "lon", right_pairs)
    right = lax.ppermute(cube_cells[:RIM], "lon", left_pairs)
    offsets = (block_source[:, 0, :] - lon_index * SRC_DEV + RIM) % (N_LON * SRC_DEV)
    forward = fourier(0)
    inverse = fourier(1)
    weighted, plain = legendre(chip)
    lift_blocks = jnp.stack(
        [
            jnp.pad(lift_in, ((row * CIN, C - (row + 1) * CIN), (0, 0)))
            for row in range(ROWS)
        ]
    )
    columns = remap(offsets.reshape(LAT_DEV * K), left, cube_cells, right, block_weight)
    columns = exchange(columns, "lon").reshape(LON_ALL, C)
    spectra = exchange(lift(columns, lift_blocks, lift_out, forward), ("lat", "lon"))
    analysis = exchange(analyse(spectra, weighted), "lon")
    mixed = exchange(mix(analysis, spectral), "lon")
    synthesis = exchange(synthesise(mixed, plain), ("lat", "lon"))
    field = invert(synthesis, inverse).reshape(N_LON, LON_PAD, ROWS * C)
    return unpack(exchange(field, "lon"))


def solution(mesh):
    in_specs = (
        P(("lat", "lon"), None, None),
        P("lat", "lon", None),
        P("lat", "lon", None, None, None),
        P(),
        P(),
        P("lon", None, None),
    )
    out_specs = P("lat", "lon", None)
    return jax.shard_map(shards, mesh=mesh, in_specs=in_specs, out_specs=out_specs, check_vma=False)
```

time: 1450 us -> 298 us (0.21); the launches traced: 1430 us -> 297 us
  other arithmetic: 535 us -> 11.4 us
  local copies, waits for them, and re-layouts: 388 us -> 12 us
  loops' own time: 255 us -> 0 us
  matrix products: 64.1 us -> 0 us
  waiting for transfers between devices: 44.8 us -> 92.1 us
  Pallas kernels: 0 us -> 29.2 us
    while x360 -> x0, other arithmetic: 371 us -> none
    another operation x5 -> x0, loops' own time: 255 us -> none  [the longest x1 255 us: legendre_tables(): lax.scan(advance, (zeroed, zeroed), jnp.arange(0, L, unroll_steps, dtype=...]
    unnamed x22 -> x21, local copies, waits for them, and re-layouts: 89.6 us -> 8.66 us
    all_to_all x10 -> x0, local copies, waits for them, and re-layouts: 72.6 us -> none  [the longest x3 29 us: regroup(): lax.all_to_all(values, 'lon', split_axis=3, concat_axis=1, tiled=True)]
    dot_general x17 -> x0, matrix products: 64.1 us -> none  [the longest x6 23.4 us: add_block(): jnp.einsum('lmt,mlpd->mpdt', table_block, degree_rows, preferred_element_...]
    sqrt x96 -> x1, other arithmetic: 59.3 us -> 0.08 us  [legendre(): jnp.sqrt(jnp.maximum(shifted - order_row * order_row, 0.0) / jnp.maximum(...]
    dynamic_update_slice x24 -> x0, local copies, waits for them, and re-layouts: 57.2 us -> none  [legendre_tables(): lax.scan(advance, (zeroed, zeroed), jnp.arange(0, L, unroll_steps, dtype=...]
    another operation x27 -> x1, other arithmetic: 47.2 us -> 0.05 us  [shards(): jnp.stack([jnp.pad(lift_in, ((row * CIN, C - (row + 1) * CIN), (0, 0))) f...]
  transfers between devices with their start and end apart: 5 -> 5, of which waited for: 3 -> 5; matrix products, arithmetic and copies ran while one was open for 47% -> 6% of each run, Pallas kernels for 0% -> 1%
where the time goes in v1:
time: 298 us; the launch traced here: 297 us
  blocking collectives  115 us (39%)
  waiting for transfers between devices  92.1 us (31%)
  starting transfers between devices  36.5 us (12%)
  Pallas kernels  29.2 us (10%)
  local copies, waits for them, and re-layouts  12 us (4%)
  other arithmetic  11.4 us (4%)
    all_to_all x3, blocking collectives, exchange(): return lax.all_to_all(values, axes, split_axis=0, concat_axis=0, tiled=True)  115 us
    all_to_all x3, waiting for transfers between devices, exchange(): return lax.all_to_all(values, axes, split_axis=0, concat_axis=0, tiled=True)  88.4 us
    all_to_all x3, starting transfers between devices, exchange(): return lax.all_to_all(values, axes, split_axis=0, concat_axis=0, tiled=True)  34.6 us
    convert_element_type x2, other arithmetic, fourier(): return (total * angle * held).astype(jnp.bfloat16)  9.48 us
    unnamed x21, local copies, waits for them, and re-layouts  8.66 us
    pallas_call x1, Pallas kernels, remap(): pl.pallas_call(remap_kernel, out_shape=jax.ShapeDtypeStruct((N_LON, LON_P...  8.16 us
  transfers between devices with their start and end apart: 5, of which 5 were waited for; matrix products, arithmetic and copies ran while one was open for 6% of the time, Pallas kernels for 1%

profile of v1, /device:TPU:33, one launch (start us, length us, event | category | flops | bytes accessed | tf_op | source)
XLA Modules:
  0.0 296.9 jit_solution(2536522354769554218)
XLA Ops:
  0.0 1.2 fusion.54
  1.2 0.0 copy-start.1
  1.3 1.8 collective-permute-start
  3.1 0.0 collective-permute-start.1
  3.1 0.7 add_remainder_fusion
  3.8 0.1 copy.10
  3.9 0.1 rem.220
  4.0 3.3 %copy.11.weight = bf16[45,1,4,90,128]{4,3,2,1,0:T(8,128)(2,1)S(1)} copy(bf16[45,1,4,90,128]{4,2,3,1,0:T(4,128)(2,1)} %param.8) | data formatting | bytes 8294400 | tf_op args[2]
  7.3 0.0 copy-start.6
  7.3 0.6 fusion.25
  7.9 1.0 collective-permute-done.left
  8.9 2.8 collective-permute-done.1.right
  11.7 0.0 copy-done.1
  11.7 8.2 %remap.1 = bf16[16,96,256]{2,1,0:T(8,128)(2,1)} custom-call(s32[180]{0:T(256)S(1)} %and_select_fusion.offsets, bf16[24,80,128]{2,1,0:T(8,128)(2,1)S(1)} %collective-permute-done.left, bf16[48,80,128]{2,1,0:T(8,128)(2,1)S(1)} %copy-done.1, bf16[24,80,128]{2,1,0:T(8,128)(2,1)S(1)} %collective-permute-done.1.right, bf16[45,1,4,90,128]{4,3,2,1,0:T(8,128)(2,1)S(1)} %copy.11.weight), custom_call_target="tpu_custom_call" | custom-call | tf_op jit(solution)/shard_map/remap/pallas_call | solution.py:77
  19.8 19.9 %all-to-all-start = ((bf16[16,96,256]{2,1,0:T(8,128)(2,1)}), bf16[16,96,256]{2,1,0:T(8,128)(2,1)S(1)}, u32[]{:S(2)}, u32[]{:S(2)}) async-start(bf16[16,96,256]{2,1,0:T(8,128)(2,1)} %remap.1), calls=%async_computation | async-start | bytes 1572864 | tf_op jit(solution)/shard_map/all_to_all | solution.py:385
  39.7 0.0 copy-start.8
  39.7 0.0 copy-done.6
  39.8 0.5 copy-done.8
  40.3 4.8 %multiply_convert_fusion.1.forward = bf16[768,1536]{1,0:T(8,128)(2,1)S(1)} fusion(f32[1536]{0:T(1024)S(1)} %fusion.21, f32[768]{0:T(1024)S(1)} %fusion.27, f32[768]{0:T(1024)} %fusion.25, f32[1536]{0:T(1024)S(1)} %fusion.14), kind=kLoop, calls=%fused_computation.7 | loop fusion | flops 27131904 | bytes 2377728 | tf_op jit(solution)/shard_map/convert_element_type | solution.py:381
  45.1 18.9 %all-to-all-done = bf16[16,96,256]{2,1,0:T(8,128)(2,1)S(1)} async-done(((bf16[16,96,256]{2,1,0:T(8,128)(2,1)}), bf16[16,96,256]{2,1,0:T(8,128)(2,1)S(1)}, u32[]{:S(2)}, u32[]{:S(2)}) %all-to-all-start) | async-done | bytes 786464 | tf_op jit(solution)/shard_map/all_to_all | solution.py:385
  64.0 0.0 copy-start.5
  64.0 0.9 copy-done.5
  64.9 4.2 %lift.1 = bf16[256,24,128]{2,1,0:T(8,128)(2,1)S(1)} custom-call(bf16[1536,256]{1,0:T(8,128)(2,1)S(1)} %bitcast.11, bf16[3,256,256]{2,1,0:T(8,128)(2,1)S(1)} %pad_maximum_fusion.lift_in, bf16[256,256]{1,0:T(8,128)(2,1)S(1)} %copy-done.5, bf16[768,1536]{1,0:T(8,128)(2,1)S(1)} %multiply_convert_fusion.1.forward), custom_call_target="tpu_custom_call" | custom-call | tf_op jit(solution)/shard_map/lift/pallas_call | solution.py:117
  69.2 0.0 copy-start
  69.2 1.2 copy-done
  70.4 9.2 %all-to-all-start.1 = ((bf16[256,24,128]{2,1,0:T(8,128)(2,1)}), bf16[256,24,128]{2,1,0:T(8,128)(2,1)S(1)}, u32[]{:S(2)}, u32[]{:S(2)}) async-start(bf16[256,24,128]{2,1,0:T(8,128)(2,1)} %copy-done), calls=%async_computation.1 | async-start | bytes 3145728 | tf_op jit(solution)/shard_map/all_to_all | solution.py:385
  79.6 0.1 divide_sqrt_fusion
  79.7 0.1 copy.12
  79.8 0.1 copy.13
  80.0 0.1 compare_select_fusion
  80.1 0.1 copy.14
  80.2 0.1 compare_select_fusion.3
  80.3 0.1 fusion.44
  80.3 0.1 fusion.42
  80.4 0.1 broadcast_multiply_fusion
  80.5 0.1 exponential_select_fusion
  80.5 0.5 broadcast_in_dim.44.rise
  81.0 0.5 broadcast_in_dim.45.fall
  81.5 0.5 broadcast_in_dim.46.start
  82.0 0.1 broadcast_in_dim.72.factor
  82.0 3.1 %legendre.1 = (bf16[3,384,768]{2,1,0:T(8,128)(2,1)S(1)}, bf16[3,768,384]{2,1,0:T(8,128)(2,1)S(1)}) custom-call(f32[384,8,128]{2,1,0:T(8,128)S(1)} %broadcast_in_dim.44.rise, f32[384,8,128]{2,1,0:T(8,128)S(1)} %broadcast_in_dim.45.fall, f32[384,8,128]{2,1,0:T(8,128)S(1)} %broadcast_in_dim.46.start, f32[8,768]{1,0:T(8,128)S(1)} %get-tuple-element.15.initial, ...), custom_call_target="tpu_custom_call" | custom-call | tf_op jit(solution)/shard_map/legendre/pallas_call | solution.py:196
  85.2 0.0 copy-start.3
  85.2 1.2 copy-done.3
  86.4 33.7 %all-to-all-done.1.pieces = bf16[256,24,128]{2,1,0:T(8,128)(2,1)S(1)} async-done(((bf16[256,24,128]{2,1,0:T(8,128)(2,1)}), bf16[256,24,128]{2,1,0:T(8,128)(2,1)S(1)}, u32[]{:S(2)}, u32[]{:S(2)}) %all-to-all-start.1) | async-done | bytes 1572896 | tf_op jit(solution)/shard_map/all_to_all | solution.py:385
  120.0 0.0 copy-start.2
  120.0 0.0 copy-start.4
  120.0 1.6 copy-done.4
  121.7 0.9 analyse.1
  122.5 27.6 %all_to_all.30.pieces = bf16[16,72,256]{2,1,0:T(8,128)(2,1)S(1)} all-to-all(bf16[16,72,256]{2,1,0:T(8,128)(2,1)S(1)} %analyse.1), channel_id=1, replica_groups=mesh['lat'=16,'lon'=16] {'lon'}, dimensions={0} | all-to-all | bytes 1179648 | tf_op jit(solution)/shard_map/all_to_all | solution.py:385
  150.2 0.0 copy-done.2
  150.2 1.2 mix.1
  151.4 0.0 copy-start.7
  151.4 0.0 copy-start.9
  151.4 22.9 %all_to_all.31.pieces = bf16[16,72,256]{2,1,0:T(8,128)(2,1)S(1)} all-to-all(bf16[16,72,256]{2,1,0:T(8,128)(2,1)S(1)} %mix.1), channel_id=1, replica_groups=mesh['lat'=16,'lon'=16] {'lon'}, dimensions={0} | all-to-all | bytes 1179648 | tf_op jit(solution)/shard_map/all_to_all | solution.py:385
  174.3 2.3 synthesise.1
  176.6 5.6 %all-to-all-start.4 = ((bf16[256,24,128]{2,1,0:T(8,128)(2,1)}), bf16[256,24,128]{2,1,0:T(8,128)(2,1)S(1)}, u32[]{:S(2)}, u32[]{:S(2)}) async-start(bf16[256,24,128]{2,1,0:T(8,128)(2,1)} %synthesise.1), calls=%async_computation.4 | async-start | bytes 3145728 | tf_op jit(solution)/shard_map/all_to_all | solution.py:385
  182.2 0.0 copy-done.7
  182.2 0.0 copy-done.9
  182.2 4.6 %multiply_convert_fusion.inverse = bf16[1536,768]{1,0:T(8,128)(2,1)} fusion(f32[1536]{0:T(1024)S(1)} %fusion.21, f32[768]{0:T(1024)S(1)} %copy-done.9, f32[768]{0:T(1024)S(1)} %copy-done.7, f32[1536]{0:T(1024)S(1)} %fusion.14), kind=kLoop, calls=%fused_computation | loop fusion | flops 27131904 | bytes 2377728 | tf_op jit(solution)/shard_map/convert_element_type | solution.py:381
  186.9 35.8 %all-to-all-done.4.pieces = bf16[256,24,128]{2,1,0:T(8,128)(2,1)S(1)} async-done(((bf16[256,24,128]{2,1,0:T(8,128)(2,1)}), bf16[256,24,128]{2,1,0:T(8,128)(2,1)S(1)}, u32[]{:S(2)}, u32[]{:S(2)}) %all-to-all-start.4) | async-done | bytes 1572896 | tf_op jit(solution)/shard_map/all_to_all | solution.py:385
  222.7 3.9 %invert.1 = bf16[1536,768]{1,0:T(8,128)(2,1)S(1)} custom-call(bf16[256,24,128]{2,1,0:T(8,128)(2,1)S(1)} %all-to-all-done.4.pieces, bf16[1536,768]{1,0:T(8,128)(2,1)} %multiply_convert_fusion.inverse), custom_call_target="tpu_custom_call" | custom-call | tf_op jit(solution)/shard_map/invert/pallas_call | solution.py:332
  226.6 64.9 %all_to_all.32.pieces = bf16[16,96,768]{2,1,0:T(8,128)(2,1)S(1)} all-to-all(bf16[16,96,768]{2,1,0:T(8,128)(2,1)S(1)} %bitcast.10), channel_id=1, replica_groups=mesh['lat'=16,'lon'=16] {'lon'}, dimensions={0} | all-to-all | bytes 4718592 | tf_op jit(solution)/shard_map/all_to_all | solution.py:385
  291.5 5.4 %unpack.1 = bf16[45,90,256]{2,1,0:T(8,128)(2,1)} custom-call(bf16[16,96,768]{2,1,0:T(8,128)(2,1)S(1)} %all_to_all.32.pieces), custom_call_target="tpu_custom_call" | custom-call | tf_op jit(solution)/shard_map/unpack/pallas_call | solution.py:349
  (14 shorter events, 0.2 us)
Async XLA Ops:
  1.2 10.4 %copy-start.1 = (bf16[48,80,128]{2,1,0:T(8,128)(2,1)S(1)}, bf16[48,80,128]{2,1,0:T(8,128)(2,1)}, u32[]{:S(2)}) copy-start(bf16[48,80,128]{2,1,0:T(8,128)(2,1)} %own.1) | copy-start | bytes 2949124
  1.3 7.6 %collective-permute-start = (bf16[24,80,128]{2,1,0:T(8,128)(2,1)S(1)}, bf16[24,80,128]{2,1,0:T(8,128)(2,1)S(1)}, u32[]{:S(2)}, u32[]{:S(2)}) collective-permute-start(bf16[24,80,128]{2,1,0:T(8,128)(2,1)S(1)} %get-tuple-element.10), channel_id=1, source_target_pairs={{0,1},{1,2},{2,3},{3,4},{4,5},{5,6},{6,7},{7,8},{8,9},{9,10},{10,1... | collective-permute-start | bytes 1474568 | tf_op jit(solution)/shard_map/ppermute | solution.py:394
  3.1 8.6 %collective-permute-start.1 = (bf16[24,80,128]{2,1,0:T(8,128)(2,1)S(1)}, bf16[24,80,128]{2,1,0:T(8,128)(2,1)S(1)}, u32[]{:S(2)}, u32[]{:S(2)}) collective-permute-start(bf16[24,80,128]{2,1,0:T(8,128)(2,1)S(1)} %get-tuple-element.9), channel_id=1, source_target_pairs={{1,0},{2,1},{3,2},{4,3},{5,4},{6,5},{7,6},{8,7},{9,8},{10,9},{11,1... | collective-permute-start | bytes 1474568 | tf_op jit(solution)/shard_map/ppermute | solution.py:395
  7.3 32.4 %copy-start.6 = (bf16[80,256]{1,0:T(8,128)(2,1)S(1)}, bf16[80,256]{1,0:T(8,128)(2,1)}, u32[]{:S(2)}) copy-start(bf16[80,256]{1,0:T(8,128)(2,1)} %param.9) | copy-start | bytes 122884
  19.8 44.2 %all-to-all-start = ((bf16[16,96,256]{2,1,0:T(8,128)(2,1)}), bf16[16,96,256]{2,1,0:T(8,128)(2,1)S(1)}, u32[]{:S(2)}, u32[]{:S(2)}) async-start(bf16[16,96,256]{2,1,0:T(8,128)(2,1)} %remap.1), calls=%async_computation | async-start | bytes 1572864 | tf_op jit(solution)/shard_map/all_to_all | solution.py:385
  39.7 0.6 copy-start.8
  64.0 0.9 copy-start.5
  69.2 1.2 copy-start
  70.4 49.7 %all-to-all-start.1 = ((bf16[256,24,128]{2,1,0:T(8,128)(2,1)}), bf16[256,24,128]{2,1,0:T(8,128)(2,1)S(1)}, u32[]{:S(2)}, u32[]{:S(2)}) async-start(bf16[256,24,128]{2,1,0:T(8,128)(2,1)} %copy-done), calls=%async_computation.1 | async-start | bytes 3145728 | tf_op jit(solution)/shard_map/all_to_all | solution.py:385
  85.2 1.2 copy-start.3
  120.0 30.1 %copy-start.2 = (bf16[24,256,256]{2,1,0:T(8,128)(2,1)S(1)}, bf16[24,256,256]{2,1,0:T(8,128)(2,1)}, u32[]{:S(2)}) copy-start(bf16[24,256,256]{2,1,0:T(8,128)(2,1)} %spectral.1) | copy-start | bytes 9437188
  120.0 1.6 copy-start.4
  151.4 30.8 %copy-start.7 = (f32[768]{0:T(1024)S(1)}, f32[768]{0:T(1024)}, u32[]{:S(2)}) copy-start(f32[768]{0:T(1024)} %fusion.25) | copy-start | bytes 9220
  151.4 30.8 %copy-start.9 = (f32[768]{0:T(1024)S(1)}, f32[768]{0:T(1024)}, u32[]{:S(2)}) copy-start(f32[768]{0:T(1024)} %copy-done.8) | copy-start | bytes 9220
  176.6 46.1 %all-to-all-start.4 = ((bf16[256,24,128]{2,1,0:T(8,128)(2,1)}), bf16[256,24,128]{2,1,0:T(8,128)(2,1)S(1)}, u32[]{:S(2)}, u32[]{:S(2)}) async-start(bf16[256,24,128]{2,1,0:T(8,128)(2,1)} %synthesise.1), calls=%async_computation.4 | async-start | bytes 3145728 | tf_op jit(solution)/shard_map/all_to_all | solution.py:385

commit v2 on v1

--- a/solution.py
+++ b/solution.py
@@ -24,11 +24,8 @@
 
 ROWS = 3
 GROUPS = LAT_DEV // ROWS
-LON_PAD = 96
-LON_ALL = N_LON * LON_PAD
 ITEMS = 3
-PIECES = 18
-SLOTS = 24
+PIECES = 2 * ITEMS * ROWS
 DEG = L // N_LON
 LATS = ROWS * N_DEV
 MIB = 1024 * 1024
@@ -46,7 +43,12 @@
     return lax.dot_general(a, b, (dims, ((), ())), preferred_element_type=jnp.float32)
 
 
-def remap_kernel(offsets, left, own, right, weight, out, tiles):
+REMAP_STEPS = 4
+STEP_GROUPS = N_LON // REMAP_STEPS
+GROUP_ROWS = 2 * LON_DEV
+
+
+def remap_kernel(offsets, left, own, right, weight, out, tiles, packed):
     step = pl.program_id(0)
 
     @pl.when(step == 0)
@@ -55,71 +57,89 @@
         tiles[RIM : RIM + SRC_DEV] = own[...]
         tiles[RIM + SRC_DEV :] = right[...]
 
-    @pl.when(step < GROUPS)
-    def _():
+    def store(sub, values):
+        for half in range(2):
+            packed[pl.ds(sub * GROUP_ROWS + half, LON_DEV, stride=2), :] = values[
+                :, half * 128 : (half + 1) * 128
+            ]
+
+    def fill(sub):
         columns = []
         for row in range(ROWS):
-            base = (step * ROWS + row) * K
+            base = ((step * STEP_GROUPS + sub) * ROWS + row) * K
             cells = jnp.concatenate([tiles[offsets[base + k]] for k in range(K)], axis=1)
-            blocks = jnp.concatenate([weight[row, 0, k] for k in range(K)], axis=1)
+            blocks = jnp.concatenate([weight[sub * ROWS + row, 0, k] for k in range(K)], axis=1)
             columns.append(dot(blocks, cells, ((1,), (1,))))
         columns.append(jnp.zeros((LON_DEV, C - ROWS * CIN), jnp.float32))
-        packed = jnp.concatenate(columns, axis=1)
-        packed = jnp.concatenate([packed, jnp.zeros((LON_PAD - LON_DEV, C), jnp.float32)], axis=0)
-        out[0] = packed.astype(jnp.bfloat16)
-
-    @pl.when(step >= GROUPS)
+        store(sub, jnp.concatenate(columns, axis=1))
+
+    for sub in range(STEP_GROUPS - 1):
+        fill(sub)
+
+    @pl.when(step < REMAP_STEPS - 1)
     def _():
-        out[...] = jnp.zeros_like(out)
+        fill(STEP_GROUPS - 1)
+
+    @pl.when(step == REMAP_STEPS - 1)
+    def _():
+        store(STEP_GROUPS - 1, jnp.zeros((LON_DEV, C), jnp.float32))
+
+    out[...] = packed[...].astype(jnp.bfloat16)
 
 
 def remap(offsets, left, own, right, weight):
     return pl.pallas_call(
         remap_kernel,
-        out_shape=jax.ShapeDtypeStruct((N_LON, LON_PAD, C), jnp.bfloat16),
+        out_shape=jax.ShapeDtypeStruct((N_LON * GROUP_ROWS, 128), jnp.bfloat16),
         grid_spec=pltpu.PrefetchScalarGridSpec(
             num_scalar_prefetch=1,
-            grid=(N_LON,),
+            grid=(REMAP_STEPS,),
             in_specs=[
                 pl.BlockSpec((RIM, CIN, TILE), lambda g, o: (0, 0, 0)),
                 pl.BlockSpec((SRC_DEV, CIN, TILE), lambda g, o: (0, 0, 0)),
                 pl.BlockSpec((RIM, CIN, TILE), lambda g, o: (0, 0, 0)),
                 pl.BlockSpec(
-                    (ROWS, 1, K, LON_DEV, TILE),
-                    lambda g, o: (jnp.minimum(g, GROUPS - 1), 0, 0, 0, 0),
+                    (STEP_GROUPS * ROWS, 1, K, LON_DEV, TILE), lambda g, o: (g, 0, 0, 0, 0)
                 ),
             ],
-            out_specs=pl.BlockSpec((1, LON_PAD, C), lambda g, o: (g, 0, 0)),
-            scratch_shapes=[pltpu.VMEM((RIM + SRC_DEV + RIM, CIN, TILE), jnp.bfloat16)],
+            out_specs=pl.BlockSpec((STEP_GROUPS * GROUP_ROWS, 128), lambda g, o: (g, 0)),
+            scratch_shapes=[
+                pltpu.VMEM((RIM + SRC_DEV + RIM, CIN, TILE), jnp.bfloat16),
+                pltpu.VMEM((STEP_GROUPS * GROUP_ROWS, 128), jnp.float32),
+            ],
         ),
         compiler_params=params(40),
         name="remap",
     )(offsets, left, own, right, weight)
 
 
-def lift_kernel(cols, lift_in, lift_out, forward, out, scratch):
+def lift_kernel(cols, lift_in, lift_out, forward, out, packed, scratch):
+    packed[...] = cols[...].astype(jnp.float32)
+    halves = [packed[pl.ds(h, NLON, stride=2), :] for h in range(2)]
+    values = jnp.concatenate(halves, axis=1).astype(jnp.bfloat16)
     for row in range(ROWS):
-        hidden = jax.nn.gelu(dot(cols[...], lift_in[row])).astype(jnp.bfloat16)
+        hidden = jax.nn.gelu(dot(values, lift_in[row])).astype(jnp.bfloat16)
         lifted = dot(hidden, lift_out[...]).astype(jnp.bfloat16)
         spectra = dot(forward[...], lifted)
         for item in range(ITEMS):
             for half in range(2):
                 place = (item * ROWS + row) * 2 + half
-                scratch[pl.ds(place, N_DEV, stride=SLOTS), :] = spectra[
+                scratch[pl.ds(place, N_DEV, stride=PIECES), :] = spectra[
                     item * N_DEV : (item + 1) * N_DEV, half * 128 : (half + 1) * 128
                 ]
-    for place in range(PIECES, SLOTS):
-        scratch[pl.ds(place, N_DEV, stride=SLOTS), :] = jnp.zeros((N_DEV, 128), jnp.float32)
-    out[...] = scratch[...].reshape(N_DEV, SLOTS, 128).astype(jnp.bfloat16)
+    out[...] = scratch[...].astype(jnp.bfloat16)
 
 
 def lift(cols, lift_in, lift_out, forward):
     return pl.pallas_call(
         lift_kernel,
-        out_shape=jax.ShapeDtypeStruct((N_DEV, SLOTS, 128), jnp.bfloat16),
+        out_shape=jax.ShapeDtypeStruct((N_DEV * PIECES, 128), jnp.bfloat16),
         in_specs=[whole()] * 4,
         out_specs=whole(),
-        scratch_shapes=[pltpu.VMEM((N_DEV * SLOTS, 128), jnp.float32)],
+        scratch_shapes=[
+            pltpu.VMEM((2 * NLON, 128), jnp.float32),
+            pltpu.VMEM((N_DEV * PIECES, 128), jnp.float32),
+        ],
         compiler_params=params(48),
         name="lift",
     )(cols, lift_in, lift_out, forward)
@@ -217,12 +237,12 @@
 
 
 def analyse_kernel(pieces, weighted, out, scratch):
-    scratch[...] = pieces[...].astype(jnp.float32).reshape(N_DEV * SLOTS, 128)
+    scratch[...] = pieces[...].astype(jnp.float32)
     for item in range(ITEMS):
         rows = []
         for row in range(ROWS):
             place = (item * ROWS + row) * 2
-            halves = [scratch[pl.ds(place + h, N_DEV, stride=SLOTS), :] for h in range(2)]
+            halves = [scratch[pl.ds(place + h, N_DEV, stride=PIECES), :] for h in range(2)]
             rows.append(jnp.concatenate(halves, axis=1).astype(jnp.bfloat16))
         spectra = jnp.concatenate(rows, axis=0)
         result = dot(weighted[item], spectra).reshape(N_LON, DEG, C)
@@ -235,7 +255,7 @@
         out_shape=jax.ShapeDtypeStruct((N_LON, ITEMS * DEG, C), jnp.bfloat16),
         in_specs=[whole()] * 2,
         out_specs=whole(),
-        scratch_shapes=[pltpu.VMEM((N_DEV * SLOTS, 128), jnp.float32)],
+        scratch_shapes=[pltpu.VMEM((N_DEV * PIECES, 128), jnp.float32)],
         compiler_params=params(40),
         name="analyse",
     )(pieces, weighted)
@@ -295,63 +315,80 @@
         for row in range(ROWS):
             for half in range(2):
                 place = (item * ROWS + row) * 2 + half
-                scratch[pl.ds(place, N_DEV, stride=SLOTS), :] = result[
+                scratch[pl.ds(place, N_DEV, stride=PIECES), :] = result[
                     row * N_DEV : (row + 1) * N_DEV, half * 128 : (half + 1) * 128
                 ]
-    for place in range(PIECES, SLOTS):
-        scratch[pl.ds(place, N_DEV, stride=SLOTS), :] = jnp.zeros((N_DEV, 128), jnp.float32)
-    out[...] = scratch[...].reshape(N_DEV, SLOTS, 128).astype(jnp.bfloat16)
+    out[...] = scratch[...].astype(jnp.bfloat16)
 
 
 def synthesise(pieces, plain):
     return pl.pallas_call(
         synthesise_kernel,
-        out_shape=jax.ShapeDtypeStruct((N_DEV, SLOTS, 128), jnp.bfloat16),
+        out_shape=jax.ShapeDtypeStruct((N_DEV * PIECES, 128), jnp.bfloat16),
         in_specs=[whole()] * 2,
         out_specs=whole(),
-        scratch_shapes=[pltpu.VMEM((N_DEV * SLOTS, 128), jnp.float32)],
+        scratch_shapes=[pltpu.VMEM((N_DEV * PIECES, 128), jnp.float32)],
         compiler_params=params(40),
         name="synthesise",
     )(pieces, plain)
 
 
-def inverse_kernel(pieces, inverse, out, scratch):
-    scratch[...] = pieces[...].astype(jnp.float32).reshape(N_DEV * SLOTS, 128)
+TILES = 2 * ROWS
+
+
+def inverse_kernel(pieces, inverse, out, scratch, packed):
+    scratch[...] = pieces[...].astype(jnp.float32)
     for row in range(ROWS):
         items = []
         for item in range(ITEMS):
             place = (item * ROWS + row) * 2
-            halves = [scratch[pl.ds(place + h, N_DEV, stride=SLOTS), :] for h in range(2)]
+            halves = [scratch[pl.ds(place + h, N_DEV, stride=PIECES), :] for h in range(2)]
             items.append(jnp.concatenate(halves, axis=1).astype(jnp.bfloat16))
         spectra = jnp.concatenate(items, axis=0)
-        field = dot(inverse[...], spectra).astype(jnp.bfloat16)
-        out[:, row * C : (row + 1) * C] = field
+        field = dot(inverse[...], spectra)
+        for half in range(2):
+            packed[pl.ds(row * 2 + half, NLON, stride=TILES), :] = field[
+                :, half * 128 : (half + 1) * 128
+            ]
+    out[...] = packed[...].astype(jnp.bfloat16)
 
 
 def invert(pieces, inverse):
     return pl.pallas_call(
         inverse_kernel,
-        out_shape=jax.ShapeDtypeStruct((LON_ALL, ROWS * C), jnp.bfloat16),
+        out_shape=jax.ShapeDtypeStruct((NLON * TILES, 128), jnp.bfloat16),
         in_specs=[whole()] * 2,
         out_specs=whole(),
-        scratch_shapes=[pltpu.VMEM((N_DEV * SLOTS, 128), jnp.float32)],
+        scratch_shapes=[
+            pltpu.VMEM((N_DEV * PIECES, 128), jnp.float32),
+            pltpu.VMEM((NLON * TILES, 128), jnp.float32),
+        ],
         compiler_params=params(48),
         name="invert",
     )(pieces, inverse)
 
 
-def unpack_kernel(pieces, out):
-    for row in range(ROWS):
-        out[row] = pieces[0, :LON_DEV, row * C : (row + 1) * C]
+UNPACK_GROUPS = 4
+
+
+def unpack_kernel(pieces, out, packed):
+    packed[...] = pieces[...].astype(jnp.float32)
+    for group in range(UNPACK_GROUPS):
+        for row in range(ROWS):
+            place = group * LON_DEV * TILES + row * 2
+            halves = [packed[pl.ds(place + h, LON_DEV, stride=TILES), :] for h in range(2)]
+            out[group * ROWS + row] = jnp.concatenate(halves, axis=1).astype(jnp.bfloat16)
 
 
 def unpack(pieces):
+    block = UNPACK_GROUPS * LON_DEV * TILES
     return pl.pallas_call(
         unpack_kernel,
         out_shape=jax.ShapeDtypeStruct((LAT_DEV, LON_DEV, C), jnp.bfloat16),
-        grid=(GROUPS,),
-        in_specs=[pl.BlockSpec((1, LON_PAD, ROWS * C), lambda g: (g, 0, 0))],
-        out_specs=pl.BlockSpec((ROWS, LON_DEV, C), lambda g: (g, 0, 0)),
+        grid=(N_LON // UNPACK_GROUPS,),
+        in_specs=[pl.BlockSpec((block, 128), lambda g: (g, 0))],
+        out_specs=pl.BlockSpec((UNPACK_GROUPS * ROWS, LON_DEV, C), lambda g: (g, 0, 0)),
+        scratch_shapes=[pltpu.VMEM((block, 128), jnp.float32)],
         compiler_params=params(32),
         name="unpack",
     )(pieces)
@@ -363,12 +400,9 @@
     device = index % N_DEV
     order = (index // N_DEV) * (L // ITEMS) + device // 2
     part = device % 2
-    lon = lax.broadcasted_iota(
-        jnp.int32, (1, LON_ALL) if item_axis == 0 else (LON_ALL, 1), 1 - item_axis
-    )
-    column = lon % LON_PAD
-    longitude = (lon // LON_PAD) * LON_DEV + column
-    held = jnp.where(column < LON_DEV, 1.0, 0.0)
+    longitude = lax.broadcasted_iota(
+        jnp.int32, (1, NLON) if item_axis == 0 else (NLON, 1), 1 - item_axis
+    )
     phase = longitude.astype(jnp.float32) * order.astype(jnp.float32) + 360.0 * part.astype(
         jnp.float32
     )
@@ -378,11 +412,17 @@
     total = -1.0 / 39916800.0
     for term in (1.0 / 362880.0, -1.0 / 5040.0, 1.0 / 120.0, -1.0 / 6.0, 1.0):
         total = total * square + term
-    return (total * angle * held).astype(jnp.bfloat16)
-
-
-def exchange(values, axes):
-    return lax.all_to_all(values, axes, split_axis=0, concat_axis=0, tiled=True)
+    return (total * angle).astype(jnp.bfloat16)
+
+
+def exchange(values, axes, count):
+    pairs = values.reshape(count, values.shape[0] // (2 * count), 2, 128)
+    pairs = lax.all_to_all(pairs, axes, split_axis=0, concat_axis=0, tiled=True)
+    return pairs.reshape(values.shape)
+
+
+def regroup(values):
+    return lax.all_to_all(values, "lon", split_axis=0, concat_axis=0, tiled=True)
 
 
 def shards(cube_cells, block_source, block_weight, lift_in, lift_out, spectral):
@@ -404,13 +444,14 @@
         ]
     )
     columns = remap(offsets.reshape(LAT_DEV * K), left, cube_cells, right, block_weight)
-    columns = exchange(columns, "lon").reshape(LON_ALL, C)
-    spectra = exchange(lift(columns, lift_blocks, lift_out, forward), ("lat", "lon"))
-    analysis = exchange(analyse(spectra, weighted), "lon")
-    mixed = exchange(mix(analysis, spectral), "lon")
-    synthesis = exchange(synthesise(mixed, plain), ("lat", "lon"))
-    field = invert(synthesis, inverse).reshape(N_LON, LON_PAD, ROWS * C)
-    return unpack(exchange(field, "lon"))
+    columns = exchange(columns, "lon", N_LON)
+    spectra = lift(columns, lift_blocks, lift_out, forward)
+    spectra = exchange(spectra, ("lat", "lon"), N_DEV)
+    analysis = regroup(analyse(spectra, weighted))
+    mixed = regroup(mix(analysis, spectral))
+    synthesis = exchange(synthesise(mixed, plain), ("lat", "lon"), N_DEV)
+    field = exchange(invert(synthesis, inverse), "lon", N_LON)
+    return unpack(field)
 
 
 def solution(mesh):

time: 298 us -> 267 us (0.90)
  waiting for transfers between devices: 92.1 us -> 78.1 us
  Pallas kernels: 29.2 us -> 21.1 us
  blocking collectives: 115 us -> 112 us
    all_to_all x3, waiting for transfers between devices: 88.4 us -> 73.8 us  [exchange(): pairs = lax.all_to_all(pairs, axes, split_axis=0, concat_axis=0, tiled=True)]
    pallas_call x4, Pallas kernels: 18.6 us -> 14 us  [the longest x1 5.71 us: lift(): pl.pallas_call(lift_kernel, out_shape=jax.ShapeDtypeStruct((N_DEV * PIECE...]
    all_to_all x3, blocking collectives: 115 us -> 112 us  [the longest x1 61.6 us: exchange(): pairs = lax.all_to_all(pairs, axes, split_axis=0, concat_axis=0, tiled=True)]
    pallas_call x1, Pallas kernels: 5.35 us -> 2.03 us  [unpack(): pl.pallas_call(unpack_kernel, out_shape=jax.ShapeDtypeStruct((LAT_DEV, LO...]
    unnamed x21 -> x13, local copies, waits for them, and re-layouts: 8.66 us -> 7.03 us
  transfers between devices with their start and end apart: 5 -> 5, of which waited for: 5 -> 5; matrix products, arithmetic and copies ran while one was open for 6% -> 5% of each run, Pallas kernels for 1% -> 1%
where the time goes in v2:
time: 267 us
  blocking collectives  112 us (42%)
  waiting for transfers between devices  78.1 us (29%)
  starting transfers between devices  36.5 us (14%)
  Pallas kernels  21.1 us (8%)
  local copies, waits for them, and re-layouts  10.4 us (4%)
  other arithmetic  8.96 us (3%)
    all_to_all x3, waiting for transfers between devices, exchange(): pairs = lax.all_to_all(pairs, axes, split_axis=0, concat_axis=0, tiled=True)  73.8 us
    all_to_all x1, blocking collectives, exchange(): pairs = lax.all_to_all(pairs, axes, split_axis=0, concat_axis=0, tiled=True)  61.6 us
    all_to_all x2, blocking collectives, regroup(): lax.all_to_all(values, 'lon', split_axis=0, concat_axis=0, tiled=True)  50 us
    all_to_all x3, starting transfers between devices, exchange(): pairs = lax.all_to_all(pairs, axes, split_axis=0, concat_axis=0, tiled=True)  34.6 us
    convert_element_type x2, other arithmetic, fourier(): return (total * angle).astype(jnp.bfloat16)  7.66 us
    unnamed x13, local copies, waits for them, and re-layouts  7.03 us
    pallas_call x1, Pallas kernels, lift(): pl.pallas_call(lift_kernel, out_shape=jax.ShapeDtypeStruct((N_DEV * PIECE...  5.71 us
  transfers between devices with their start and end apart: 5, of which 5 were waited for; matrix products, arithmetic and copies ran while one was open for 5% of the time, Pallas kernels for 1%

profile of v2, /device:TPU:33, one launch (start us, length us, event | category | flops | bytes accessed | tf_op | source)
XLA Modules:
  0.0 266.9 jit_solution(7474193211336748513)
XLA Ops:
  0.0 1.2 fusion.42
  1.2 0.0 copy-start
  1.3 1.8 collective-permute-start
  3.1 0.0 collective-permute-start.1
  3.1 0.7 add_remainder_fusion
  3.8 0.1 copy.10
  3.9 0.1 rem.178
  4.0 3.3 %copy.11.weight = bf16[45,1,4,90,128]{4,3,2,1,0:T(8,128)(2,1)S(1)} copy(bf16[45,1,4,90,128]{4,2,3,1,0:T(4,128)(2,1)} %param.8) | data formatting | bytes 8294400 | tf_op args[2]
  7.3 0.0 copy-start.5
  7.3 1.5 collective-permute-done.left
  8.9 2.8 %collective-permute-done.1.right = bf16[24,80,128]{2,1,0:T(8,128)(2,1)S(1)} collective-permute-done((bf16[24,80,128]{2,1,0:T(8,128)(2,1)S(1)}, bf16[24,80,128]{2,1,0:T(8,128)(2,1)S(1)}, u32[]{:S(2)}, u32[]{:S(2)}) %collective-permute-start.1) | collective-permute-done | bytes 491552 | tf_op jit(solution)/shard_map/ppermute | solution.py:435
  11.7 0.0 copy-done
  11.7 4.2 %remap.1 = bf16[2880,128]{1,0:T(8,128)(2,1)} custom-call(s32[180]{0:T(256)S(1)} %and_select_fusion.offsets, bf16[24,80,128]{2,1,0:T(8,128)(2,1)S(1)} %collective-permute-done.left, bf16[48,80,128]{2,1,0:T(8,128)(2,1)S(1)} %copy-done, bf16[24,80,128]{2,1,0:T(8,128)(2,1)S(1)} %collective-permute-done.1.right, bf16[45,1,4,90,128]{4,3,2,1,0:T(8,128)(2,1)S(1)} %copy.11.weight), custom_call_target="tpu_custom_call" | custom-call | tf_op jit(solution)/shard_map/remap/pallas_call | solution.py:91
  15.8 19.9 %all-to-all-start = ((bf16[16,90,2,128]{3,2,1,0:T(2,128)(2,1)}), bf16[16,90,2,128]{3,2,1,0:T(2,128)(2,1)S(1)}, u32[]{:S(2)}, u32[]{:S(2)}) async-start(bf16[16,90,2,128]{3,2,1,0:T(2,128)(2,1)} %bitcast), calls=%async_computation | async-start | bytes 1474560 | tf_op jit(solution)/shard_map/all_to_all | solution.py:420
  35.7 0.0 copy-done.5
  35.8 3.9 %multiply_convert_fusion.forward = bf16[768,1440]{1,0:T(8,128)(2,1)S(1)} fusion(f32[768]{0:T(1024)S(1)} %fusion.15, f32[768]{0:T(1024)S(1)} %fusion.13, f32[1440]{0:T(1024)S(1)} %iota_convert_fusion), kind=kLoop, calls=%fused_computation | loop fusion | flops 24330240 | bytes 2223744 | tf_op jit(solution)/shard_map/convert_element_type | solution.py:415
  39.8 19.3 %all-to-all-done = bf16[16,90,2,128]{3,2,1,0:T(2,128)(2,1)S(1)} async-done(((bf16[16,90,2,128]{3,2,1,0:T(2,128)(2,1)}), bf16[16,90,2,128]{3,2,1,0:T(2,128)(2,1)S(1)}, u32[]{:S(2)}, u32[]{:S(2)}) %all-to-all-start) | async-done | bytes 737312 | tf_op jit(solution)/shard_map/all_to_all | solution.py:420
  59.0 0.0 copy-start.4
  59.0 0.9 copy-done.4
  59.9 5.7 %lift.1 = bf16[4608,128]{1,0:T(8,128)(2,1)} custom-call(bf16[2880,128]{1,0:T(8,128)(2,1)S(1)} %bitcast.20, bf16[3,256,256]{2,1,0:T(8,128)(2,1)S(1)} %pad_maximum_fusion.lift_in, bf16[256,256]{1,0:T(8,128)(2,1)S(1)} %copy-done.4, bf16[768,1440]{1,0:T(8,128)(2,1)S(1)} %multiply_convert_fusion.forward), custom_call_target="tpu_custom_call" | custom-call | tf_op jit(solution)/shard_map/lift/pallas_call | solution.py:134
  65.6 9.1 %all-to-all-start.1 = ((bf16[256,9,2,128]{3,2,1,0:T(2,128)(2,1)}), bf16[256,9,2,128]{3,2,1,0:T(2,128)(2,1)S(1)}, u32[]{:S(2)}, u32[]{:S(2)}) async-start(bf16[256,9,2,128]{3,2,1,0:T(2,128)(2,1)} %bitcast.5), calls=%async_computation.1 | async-start | bytes 2359296 | tf_op jit(solution)/shard_map/all_to_all | solution.py:420
  74.8 0.1 divide_sqrt_fusion
  74.9 0.1 copy.12
  75.0 0.1 copy.13
  75.2 0.1 compare_select_fusion
  75.3 0.1 copy.14
  75.4 0.1 compare_select_fusion.3
  75.5 0.1 fusion.32
  75.5 0.1 fusion.30
  75.6 0.1 broadcast_multiply_fusion
  75.7 0.1 exponential_select_fusion
  75.8 0.5 broadcast_in_dim.30.rise
  76.2 0.5 broadcast_in_dim.31.fall
  76.7 0.5 broadcast_in_dim.32.start
  77.2 0.1 broadcast_in_dim.34.factor
  77.2 3.1 %legendre.1 = (bf16[3,384,768]{2,1,0:T(8,128)(2,1)S(1)}, bf16[3,768,384]{2,1,0:T(8,128)(2,1)S(1)}) custom-call(f32[384,8,128]{2,1,0:T(8,128)S(1)} %broadcast_in_dim.30.rise, f32[384,8,128]{2,1,0:T(8,128)S(1)} %broadcast_in_dim.31.fall, f32[384,8,128]{2,1,0:T(8,128)S(1)} %broadcast_in_dim.32.start, f32[8,768]{1,0:T(8,128)S(1)} %get-tuple-element.15.initial, ...), custom_call_target="tpu_custom_call" | custom-call | tf_op jit(solution)/shard_map/legendre/pallas_call | solution.py:216
  80.4 0.0 copy-start.2
  80.4 1.2 copy-done.2
  81.6 25.7 %all-to-all-done.1 = bf16[256,9,2,128]{3,2,1,0:T(2,128)(2,1)S(1)} async-done(((bf16[256,9,2,128]{3,2,1,0:T(2,128)(2,1)}), bf16[256,9,2,128]{3,2,1,0:T(2,128)(2,1)S(1)}, u32[]{:S(2)}, u32[]{:S(2)}) %all-to-all-start.1) | async-done | bytes 1179680 | tf_op jit(solution)/shard_map/all_to_all | solution.py:420
  107.3 0.0 copy-start.1
  107.3 0.0 copy-start.3
  107.3 1.6 copy-done.3
  108.9 0.7 analyse.1
  109.7 27.1 %all_to_all.30.pieces = bf16[16,72,256]{2,1,0:T(8,128)(2,1)S(1)} all-to-all(bf16[16,72,256]{2,1,0:T(8,128)(2,1)S(1)} %analyse.1), channel_id=1, replica_groups=mesh['lat'=16,'lon'=16] {'lon'}, dimensions={0} | all-to-all | bytes 1179648 | tf_op jit(solution)/shard_map/all_to_all | solution.py:425
  136.8 0.0 copy-done.1
  136.8 1.2 mix.1
  138.0 22.9 %all_to_all.31.pieces = bf16[16,72,256]{2,1,0:T(8,128)(2,1)S(1)} all-to-all(bf16[16,72,256]{2,1,0:T(8,128)(2,1)S(1)} %mix.1), channel_id=1, replica_groups=mesh['lat'=16,'lon'=16] {'lon'}, dimensions={0} | all-to-all | bytes 1179648 | tf_op jit(solution)/shard_map/all_to_all | solution.py:425
  160.9 1.9 synthesise.1
  162.8 5.6 %all-to-all-start.4 = ((bf16[256,9,2,128]{3,2,1,0:T(2,128)(2,1)}), bf16[256,9,2,128]{3,2,1,0:T(2,128)(2,1)S(1)}, u32[]{:S(2)}, u32[]{:S(2)}) async-start(bf16[256,9,2,128]{3,2,1,0:T(2,128)(2,1)} %bitcast.7), calls=%async_computation.4 | async-start | bytes 2359296 | tf_op jit(solution)/shard_map/all_to_all | solution.py:420
  168.4 3.8 %multiply_convert_fusion.1.inverse = bf16[1440,768]{1,0:T(8,128)(2,1)S(1)} fusion(f32[768]{0:T(1024)S(1)} %fusion.15, f32[768]{0:T(1024)S(1)} %fusion.13, f32[1440]{0:T(1024)S(1)} %iota_convert_fusion), kind=kLoop, calls=%fused_computation.7 | loop fusion | flops 24330240 | bytes 2223744 | tf_op jit(solution)/shard_map/convert_element_type | solution.py:415
  172.2 28.8 %all-to-all-done.4 = bf16[256,9,2,128]{3,2,1,0:T(2,128)(2,1)S(1)} async-done(((bf16[256,9,2,128]{3,2,1,0:T(2,128)(2,1)}), bf16[256,9,2,128]{3,2,1,0:T(2,128)(2,1)S(1)}, u32[]{:S(2)}, u32[]{:S(2)}) %all-to-all-start.4) | async-done | bytes 1179680 | tf_op jit(solution)/shard_map/all_to_all | solution.py:420
  201.0 2.3 invert.1
  203.3 61.6 %all_to_all.32 = bf16[16,270,2,128]{3,2,1,0:T(2,128)(2,1)S(1)} all-to-all(bf16[16,270,2,128]{3,2,1,0:T(2,128)(2,1)S(1)} %bitcast.16), channel_id=1, replica_groups=mesh['lat'=16,'lon'=16] {'lon'}, dimensions={0} | all-to-all | bytes 4423680 | tf_op jit(solution)/shard_map/all_to_all | solution.py:420
  264.9 2.0 unpack.1
  (14 shorter events, 0.1 us)
Async XLA Ops:
  1.2 10.4 %copy-start = (bf16[48,80,128]{2,1,0:T(8,128)(2,1)S(1)}, bf16[48,80,128]{2,1,0:T(8,128)(2,1)}, u32[]{:S(2)}) copy-start(bf16[48,80,128]{2,1,0:T(8,128)(2,1)} %own.1) | copy-start | bytes 2949124
  1.3 7.6 %collective-permute-start = (bf16[24,80,128]{2,1,0:T(8,128)(2,1)S(1)}, bf16[24,80,128]{2,1,0:T(8,128)(2,1)S(1)}, u32[]{:S(2)}, u32[]{:S(2)}) collective-permute-start(bf16[24,80,128]{2,1,0:T(8,128)(2,1)S(1)} %get-tuple-element.10), channel_id=1, source_target_pairs={{0,1},{1,2},{2,3},{3,4},{4,5},{5,6},{6,7},{7,8},{8,9},{9,10},{10,1... | collective-permute-start | bytes 1474568 | tf_op jit(solution)/shard_map/ppermute | solution.py:434
  3.1 8.6 %collective-permute-start.1 = (bf16[24,80,128]{2,1,0:T(8,128)(2,1)S(1)}, bf16[24,80,128]{2,1,0:T(8,128)(2,1)S(1)}, u32[]{:S(2)}, u32[]{:S(2)}) collective-permute-start(bf16[24,80,128]{2,1,0:T(8,128)(2,1)S(1)} %get-tuple-element.9), channel_id=1, source_target_pairs={{1,0},{2,1},{3,2},{4,3},{5,4},{6,5},{7,6},{8,7},{9,8},{10,9},{11,1... | collective-permute-start | bytes 1474568 | tf_op jit(solution)/shard_map/ppermute | solution.py:435
  7.3 28.4 %copy-start.5 = (bf16[80,256]{1,0:T(8,128)(2,1)S(1)}, bf16[80,256]{1,0:T(8,128)(2,1)}, u32[]{:S(2)}) copy-start(bf16[80,256]{1,0:T(8,128)(2,1)} %param.9) | copy-start | bytes 122884
  15.8 43.2 %all-to-all-start = ((bf16[16,90,2,128]{3,2,1,0:T(2,128)(2,1)}), bf16[16,90,2,128]{3,2,1,0:T(2,128)(2,1)S(1)}, u32[]{:S(2)}, u32[]{:S(2)}) async-start(bf16[16,90,2,128]{3,2,1,0:T(2,128)(2,1)} %bitcast), calls=%async_computation | async-start | bytes 1474560 | tf_op jit(solution)/shard_map/all_to_all | solution.py:420
  59.0 0.9 copy-start.4
  65.6 41.7 %all-to-all-start.1 = ((bf16[256,9,2,128]{3,2,1,0:T(2,128)(2,1)}), bf16[256,9,2,128]{3,2,1,0:T(2,128)(2,1)S(1)}, u32[]{:S(2)}, u32[]{:S(2)}) async-start(bf16[256,9,2,128]{3,2,1,0:T(2,128)(2,1)} %bitcast.5), calls=%async_computation.1 | async-start | bytes 2359296 | tf_op jit(solution)/shard_map/all_to_all | solution.py:420
  80.4 1.2 copy-start.2
  107.3 29.5 %copy-start.1 = (bf16[24,256,256]{2,1,0:T(8,128)(2,1)S(1)}, bf16[24,256,256]{2,1,0:T(8,128)(2,1)}, u32[]{:S(2)}) copy-start(bf16[24,256,256]{2,1,0:T(8,128)(2,1)} %spectral.1) | copy-start | bytes 9437188
  107.3 1.6 copy-start.3
  162.8 38.2 %all-to-all-start.4 = ((bf16[256,9,2,128]{3,2,1,0:T(2,128)(2,1)}), bf16[256,9,2,128]{3,2,1,0:T(2,128)(2,1)S(1)}, u32[]{:S(2)}, u32[]{:S(2)}) async-start(bf16[256,9,2,128]{3,2,1,0:T(2,128)(2,1)} %bitcast.7), calls=%async_computation.4 | async-start | bytes 2359296 | tf_op jit(solution)/shard_map/all_to_all | solution.py:420

commit v3 on v2

--- a/solution.py
+++ b/solution.py
@@ -48,14 +48,15 @@
 GROUP_ROWS = 2 * LON_DEV
 
 
-def remap_kernel(offsets, left, own, right, weight, out, tiles, packed):
+def remap_kernel(offsets, across, own, beside, weight, out, tiles, packed):
     step = pl.program_id(0)
 
     @pl.when(step == 0)
     def _():
-        tiles[0:RIM] = left[...]
+        place = offsets[LAT_DEV * K]
+        tiles[pl.ds(place, RIM)] = across[...]
+        tiles[pl.ds(RIM + SRC_DEV - place, RIM)] = beside[...]
         tiles[RIM : RIM + SRC_DEV] = own[...]
-        tiles[RIM + SRC_DEV :] = right[...]
 
     def store(sub, values):
         for half in range(2):
@@ -87,7 +88,7 @@
     out[...] = packed[...].astype(jnp.bfloat16)
 
 
-def remap(offsets, left, own, right, weight):
+def remap(offsets, across, own, beside, weight):
     return pl.pallas_call(
         remap_kernel,
         out_shape=jax.ShapeDtypeStruct((N_LON * GROUP_ROWS, 128), jnp.bfloat16),
@@ -110,10 +111,11 @@
         ),
         compiler_params=params(40),
         name="remap",
-    )(offsets, left, own, right, weight)
-
-
-def lift_kernel(cols, lift_in, lift_out, forward, out, packed, scratch):
+    )(offsets, across, own, beside, weight)
+
+
+def lift_kernel(cols, lift_in, lift_out, forward, *rest):
+    out, packed, scratch = rest[-3:]
     packed[...] = cols[...].astype(jnp.float32)
     halves = [packed[pl.ds(h, NLON, stride=2), :] for h in range(2)]
     values = jnp.concatenate(halves, axis=1).astype(jnp.bfloat16)
@@ -130,11 +132,11 @@
     out[...] = scratch[...].astype(jnp.bfloat16)
 
 
-def lift(cols, lift_in, lift_out, forward):
+def lift(cols, lift_in, lift_out, forward, tables):
     return pl.pallas_call(
         lift_kernel,
         out_shape=jax.ShapeDtypeStruct((N_DEV * PIECES, 128), jnp.bfloat16),
-        in_specs=[whole()] * 4,
+        in_specs=[whole()] * 4 + [pl.BlockSpec(memory_space=pl.ANY)] * len(tables),
         out_specs=whole(),
         scratch_shapes=[
             pltpu.VMEM((2 * NLON, 128), jnp.float32),
@@ -142,7 +144,7 @@
         ],
         compiler_params=params(48),
         name="lift",
-    )(cols, lift_in, lift_out, forward)
+    )(cols, lift_in, lift_out, forward, *tables)
 
 
 def legendre_kernel(rise, fall, start, initial, restore, factor, cosine, quad, weighted, plain, table):
@@ -429,11 +431,22 @@
     lat_index = lax.axis_index("lat")
     lon_index = lax.axis_index("lon")
     chip = lat_index * (N_LON // 2) + lon_index // 2
-    right_pairs = [(i, (i + 1) % N_LON) for i in range(N_LON)]
-    left_pairs = [(j, i) for i, j in right_pairs]
-    left = lax.ppermute(cube_cells[SRC_DEV - RIM :], "lon", right_pairs)
-    right = lax.ppermute(cube_cells[:RIM], "lon", left_pairs)
+    odd = lon_index % 2
+    far = SRC_DEV - RIM
+    across = lax.ppermute(
+        lax.dynamic_slice_in_dim(cube_cells, odd * far, RIM, 0),
+        "lon",
+        [(i, (i + 1) % N_LON if i % 2 else (i - 1) % N_LON) for i in range(N_LON)],
+    )
+    beside = lax.ppermute(
+        lax.dynamic_slice_in_dim(cube_cells, (1 - odd) * far, RIM, 0),
+        "lon",
+        [(i, i ^ 1) for i in range(N_LON)],
+    )
     offsets = (block_source[:, 0, :] - lon_index * SRC_DEV + RIM) % (N_LON * SRC_DEV)
+    places = jnp.concatenate(
+        [offsets.reshape(LAT_DEV * K), (odd * (RIM + SRC_DEV)).reshape(1).astype(jnp.int32)]
+    )
     forward = fourier(0)
     inverse = fourier(1)
     weighted, plain = legendre(chip)
@@ -443,9 +456,9 @@
             for row in range(ROWS)
         ]
     )
-    columns = remap(offsets.reshape(LAT_DEV * K), left, cube_cells, right, block_weight)
+    columns = remap(places, across, cube_cells, beside, block_weight)
     columns = exchange(columns, "lon", N_LON)
-    spectra = lift(columns, lift_blocks, lift_out, forward)
+    spectra = lift(columns, lift_blocks, lift_out, forward, (inverse, weighted, plain))
     spectra = exchange(spectra, ("lat", "lon"), N_DEV)
     analysis = regroup(analyse(spectra, weighted))
     mixed = regroup(mix(analysis, spectral))

time: 267 us -> 265 us (level)
  blocking collectives: 112 us -> 191 us
  waiting for transfers between devices: 78.1 us -> 12.5 us
  starting transfers between devices: 36.5 us -> 14.9 us
  other arithmetic: 8.96 us -> 16.4 us
    all_to_all x1 -> x3, blocking collectives: 61.6 us -> 140 us  [exchange(): pairs = lax.all_to_all(pairs, axes, split_axis=0, concat_axis=0, tiled=True)]
    all_to_all x3 -> x1, waiting for transfers between devices: 73.8 us -> 12.5 us  [exchange(): pairs = lax.all_to_all(pairs, axes, split_axis=0, concat_axis=0, tiled=True)]
    all_to_all x3 -> x1, starting transfers between devices: 34.6 us -> 6.23 us  [exchange(): pairs = lax.all_to_all(pairs, axes, split_axis=0, concat_axis=0, tiled=True)]
    ppermute x2, starting transfers between devices: 1.85 us -> 8.69 us  [the longest x1 6.83 us: shards(): lax.ppermute(lax.dynamic_slice_in_dim(cube_cells, (1 - odd) * far, RIM, 0...]
    ppermute x2, waiting for transfers between devices: 4.32 us -> 0.01 us  [the longest x1 0.01 us: shards(): lax.ppermute(lax.dynamic_slice_in_dim(cube_cells, odd * far, RIM, 0), 'lo...]
    unnamed x13 -> x25, local copies, waits for them, and re-layouts: 7.03 us -> 5.23 us
  transfers between devices with their start and end apart: 5 -> 3, of which waited for: 5 -> 1; matrix products, arithmetic and copies ran while one was open for 5% -> 9% of each run, Pallas kernels for 1% -> 1%
where the time goes in v3:
time: 265 us
  blocking collectives  191 us (72%)
  Pallas kernels  21 us (8%)
  other arithmetic  16.4 us (6%)
  starting transfers between devices  14.9 us (6%)
  waiting for transfers between devices  12.5 us (5%)
  local copies, waits for them, and re-layouts  9.33 us (4%)
    all_to_all x3, blocking collectives, exchange(): pairs = lax.all_to_all(pairs, axes, split_axis=0, concat_axis=0, tiled=True)  140 us
    all_to_all x2, blocking collectives, regroup(): lax.all_to_all(values, 'lon', split_axis=0, concat_axis=0, tiled=True)  50.1 us
    all_to_all x1, waiting for transfers between devices, exchange(): pairs = lax.all_to_all(pairs, axes, split_axis=0, concat_axis=0, tiled=True)  12.5 us
    convert_element_type x2, other arithmetic, fourier(): return (total * angle).astype(jnp.bfloat16)  9.59 us
    ppermute x1, starting transfers between devices, shards(): lax.ppermute(lax.dynamic_slice_in_dim(cube_cells, (1 - odd) * far, RIM, 0...  6.83 us
    pallas_call x1, Pallas kernels, lift(): pl.pallas_call(lift_kernel, out_shape=jax.ShapeDtypeStruct((N_DEV * PIECE...  6.56 us
    all_to_all x1, starting transfers between devices, exchange(): pairs = lax.all_to_all(pairs, axes, split_axis=0, concat_axis=0, tiled=True)  6.23 us
  transfers between devices with their start and end apart: 3, of which 1 were waited for; matrix products, arithmetic and copies ran while one was open for 9% of the time, Pallas kernels for 1%

profile of v3, /device:TPU:33, one launch (start us, length us, event | category | flops | bytes accessed | tf_op | source)
XLA Modules:
  0.0 264.9 jit_solution(15777117545853743509)
XLA Ops:
  0.0 1.2 constant_dynamic-slice_fusion
  1.2 1.9 collective-permute-start
  3.1 6.8 %collective-permute-start.1 = (bf16[24,80,128]{2,1,0:T(8,128)(2,1)S(1)}, bf16[24,80,128]{2,1,0:T(8,128)(2,1)S(1)}, u32[]{:S(2)}, u32[]{:S(2)}) collective-permute-start(bf16[24,80,128]{2,1,0:T(8,128)(2,1)S(1)} %get-tuple-element.9), channel_id=1, source_target_pairs={{0,1},{1,0},{2,3},{3,2},{4,5},{5,4},{6,7},{7,6},{8,9},{9,8},{10,11... | collective-permute-start | bytes 1474568 | tf_op jit(solution)/shard_map/ppermute | solution.py:441
  10.0 0.0 copy-start.10
  10.0 0.6 compare_select_fusion.3
  10.7 0.7 add_remainder_fusion
  11.4 0.1 copy.10
  11.5 0.1 rem.194
  11.6 0.5 and_select_fusion
  12.1 0.7 compare_select_fusion
  12.8 4.7 %multiply_convert_fusion.1.rest_0_.inverse = bf16[1440,768]{1,0:T(8,128)(2,1)} fusion(f32[768]{0:T(1024)S(1)} %fusion.15, f32[768]{0:T(1024)S(1)} %fusion.13, f32[1440]{0:T(1024)S(1)} %iota_convert_fusion), kind=kLoop, calls=%fused_computation.7 | loop fusion | flops 24330240 | bytes 2223744 | tf_op jit(solution)/shard_map/convert_element_type | solution.py:417
  17.5 0.1 divide_sqrt_fusion
  17.5 0.6 fusion.29
  18.1 0.1 copy.12
  18.3 0.0 copy-done.10
  18.3 0.1 copy.13
  18.4 0.0 copy-start.1
  18.4 0.9 copy.14
  19.3 0.0 copy-start.9
  19.3 3.3 %copy.11.weight = bf16[45,1,4,90,128]{4,3,2,1,0:T(8,128)(2,1)S(1)} copy(bf16[45,1,4,90,128]{4,2,3,1,0:T(4,128)(2,1)} %param.8) | data formatting | bytes 8294400 | tf_op args[2]
  22.6 0.0 copy-done.9
  22.6 0.1 pad_add_fusion.offsets
  22.7 0.7 fusion.32
  23.4 0.6 fusion.30
  24.0 0.6 broadcast_multiply_fusion
  24.7 0.0 collective-permute-done.across
  24.7 0.0 copy-start.8
  24.7 0.0 collective-permute-done.1.beside
  24.7 0.0 copy-done.1
  24.7 4.2 %remap.1 = bf16[2880,128]{1,0:T(8,128)(2,1)} custom-call(s32[181]{0:T(256)S(1)} %pad_add_fusion.offsets, bf16[24,80,128]{2,1,0:T(8,128)(2,1)S(1)} %collective-permute-done.across, bf16[48,80,128]{2,1,0:T(8,128)(2,1)S(1)} %copy-done.1, bf16[24,80,128]{2,1,0:T(8,128)(2,1)S(1)} %collective-permute-done.1.beside, bf16[45,1,4,90,128]{4,3,2,1,0:T(8,128)(2,1)S(1)} %copy.11.weight), custom_call_target="tpu_custom_call" | custom-call | tf_op jit(solution)/shard_map/remap/pallas_call | solution.py:92
  28.9 0.0 copy-start.11
  28.9 6.2 %all-to-all-start = ((bf16[16,90,2,128]{3,2,1,0:T(2,128)(2,1)}), bf16[16,90,2,128]{3,2,1,0:T(2,128)(2,1)}, u32[]{:S(2)}, u32[]{:S(2)}) async-start(bf16[16,90,2,128]{3,2,1,0:T(2,128)(2,1)} %bitcast.1), calls=%async_computation | async-start | bytes 1474560 | tf_op jit(solution)/shard_map/all_to_all | solution.py:422
  35.1 0.0 copy-done.8
  35.1 0.8 exponential_select_fusion
  35.9 0.5 broadcast_in_dim.30.rise
  36.4 0.0 copy-start.5
  36.4 0.5 broadcast_in_dim.31.fall
  36.8 0.5 broadcast_in_dim.32.start
  37.3 0.0 copy-done.11
  37.3 0.1 broadcast_in_dim.34.factor
  37.4 0.0 copy-done.7
  37.4 0.0 copy-done.6
  37.4 3.1 %legendre.1 = (bf16[3,384,768]{2,1,0:T(8,128)(2,1)S(1)}, bf16[3,768,384]{2,1,0:T(8,128)(2,1)S(1)}) custom-call(f32[384,8,128]{2,1,0:T(8,128)S(1)} %broadcast_in_dim.30.rise, f32[384,8,128]{2,1,0:T(8,128)S(1)} %broadcast_in_dim.31.fall, f32[384,8,128]{2,1,0:T(8,128)S(1)} %broadcast_in_dim.32.start, f32[8,768]{1,0:T(8,128)S(1)} %get-tuple-element.15.initial, ...), custom_call_target="tpu_custom_call" | custom-call | tf_op jit(solution)/shard_map/legendre/pallas_call | solution.py:218
  40.5 0.0 copy-done.5
  40.6 0.8 pad_maximum_fusion.lift_in
  41.4 4.9 %multiply_convert_fusion.forward = bf16[768,1440]{1,0:T(8,128)(2,1)} fusion(f32[768]{0:T(1024)S(1)} %fusion.15, f32[768]{0:T(1024)S(1)} %fusion.13, f32[1440]{0:T(1024)S(1)} %iota_convert_fusion), kind=kLoop, calls=%fused_computation | loop fusion | flops 24330240 | bytes 2223744 | tf_op jit(solution)/shard_map/convert_element_type | solution.py:417
  46.3 12.5 %all-to-all-done = bf16[16,90,2,128]{3,2,1,0:T(2,128)(2,1)} async-done(((bf16[16,90,2,128]{3,2,1,0:T(2,128)(2,1)}), bf16[16,90,2,128]{3,2,1,0:T(2,128)(2,1)}, u32[]{:S(2)}, u32[]{:S(2)}) %all-to-all-start) | async-done | bytes 737312 | tf_op jit(solution)/shard_map/all_to_all | solution.py:422
  58.7 1.0 copy-done.3
  59.7 0.9 copy-done.4
  60.6 6.6 %lift.1 = bf16[4608,128]{1,0:T(8,128)(2,1)S(1)} custom-call(bf16[2880,128]{1,0:T(8,128)(2,1)} %bitcast.2.cols, bf16[3,256,256]{2,1,0:T(8,128)(2,1)S(1)} %copy-done.3, bf16[256,256]{1,0:T(8,128)(2,1)S(1)} %copy-done.4, bf16[768,1440]{1,0:T(8,128)(2,1)} %multiply_convert_fusion.forward, bf16[1440,768]{1,0:T(8,128)(2,1)} %multiply_convert_fusion.1.rest_0_.inverse, ...), custom_call_target="tpu_custom_call" | custom-call | tf_op jit(solution)/shard_map/lift/pallas_call | solution.py:136
  67.2 0.0 copy-start.2
  67.2 40.1 %all_to_all.30 = bf16[256,9,2,128]{3,2,1,0:T(2,128)(2,1)S(1)} all-to-all(bf16[256,9,2,128]{3,2,1,0:T(2,128)(2,1)S(1)} %bitcast.19), channel_id=1, replica_groups=mesh['lat'=16,'lon'=16] {'lat','lon'}, dimensions={0} | all-to-all | bytes 2359296 | tf_op jit(solution)/shard_map/all_to_all | solution.py:422
  107.3 0.7 analyse.1
  108.1 27.1 %all_to_all.31.pieces = bf16[16,72,256]{2,1,0:T(8,128)(2,1)S(1)} all-to-all(bf16[16,72,256]{2,1,0:T(8,128)(2,1)S(1)} %analyse.1), channel_id=1, replica_groups=mesh['lat'=16,'lon'=16] {'lon'}, dimensions={0} | all-to-all | bytes 1179648 | tf_op jit(solution)/shard_map/all_to_all | solution.py:427
  135.2 0.0 copy-done.2
  135.2 1.2 mix.1
  136.4 0.0 copy-start
  136.4 23.0 %all_to_all.32.pieces = bf16[16,72,256]{2,1,0:T(8,128)(2,1)S(1)} all-to-all(bf16[16,72,256]{2,1,0:T(8,128)(2,1)S(1)} %mix.1), channel_id=1, replica_groups=mesh['lat'=16,'lon'=16] {'lon'}, dimensions={0} | all-to-all | bytes 1179648 | tf_op jit(solution)/shard_map/all_to_all | solution.py:427
  159.4 0.8 synthesise.1
  160.3 38.7 %all_to_all.33 = bf16[256,9,2,128]{3,2,1,0:T(2,128)(2,1)S(1)} all-to-all(bf16[256,9,2,128]{3,2,1,0:T(2,128)(2,1)S(1)} %bitcast.21), channel_id=1, replica_groups=mesh['lat'=16,'lon'=16] {'lat','lon'}, dimensions={0} | all-to-all | bytes 2359296 | tf_op jit(solution)/shard_map/all_to_all | solution.py:422
  199.0 0.0 copy-done
  199.0 2.3 invert.1
  201.2 61.6 %all_to_all.34 = bf16[16,270,2,128]{3,2,1,0:T(2,128)(2,1)S(1)} all-to-all(bf16[16,270,2,128]{3,2,1,0:T(2,128)(2,1)S(1)} %bitcast.17), channel_id=1, replica_groups=mesh['lat'=16,'lon'=16] {'lon'}, dimensions={0} | all-to-all | bytes 4423680 | tf_op jit(solution)/shard_map/all_to_all | solution.py:422
  262.9 2.0 unpack.1
  (15 shorter events, 0.1 us)
Async XLA Ops:
  1.2 23.4 %collective-permute-start = (bf16[24,80,128]{2,1,0:T(8,128)(2,1)S(1)}, bf16[24,80,128]{2,1,0:T(8,128)(2,1)S(1)}, u32[]{:S(2)}, u32[]{:S(2)}) collective-permute-start(bf16[24,80,128]{2,1,0:T(8,128)(2,1)S(1)} %get-tuple-element.10), channel_id=1, source_target_pairs={{0,15},{1,2},{2,1},{3,4},{4,3},{5,6},{6,5},{7,8},{8,7},{9,10},{10,... | collective-permute-start | bytes 1474568 | tf_op jit(solution)/shard_map/ppermute | solution.py:436
  3.1 21.6 %collective-permute-start.1 = (bf16[24,80,128]{2,1,0:T(8,128)(2,1)S(1)}, bf16[24,80,128]{2,1,0:T(8,128)(2,1)S(1)}, u32[]{:S(2)}, u32[]{:S(2)}) collective-permute-start(bf16[24,80,128]{2,1,0:T(8,128)(2,1)S(1)} %get-tuple-element.9), channel_id=1, source_target_pairs={{0,1},{1,0},{2,3},{3,2},{4,5},{5,4},{6,7},{7,6},{8,9},{9,8},{10,11... | collective-permute-start | bytes 1474568 | tf_op jit(solution)/shard_map/ppermute | solution.py:441
  10.0 8.3 %copy-start.10 = (f32[8]{0:T(128)}, f32[8]{0:T(128)S(1)}, u32[]{:S(2)}) copy-start(f32[8]{0:T(128)S(1)} %add_convert_fusion) | copy-start | bytes 100
  18.4 6.3 %copy-start.1 = (bf16[48,80,128]{2,1,0:T(8,128)(2,1)S(1)}, bf16[48,80,128]{2,1,0:T(8,128)(2,1)}, u32[]{:S(2)}) copy-start(bf16[48,80,128]{2,1,0:T(8,128)(2,1)} %own.1) | copy-start | bytes 2949124
  19.3 3.3 %copy-start.9 = (s32[180]{0:T(256)S(1)}, s32[180]{0:T(256)}, u32[]{:S(2)}) copy-start(s32[180]{0:T(256)} %and_select_fusion) | copy-start | bytes 2164
  24.7 10.4 %copy-start.8 = (f32[768]{0:T(1024)S(1)}, f32[768]{0:T(1024)}, u32[]{:S(2)}) copy-start(f32[768]{0:T(1024)} %fusion.32) | copy-start | bytes 9220
  28.9 8.4 %copy-start.11 = (f32[8]{0:T(128)S(1)}, f32[8]{0:T(128)}, u32[]{:S(2)}) copy-start(f32[8]{0:T(128)} %get-tuple-element.18) | copy-start | bytes 100
  28.9 8.5 %copy-start.7 = (f32[768]{0:T(1024)S(1)}, f32[768]{0:T(1024)}, u32[]{:S(2)}) copy-start(f32[768]{0:T(1024)} %fusion.30) | copy-start | bytes 9220
  28.9 8.5 %copy-start.6 = (f32[768]{0:T(1024)S(1)}, f32[768]{0:T(1024)}, u32[]{:S(2)}) copy-start(f32[768]{0:T(1024)} %broadcast_multiply_fusion) | copy-start | bytes 9220
  28.9 29.9 %all-to-all-start = ((bf16[16,90,2,128]{3,2,1,0:T(2,128)(2,1)}), bf16[16,90,2,128]{3,2,1,0:T(2,128)(2,1)}, u32[]{:S(2)}, u32[]{:S(2)}) async-start(bf16[16,90,2,128]{3,2,1,0:T(2,128)(2,1)} %bitcast.1), calls=%async_computation | async-start | bytes 1474560 | tf_op jit(solution)/shard_map/all_to_all | solution.py:422
  36.4 4.2 %copy-start.5 = (bf16[80,256]{1,0:T(8,128)(2,1)S(1)}, bf16[80,256]{1,0:T(8,128)(2,1)}, u32[]{:S(2)}) copy-start(bf16[80,256]{1,0:T(8,128)(2,1)} %param.9) | copy-start | bytes 122884
  58.7 1.0 copy-start.3
  59.7 0.9 copy-start.4
  67.2 68.0 %copy-start.2 = (bf16[24,256,256]{2,1,0:T(8,128)(2,1)S(1)}, bf16[24,256,256]{2,1,0:T(8,128)(2,1)}, u32[]{:S(2)}) copy-start(bf16[24,256,256]{2,1,0:T(8,128)(2,1)} %spectral.1) | copy-start | bytes 9437188
  136.4 62.6 %copy-start = (bf16[1440,768]{1,0:T(8,128)(2,1)S(1)}, bf16[1440,768]{1,0:T(8,128)(2,1)}, u32[]{:S(2)}) copy-start(bf16[1440,768]{1,0:T(8,128)(2,1)} %multiply_convert_fusion.1.rest_0_.inverse) | copy-start | bytes 6635524

commit v4 on v3

--- a/solution.py
+++ b/solution.py
@@ -114,37 +114,57 @@
     )(offsets, across, own, beside, weight)
 
 
-def lift_kernel(cols, lift_in, lift_out, forward, *rest):
-    out, packed, scratch = rest[-3:]
+def lift_kernel(cols, matrices, *rest):
+    out, packed, scratch, lifted, first, second, table, sems = rest[-8:]
+    first[...] = jnp.zeros_like(first)
+    count = ITEMS * N_DEV
+    places = [first.at[row, row * CIN : (row + 1) * CIN] for row in range(ROWS)]
+    copies = [
+        pltpu.make_async_copy(matrices.at[count + C : count + C + CIN, :C], place, sems.at[row])
+        for row, place in enumerate(places)
+    ]
+    copies.append(
+        pltpu.make_async_copy(matrices.at[count : count + C, :C], second, sems.at[ROWS])
+    )
+    copies.append(pltpu.make_async_copy(matrices.at[:count], table, sems.at[ROWS + 1]))
+    for copy in copies:
+        copy.start()
     packed[...] = cols[...].astype(jnp.float32)
     halves = [packed[pl.ds(h, NLON, stride=2), :] for h in range(2)]
     values = jnp.concatenate(halves, axis=1).astype(jnp.bfloat16)
+    for copy in copies[:-1]:
+        copy.wait()
     for row in range(ROWS):
-        hidden = jax.nn.gelu(dot(values, lift_in[row])).astype(jnp.bfloat16)
-        lifted = dot(hidden, lift_out[...]).astype(jnp.bfloat16)
-        spectra = dot(forward[...], lifted)
-        for item in range(ITEMS):
-            for half in range(2):
-                place = (item * ROWS + row) * 2 + half
-                scratch[pl.ds(place, N_DEV, stride=PIECES), :] = spectra[
-                    item * N_DEV : (item + 1) * N_DEV, half * 128 : (half + 1) * 128
-                ]
+        hidden = jax.nn.gelu(dot(values, first[row])).astype(jnp.bfloat16)
+        lifted[:, row * C : (row + 1) * C] = dot(hidden, second[...]).astype(jnp.bfloat16)
+    copies[-1].wait()
+    for item in range(ITEMS):
+        spectra = dot(table[item * N_DEV : (item + 1) * N_DEV], lifted[...])
+        for piece in range(2 * ROWS):
+            scratch[pl.ds(item * 2 * ROWS + piece, N_DEV, stride=PIECES), :] = spectra[
+                :, piece * 128 : (piece + 1) * 128
+            ]
     out[...] = scratch[...].astype(jnp.bfloat16)
 
 
-def lift(cols, lift_in, lift_out, forward, tables):
+def lift(cols, matrices, tables):
     return pl.pallas_call(
         lift_kernel,
         out_shape=jax.ShapeDtypeStruct((N_DEV * PIECES, 128), jnp.bfloat16),
-        in_specs=[whole()] * 4 + [pl.BlockSpec(memory_space=pl.ANY)] * len(tables),
+        in_specs=[whole()] + [pl.BlockSpec(memory_space=pl.ANY)] * (1 + len(tables)),
         out_specs=whole(),
         scratch_shapes=[
             pltpu.VMEM((2 * NLON, 128), jnp.float32),
             pltpu.VMEM((N_DEV * PIECES, 128), jnp.float32),
+            pltpu.VMEM((NLON, ROWS * C), jnp.bfloat16),
+            pltpu.VMEM((ROWS, C, C), jnp.bfloat16),
+            pltpu.VMEM((C, C), jnp.bfloat16),
+            pltpu.VMEM((ITEMS * N_DEV, NLON), jnp.bfloat16),
+            pltpu.SemaphoreType.DMA((ROWS + 2,)),
         ],
         compiler_params=params(48),
         name="lift",
-    )(cols, lift_in, lift_out, forward, *tables)
+    )(cols, matrices, *tables)
 
 
 def legendre_kernel(rise, fall, start, initial, restore, factor, cosine, quad, weighted, plain, table):
@@ -336,21 +356,22 @@
 
 
 TILES = 2 * ROWS
+INVERT_BLOCK = NLON // 3
 
 
 def inverse_kernel(pieces, inverse, out, scratch, packed):
     scratch[...] = pieces[...].astype(jnp.float32)
-    for row in range(ROWS):
-        items = []
-        for item in range(ITEMS):
-            place = (item * ROWS + row) * 2
-            halves = [scratch[pl.ds(place + h, N_DEV, stride=PIECES), :] for h in range(2)]
-            items.append(jnp.concatenate(halves, axis=1).astype(jnp.bfloat16))
-        spectra = jnp.concatenate(items, axis=0)
-        field = dot(inverse[...], spectra)
-        for half in range(2):
-            packed[pl.ds(row * 2 + half, NLON, stride=TILES), :] = field[
-                :, half * 128 : (half + 1) * 128
+    items = []
+    for item in range(ITEMS):
+        places = [item * TILES + piece for piece in range(TILES)]
+        parts = [scratch[pl.ds(place, N_DEV, stride=PIECES), :] for place in places]
+        items.append(jnp.concatenate(parts, axis=1).astype(jnp.bfloat16))
+    spectra = jnp.concatenate(items, axis=0)
+    for start in range(0, NLON, INVERT_BLOCK):
+        field = dot(inverse[start : start + INVERT_BLOCK], spectra)
+        for piece in range(TILES):
+            packed[pl.ds(start * TILES + piece, INVERT_BLOCK, stride=TILES), :] = field[
+                :, piece * 128 : (piece + 1) * 128
             ]
     out[...] = packed[...].astype(jnp.bfloat16)
 
@@ -396,8 +417,9 @@
     )(pieces)
 
 
-def fourier(item_axis):
-    shape = (ITEMS * N_DEV, 1) if item_axis == 0 else (1, ITEMS * N_DEV)
+def fourier(item_axis, extra=0):
+    items = ITEMS * N_DEV + extra
+    shape = (items, 1) if item_axis == 0 else (1, items)
     index = lax.broadcasted_iota(jnp.int32, shape, item_axis)
     device = index % N_DEV
     order = (index // N_DEV) * (L // ITEMS) + device // 2
@@ -415,6 +437,14 @@
     for term in (1.0 / 362880.0, -1.0 / 5040.0, 1.0 / 120.0, -1.0 / 6.0, 1.0):
         total = total * square + term
     return (total * angle).astype(jnp.bfloat16)
+
+
+def lift_matrices(lift_in, lift_out):
+    table = fourier(0, C + CIN)
+    rows, wide = table.shape[0], (0, NLON - C)
+    below = jnp.pad(lift_out, ((ITEMS * N_DEV, CIN), wide)) + jnp.pad(lift_in, ((rows - CIN, 0), wide))
+    index = lax.broadcasted_iota(jnp.int32, (rows, 1), 0)
+    return jnp.where(index < ITEMS * N_DEV, table, below)
 
 
 def exchange(values, axes, count):
@@ -447,18 +477,12 @@
     places = jnp.concatenate(
         [offsets.reshape(LAT_DEV * K), (odd * (RIM + SRC_DEV)).reshape(1).astype(jnp.int32)]
     )
-    forward = fourier(0)
+    matrices = lift_matrices(lift_in, lift_out)
     inverse = fourier(1)
     weighted, plain = legendre(chip)
-    lift_blocks = jnp.stack(
-        [
-            jnp.pad(lift_in, ((row * CIN, C - (row + 1) * CIN), (0, 0)))
-            for row in range(ROWS)
-        ]
-    )
     columns = remap(places, across, cube_cells, beside, block_weight)
     columns = exchange(columns, "lon", N_LON)
-    spectra = lift(columns, lift_blocks, lift_out, forward, (inverse, weighted, plain))
+    spectra = lift(columns, matrices, (inverse, weighted, plain))
     spectra = exchange(spectra, ("lat", "lon"), N_DEV)
     analysis = regroup(analyse(spectra, weighted))
     mixed = regroup(mix(analysis, spectral))

time: 265 us -> 263 us (level)
    select_n x0 -> x1, other arithmetic: none -> 7.57 us  [lift_matrices(): return jnp.where(index < ITEMS * N_DEV, table, below)]
    convert_element_type x2 -> x1, other arithmetic: 9.59 us -> 4.71 us  [fourier(): return (total * angle).astype(jnp.bfloat16)]
where the time goes in v4:
time: 263 us
  blocking collectives  190 us (72%)
  Pallas kernels  20.6 us (8%)
  other arithmetic  16.7 us (6%)
  waiting for transfers between devices  14.3 us (5%)
  starting transfers between devices  13.7 us (5%)
  local copies, waits for them, and re-layouts  7.4 us (3%)
    all_to_all x3, blocking collectives, exchange(): pairs = lax.all_to_all(pairs, axes, split_axis=0, concat_axis=0, tiled=True)  140 us
    all_to_all x2, blocking collectives, regroup(): lax.all_to_all(values, 'lon', split_axis=0, concat_axis=0, tiled=True)  50.1 us
    all_to_all x1, waiting for transfers between devices, exchange(): pairs = lax.all_to_all(pairs, axes, split_axis=0, concat_axis=0, tiled=True)  14.3 us
    select_n x1, other arithmetic, lift_matrices(): return jnp.where(index < ITEMS * N_DEV, table, below)  7.57 us
    ppermute x1, starting transfers between devices, shards(): lax.ppermute(lax.dynamic_slice_in_dim(cube_cells, (1 - odd) * far, RIM, 0...  6.83 us
    pallas_call x1, Pallas kernels, lift(): pl.pallas_call(lift_kernel, out_shape=jax.ShapeDtypeStruct((N_DEV * PIECE...  6.19 us
  transfers between devices with their start and end apart: 3, of which 1 were waited for; matrix products, arithmetic and copies ran while one was open for 9% of the time, Pallas kernels for 1%

profile of v4, /device:TPU:33, one launch (start us, length us, event | category | flops | bytes accessed | tf_op | source)
XLA Modules:
  0.0 263.4 jit_solution(4548236383333328756)
XLA Ops:
  0.0 1.2 constant_dynamic-slice_fusion
  1.2 1.9 collective-permute-start
  3.1 6.8 %collective-permute-start.1 = (bf16[24,80,128]{2,1,0:T(8,128)(2,1)S(1)}, bf16[24,80,128]{2,1,0:T(8,128)(2,1)S(1)}, u32[]{:S(2)}, u32[]{:S(2)}) collective-permute-start(bf16[24,80,128]{2,1,0:T(8,128)(2,1)S(1)} %get-tuple-element.9), channel_id=1, source_target_pairs={{0,1},{1,0},{2,3},{3,2},{4,5},{5,4},{6,7},{7,6},{8,9},{9,8},{10,11... | collective-permute-start | bytes 1474568 | tf_op jit(solution)/shard_map/ppermute | solution.py:471
  10.0 0.0 copy-start.4
  10.0 0.7 compare_select_fusion.3
  10.7 0.7 add_remainder_fusion
  11.4 0.1 copy.10
  11.5 0.1 rem.200
  11.6 0.7 compare_select_fusion
  12.3 0.1 divide_sqrt_fusion
  12.4 7.6 %fusion.6.matrices = bf16[1104,1440]{1,0:T(8,128)(2,1)} fusion(bf16[80,256]{1,0:T(8,128)(2,1)} %param.9, bf16[256,256]{1,0:T(8,128)(2,1)} %param.10, f32[1104]{0:T(1024)S(1)} %fusion.17, f32[1104]{0:T(1024)S(1)} %fusion.15, f32[1440]{0:T(1024)S(1)} %iota_convert_fusion, pred[1104]{0:T(1024)(128)(4,1)S(1)} %iota_compare_fusion), kind=kLoop, calls=%fused_computation.14 | loop fusion | flops 42923520 | bytes 3367248 | tf_op jit(solution)/shard_map/jit(_where)/select_n | solution.py:447
  20.0 0.6 fusion.47
  20.6 0.1 copy.12
  20.7 0.0 copy-done.4
  20.7 0.1 copy.13
  20.8 0.0 copy-start.1
  20.8 0.9 copy.14
  21.8 3.3 %copy.11.weight = bf16[45,1,4,90,128]{4,3,2,1,0:T(8,128)(2,1)S(1)} copy(bf16[45,1,4,90,128]{4,2,3,1,0:T(4,128)(2,1)} %param.8) | data formatting | bytes 8294400 | tf_op args[2]
  25.1 0.1 pad_add_fusion.offsets
  25.1 0.7 fusion.50
  25.8 0.1 fusion.48
  25.8 0.1 broadcast_multiply_fusion
  25.9 0.0 collective-permute-done.across
  25.9 0.0 copy-start.3
  25.9 0.0 collective-permute-done.1.beside
  25.9 0.0 copy-done.1
  25.9 4.2 %remap.1 = bf16[2880,128]{1,0:T(8,128)(2,1)} custom-call(s32[181]{0:T(256)S(1)} %pad_add_fusion.offsets, bf16[24,80,128]{2,1,0:T(8,128)(2,1)S(1)} %collective-permute-done.across, bf16[48,80,128]{2,1,0:T(8,128)(2,1)S(1)} %copy-done.1, bf16[24,80,128]{2,1,0:T(8,128)(2,1)S(1)} %collective-permute-done.1.beside, bf16[45,1,4,90,128]{4,3,2,1,0:T(8,128)(2,1)S(1)} %copy.11.weight), custom_call_target="tpu_custom_call" | custom-call | tf_op jit(solution)/shard_map/remap/pallas_call | solution.py:92
  30.1 0.0 copy-start.5
  30.1 5.0 %all-to-all-start = ((bf16[16,90,2,128]{3,2,1,0:T(2,128)(2,1)}), bf16[16,90,2,128]{3,2,1,0:T(2,128)(2,1)}, u32[]{:S(2)}, u32[]{:S(2)}) async-start(bf16[16,90,2,128]{3,2,1,0:T(2,128)(2,1)} %bitcast.1), calls=%async_computation | async-start | bytes 1474560 | tf_op jit(solution)/shard_map/all_to_all | solution.py:452
  35.1 0.0 copy-done.3
  35.1 0.8 exponential_select_fusion
  35.9 0.5 broadcast_in_dim.39.rise
  36.4 0.5 broadcast_in_dim.40.fall
  36.8 0.5 broadcast_in_dim.41.start
  37.3 0.0 copy-done.5
  37.3 0.1 broadcast_in_dim.43.factor
  37.4 3.1 %legendre.1 = (bf16[3,384,768]{2,1,0:T(8,128)(2,1)S(1)}, bf16[3,768,384]{2,1,0:T(8,128)(2,1)S(1)}) custom-call(f32[384,8,128]{2,1,0:T(8,128)S(1)} %broadcast_in_dim.39.rise, f32[384,8,128]{2,1,0:T(8,128)S(1)} %broadcast_in_dim.40.fall, f32[384,8,128]{2,1,0:T(8,128)S(1)} %broadcast_in_dim.41.start, f32[8,768]{1,0:T(8,128)S(1)} %get-tuple-element.12.initial, ...), custom_call_target="tpu_custom_call" | custom-call | tf_op jit(solution)/shard_map/legendre/pallas_call | solution.py:238
  40.5 4.7 %multiply_convert_fusion.1.rest_0_.inverse = bf16[1440,768]{1,0:T(8,128)(2,1)} fusion(f32[768]{0:T(1024)S(1)} %fusion.33, f32[768]{0:T(1024)S(1)} %fusion.31, f32[1440]{0:T(1024)S(1)} %iota_convert_fusion), kind=kLoop, calls=%fused_computation.7 | loop fusion | flops 24330240 | bytes 2223744 | tf_op jit(solution)/shard_map/convert_element_type | solution.py:439
  45.2 14.3 %all-to-all-done = bf16[16,90,2,128]{3,2,1,0:T(2,128)(2,1)} async-done(((bf16[16,90,2,128]{3,2,1,0:T(2,128)(2,1)}), bf16[16,90,2,128]{3,2,1,0:T(2,128)(2,1)}, u32[]{:S(2)}, u32[]{:S(2)}) %all-to-all-start) | async-done | bytes 737312 | tf_op jit(solution)/shard_map/all_to_all | solution.py:452
  59.5 6.2 %lift.1 = bf16[4608,128]{1,0:T(8,128)(2,1)S(1)} custom-call(bf16[2880,128]{1,0:T(8,128)(2,1)} %bitcast.2.cols, bf16[1104,1440]{1,0:T(8,128)(2,1)} %fusion.6.matrices, bf16[1440,768]{1,0:T(8,128)(2,1)} %multiply_convert_fusion.1.rest_0_.inverse, bf16[3,384,768]{2,1,0:T(8,128)(2,1)S(1)} %get-tuple-element.7.rest_1_.weighted, ...), custom_call_target="tpu_custom_call" | custom-call | tf_op jit(solution)/shard_map/lift/pallas_call | solution.py:151
  65.7 0.0 copy-start.2
  65.7 40.0 %all_to_all.30 = bf16[256,9,2,128]{3,2,1,0:T(2,128)(2,1)S(1)} all-to-all(bf16[256,9,2,128]{3,2,1,0:T(2,128)(2,1)S(1)} %bitcast.15), channel_id=1, replica_groups=mesh['lat'=16,'lon'=16] {'lat','lon'}, dimensions={0} | all-to-all | bytes 2359296 | tf_op jit(solution)/shard_map/all_to_all | solution.py:452
  105.8 0.7 analyse.1
  106.5 27.1 %all_to_all.31.pieces = bf16[16,72,256]{2,1,0:T(8,128)(2,1)S(1)} all-to-all(bf16[16,72,256]{2,1,0:T(8,128)(2,1)S(1)} %analyse.1), channel_id=1, replica_groups=mesh['lat'=16,'lon'=16] {'lon'}, dimensions={0} | all-to-all | bytes 1179648 | tf_op jit(solution)/shard_map/all_to_all | solution.py:457
  133.6 0.0 copy-done.2
  133.6 1.2 mix.1
  134.9 0.0 copy-start
  134.9 23.0 %all_to_all.32.pieces = bf16[16,72,256]{2,1,0:T(8,128)(2,1)S(1)} all-to-all(bf16[16,72,256]{2,1,0:T(8,128)(2,1)S(1)} %mix.1), channel_id=1, replica_groups=mesh['lat'=16,'lon'=16] {'lon'}, dimensions={0} | all-to-all | bytes 1179648 | tf_op jit(solution)/shard_map/all_to_all | solution.py:457
  157.9 0.8 synthesise.1
  158.8 38.7 %all_to_all.33 = bf16[256,9,2,128]{3,2,1,0:T(2,128)(2,1)S(1)} all-to-all(bf16[256,9,2,128]{3,2,1,0:T(2,128)(2,1)S(1)} %bitcast.14), channel_id=1, replica_groups=mesh['lat'=16,'lon'=16] {'lat','lon'}, dimensions={0} | all-to-all | bytes 2359296 | tf_op jit(solution)/shard_map/all_to_all | solution.py:452
  197.5 0.0 copy-done
  197.5 2.2 invert.1
  199.7 61.6 %all_to_all.34 = bf16[16,270,2,128]{3,2,1,0:T(2,128)(2,1)S(1)} all-to-all(bf16[16,270,2,128]{3,2,1,0:T(2,128)(2,1)S(1)} %bitcast.11), channel_id=1, replica_groups=mesh['lat'=16,'lon'=16] {'lon'}, dimensions={0} | all-to-all | bytes 4423680 | tf_op jit(solution)/shard_map/all_to_all | solution.py:452
  261.3 2.0 unpack.1
  (14 shorter events, 0.1 us)
Async XLA Ops:
  1.2 24.7 %collective-permute-start = (bf16[24,80,128]{2,1,0:T(8,128)(2,1)S(1)}, bf16[24,80,128]{2,1,0:T(8,128)(2,1)S(1)}, u32[]{:S(2)}, u32[]{:S(2)}) collective-permute-start(bf16[24,80,128]{2,1,0:T(8,128)(2,1)S(1)} %get-tuple-element.10), channel_id=1, source_target_pairs={{0,15},{1,2},{2,1},{3,4},{4,3},{5,6},{6,5},{7,8},{8,7},{9,10},{10,... | collective-permute-start | bytes 1474568 | tf_op jit(solution)/shard_map/ppermute | solution.py:466
  3.1 22.8 %collective-permute-start.1 = (bf16[24,80,128]{2,1,0:T(8,128)(2,1)S(1)}, bf16[24,80,128]{2,1,0:T(8,128)(2,1)S(1)}, u32[]{:S(2)}, u32[]{:S(2)}) collective-permute-start(bf16[24,80,128]{2,1,0:T(8,128)(2,1)S(1)} %get-tuple-element.9), channel_id=1, source_target_pairs={{0,1},{1,0},{2,3},{3,2},{4,5},{5,4},{6,7},{7,6},{8,9},{9,8},{10,11... | collective-permute-start | bytes 1474568 | tf_op jit(solution)/shard_map/ppermute | solution.py:471
  10.0 10.7 %copy-start.4 = (f32[8]{0:T(128)}, f32[8]{0:T(128)S(1)}, u32[]{:S(2)}) copy-start(f32[8]{0:T(128)S(1)} %add_convert_fusion) | copy-start | bytes 100
  20.8 5.1 %copy-start.1 = (bf16[48,80,128]{2,1,0:T(8,128)(2,1)S(1)}, bf16[48,80,128]{2,1,0:T(8,128)(2,1)}, u32[]{:S(2)}) copy-start(bf16[48,80,128]{2,1,0:T(8,128)(2,1)} %own.1) | copy-start | bytes 2949124
  25.9 9.2 %copy-start.3 = (f32[768]{0:T(1024)S(1)}, f32[768]{0:T(1024)}, u32[]{:S(2)}) copy-start(f32[768]{0:T(1024)} %fusion.50) | copy-start | bytes 9220
  30.1 7.2 %copy-start.5 = (f32[8]{0:T(128)S(1)}, f32[8]{0:T(128)}, u32[]{:S(2)}) copy-start(f32[8]{0:T(128)} %get-tuple-element.15) | copy-start | bytes 100
  30.1 29.4 %all-to-all-start = ((bf16[16,90,2,128]{3,2,1,0:T(2,128)(2,1)}), bf16[16,90,2,128]{3,2,1,0:T(2,128)(2,1)}, u32[]{:S(2)}, u32[]{:S(2)}) async-start(bf16[16,90,2,128]{3,2,1,0:T(2,128)(2,1)} %bitcast.1), calls=%async_computation | async-start | bytes 1474560 | tf_op jit(solution)/shard_map/all_to_all | solution.py:452
  65.7 67.9 %copy-start.2 = (bf16[24,256,256]{2,1,0:T(8,128)(2,1)S(1)}, bf16[24,256,256]{2,1,0:T(8,128)(2,1)}, u32[]{:S(2)}) copy-start(bf16[24,256,256]{2,1,0:T(8,128)(2,1)} %spectral.1) | copy-start | bytes 9437188
  134.9 62.6 %copy-start = (bf16[1440,768]{1,0:T(8,128)(2,1)S(1)}, bf16[1440,768]{1,0:T(8,128)(2,1)}, u32[]{:S(2)}) copy-start(bf16[1440,768]{1,0:T(8,128)(2,1)} %multiply_convert_fusion.1.rest_0_.inverse) | copy-start | bytes 6635524

commit v5 on v4

--- a/solution.py
+++ b/solution.py
@@ -43,72 +43,45 @@
     return lax.dot_general(a, b, (dims, ((), ())), preferred_element_type=jnp.float32)
 
 
-REMAP_STEPS = 4
-STEP_GROUPS = N_LON // REMAP_STEPS
 GROUP_ROWS = 2 * LON_DEV
 
 
-def remap_kernel(offsets, across, own, beside, weight, out, tiles, packed):
-    step = pl.program_id(0)
-
-    @pl.when(step == 0)
-    def _():
-        place = offsets[LAT_DEV * K]
-        tiles[pl.ds(place, RIM)] = across[...]
-        tiles[pl.ds(RIM + SRC_DEV - place, RIM)] = beside[...]
-        tiles[RIM : RIM + SRC_DEV] = own[...]
-
-    def store(sub, values):
+def remap_kernel(offsets, across, own, beside, weight, out, zero, tiles, packed):
+    place = offsets[LAT_DEV * K]
+    tiles[pl.ds(place, RIM)] = across[...]
+    tiles[pl.ds(RIM + SRC_DEV - place, RIM)] = beside[...]
+    tiles[RIM : RIM + SRC_DEV] = own[...]
+    zero[...] = jnp.zeros_like(zero)
+    for group in range(GROUPS):
+        columns = []
+        for row in range(group * ROWS, (group + 1) * ROWS):
+            cells = jnp.concatenate([tiles[offsets[row * K + k]] for k in range(K)], axis=1)
+            blocks = jnp.concatenate([weight[row, 0, k] for k in range(K)], axis=1)
+            columns.append(dot(blocks, cells, ((1,), (1,))))
+        columns.append(jnp.zeros((LON_DEV, C - ROWS * CIN), jnp.float32))
+        values = jnp.concatenate(columns, axis=1)
         for half in range(2):
-            packed[pl.ds(sub * GROUP_ROWS + half, LON_DEV, stride=2), :] = values[
+            packed[pl.ds(group * GROUP_ROWS + half, LON_DEV, stride=2), :] = values[
                 :, half * 128 : (half + 1) * 128
             ]
-
-    def fill(sub):
-        columns = []
-        for row in range(ROWS):
-            base = ((step * STEP_GROUPS + sub) * ROWS + row) * K
-            cells = jnp.concatenate([tiles[offsets[base + k]] for k in range(K)], axis=1)
-            blocks = jnp.concatenate([weight[sub * ROWS + row, 0, k] for k in range(K)], axis=1)
-            columns.append(dot(blocks, cells, ((1,), (1,))))
-        columns.append(jnp.zeros((LON_DEV, C - ROWS * CIN), jnp.float32))
-        store(sub, jnp.concatenate(columns, axis=1))
-
-    for sub in range(STEP_GROUPS - 1):
-        fill(sub)
-
-    @pl.when(step < REMAP_STEPS - 1)
-    def _():
-        fill(STEP_GROUPS - 1)
-
-    @pl.when(step == REMAP_STEPS - 1)
-    def _():
-        store(STEP_GROUPS - 1, jnp.zeros((LON_DEV, C), jnp.float32))
-
+    packed[GROUPS * GROUP_ROWS :] = jnp.zeros(((N_LON - GROUPS) * GROUP_ROWS, 128), jnp.float32)
     out[...] = packed[...].astype(jnp.bfloat16)
 
 
 def remap(offsets, across, own, beside, weight):
     return pl.pallas_call(
         remap_kernel,
-        out_shape=jax.ShapeDtypeStruct((N_LON * GROUP_ROWS, 128), jnp.bfloat16),
-        grid_spec=pltpu.PrefetchScalarGridSpec(
-            num_scalar_prefetch=1,
-            grid=(REMAP_STEPS,),
-            in_specs=[
-                pl.BlockSpec((RIM, CIN, TILE), lambda g, o: (0, 0, 0)),
-                pl.BlockSpec((SRC_DEV, CIN, TILE), lambda g, o: (0, 0, 0)),
-                pl.BlockSpec((RIM, CIN, TILE), lambda g, o: (0, 0, 0)),
-                pl.BlockSpec(
-                    (STEP_GROUPS * ROWS, 1, K, LON_DEV, TILE), lambda g, o: (g, 0, 0, 0, 0)
-                ),
-            ],
-            out_specs=pl.BlockSpec((STEP_GROUPS * GROUP_ROWS, 128), lambda g, o: (g, 0)),
-            scratch_shapes=[
-                pltpu.VMEM((RIM + SRC_DEV + RIM, CIN, TILE), jnp.bfloat16),
-                pltpu.VMEM((STEP_GROUPS * GROUP_ROWS, 128), jnp.float32),
-            ],
+        out_shape=(
+            jax.ShapeDtypeStruct((N_LON * GROUP_ROWS, 128), jnp.bfloat16),
+            jax.ShapeDtypeStruct((8, 128), jnp.float32),
         ),
+        grid=(1,),
+        in_specs=[pl.BlockSpec(memory_space=pltpu.SMEM)] + [whole()] * 4,
+        out_specs=(pl.BlockSpec((N_LON * GROUP_ROWS, 128), lambda g: (0, 0)), whole()),
+        scratch_shapes=[
+            pltpu.VMEM((RIM + SRC_DEV + RIM, CIN, TILE), jnp.bfloat16),
+            pltpu.VMEM((N_LON * GROUP_ROWS, 128), jnp.float32),
+        ],
         compiler_params=params(40),
         name="remap",
     )(offsets, across, own, beside, weight)
@@ -126,19 +99,23 @@
     copies.append(
         pltpu.make_async_copy(matrices.at[count : count + C, :C], second, sems.at[ROWS])
     )
-    copies.append(pltpu.make_async_copy(matrices.at[:count], table, sems.at[ROWS + 1]))
+    for item in range(ITEMS):
+        block = pl.ds(item * N_DEV, N_DEV)
+        copies.append(
+            pltpu.make_async_copy(matrices.at[block], table.at[block], sems.at[ROWS + 1 + item])
+        )
     for copy in copies:
         copy.start()
     packed[...] = cols[...].astype(jnp.float32)
     halves = [packed[pl.ds(h, NLON, stride=2), :] for h in range(2)]
     values = jnp.concatenate(halves, axis=1).astype(jnp.bfloat16)
-    for copy in copies[:-1]:
+    for copy in copies[: ROWS + 1]:
         copy.wait()
     for row in range(ROWS):
         hidden = jax.nn.gelu(dot(values, first[row])).astype(jnp.bfloat16)
         lifted[:, row * C : (row + 1) * C] = dot(hidden, second[...]).astype(jnp.bfloat16)
-    copies[-1].wait()
-    for item in range(ITEMS):
+    for item in range(ITEMS):
+        copies[ROWS + 1 + item].wait()
         spectra = dot(table[item * N_DEV : (item + 1) * N_DEV], lifted[...])
         for piece in range(2 * ROWS):
             scratch[pl.ds(item * 2 * ROWS + piece, N_DEV, stride=PIECES), :] = spectra[
@@ -160,14 +137,16 @@
             pltpu.VMEM((ROWS, C, C), jnp.bfloat16),
             pltpu.VMEM((C, C), jnp.bfloat16),
             pltpu.VMEM((ITEMS * N_DEV, NLON), jnp.bfloat16),
-            pltpu.SemaphoreType.DMA((ROWS + 2,)),
+            pltpu.SemaphoreType.DMA((ROWS + 1 + ITEMS,)),
         ],
         compiler_params=params(48),
         name="lift",
     )(cols, matrices, *tables)
 
 
-def legendre_kernel(rise, fall, start, initial, restore, factor, cosine, quad, weighted, plain, table):
+def legendre_kernel(
+    rise, fall, start, initial, restore, factor, cosine, quad, after, weighted, plain, table
+):
     tiles = LATS // 128
     cos = [cosine[:, t * 128 : (t + 1) * 128] for t in range(tiles)]
     init = [initial[:, t * 128 : (t + 1) * 128] for t in range(tiles)]
@@ -196,7 +175,7 @@
             plain[item, lanes, :] = values.T.astype(jnp.bfloat16)
 
 
-def legendre(chip):
+def legendre(chip, after):
     lane = jnp.arange(LATS, dtype=jnp.int32)
     row, device = lane // N_DEV, lane % N_DEV
     band, group = device // N_LON, device % N_LON
@@ -241,7 +220,7 @@
             jax.ShapeDtypeStruct((ITEMS, L, LATS), jnp.bfloat16),
             jax.ShapeDtypeStruct((ITEMS, LATS, L), jnp.bfloat16),
         ),
-        in_specs=[whole()] * 8,
+        in_specs=[whole()] * 8 + [pl.BlockSpec(memory_space=pl.ANY)],
         out_specs=(whole(), whole()),
         scratch_shapes=[pltpu.VMEM((LATS // 128, L * 8, 128), jnp.float32)],
         compiler_params=params(40),
@@ -255,6 +234,7 @@
         factor,
         jnp.broadcast_to(cosine, (8, LATS)),
         quad,
+        after,
     )
 
 
@@ -283,46 +263,28 @@
     )(pieces, weighted)
 
 
-MIX_STEPS = 4
-MIX_DEG = DEG // MIX_STEPS
-
-
 def mix_kernel(pieces, spectral, out, source, result):
-    step = pl.program_id(0)
     count = N_LON * ITEMS
-
-    @pl.when(step == 0)
-    def _():
-        values = pieces[...].astype(jnp.float32).reshape(count * DEG, C)
-        source[0] = values[:, :128]
-        source[1] = values[:, 128:]
-
-    for index in range(MIX_DEG):
-        degree = step * MIX_DEG + index
+    values = pieces[...].astype(jnp.float32).reshape(count * DEG, C)
+    source[0] = values[:, :128]
+    source[1] = values[:, 128:]
+    for degree in range(DEG):
         halves = [source[h, pl.ds(degree, count, stride=DEG), :] for h in range(2)]
         values = jnp.concatenate(halves, axis=1).astype(jnp.bfloat16)
-        mixed = dot(values, spectral[index])
+        mixed = dot(values, spectral[degree])
         for h in range(2):
             result[h, pl.ds(degree, count, stride=DEG), :] = mixed[:, h * 128 : (h + 1) * 128]
-
-    @pl.when(step == MIX_STEPS - 1)
-    def _():
-        for h in range(2):
-            values = result[h].reshape(N_LON, ITEMS * DEG, 128)
-            out[:, :, h * 128 : (h + 1) * 128] = values.astype(jnp.bfloat16)
+    for h in range(2):
+        values = result[h].reshape(N_LON, ITEMS * DEG, 128)
+        out[:, :, h * 128 : (h + 1) * 128] = values.astype(jnp.bfloat16)
 
 
 def mix(pieces, spectral):
-    shape = (N_LON, ITEMS * DEG, C)
     return pl.pallas_call(
         mix_kernel,
-        out_shape=jax.ShapeDtypeStruct(shape, jnp.bfloat16),
-        grid=(MIX_STEPS,),
-        in_specs=[
-            pl.BlockSpec(shape, lambda g: (0, 0, 0)),
-            pl.BlockSpec((MIX_DEG, C, C), lambda g: (g, 0, 0)),
-        ],
-        out_specs=pl.BlockSpec(shape, lambda g: (0, 0, 0)),
+        out_shape=jax.ShapeDtypeStruct((N_LON, ITEMS * DEG, C), jnp.bfloat16),
+        in_specs=[whole()] * 2,
+        out_specs=whole(),
         scratch_shapes=[pltpu.VMEM((2, N_LON * ITEMS * DEG, 128), jnp.float32)] * 2,
         compiler_params=params(40),
         name="mix",
@@ -417,7 +379,7 @@
     )(pieces)
 
 
-def fourier(item_axis, extra=0):
+def fourier(item_axis, extra=0, shift=0.0):
     items = ITEMS * N_DEV + extra
     shape = (items, 1) if item_axis == 0 else (1, items)
     index = lax.broadcasted_iota(jnp.int32, shape, item_axis)
@@ -430,6 +392,7 @@
     phase = longitude.astype(jnp.float32) * order.astype(jnp.float32) + 360.0 * part.astype(
         jnp.float32
     )
+    phase = phase + shift
     phase = phase - 1440.0 * jnp.round(phase * (1.0 / 1440.0))
     angle = (360.0 - jnp.abs(phase)) * (math.pi / 720.0)
     square = angle * angle
@@ -439,8 +402,8 @@
     return (total * angle).astype(jnp.bfloat16)
 
 
-def lift_matrices(lift_in, lift_out):
-    table = fourier(0, C + CIN)
+def lift_matrices(lift_in, lift_out, shift):
+    table = fourier(0, C + CIN, shift)
     rows, wide = table.shape[0], (0, NLON - C)
     below = jnp.pad(lift_out, ((ITEMS * N_DEV, CIN), wide)) + jnp.pad(lift_in, ((rows - CIN, 0), wide))
     index = lax.broadcasted_iota(jnp.int32, (rows, 1), 0)
@@ -477,10 +440,10 @@
     places = jnp.concatenate(
         [offsets.reshape(LAT_DEV * K), (odd * (RIM + SRC_DEV)).reshape(1).astype(jnp.int32)]
     )
-    matrices = lift_matrices(lift_in, lift_out)
     inverse = fourier(1)
-    weighted, plain = legendre(chip)
-    columns = remap(places, across, cube_cells, beside, block_weight)
+    columns, zero = remap(places, across, cube_cells, beside, block_weight)
+    matrices = lift_matrices(lift_in, lift_out, zero[0, 0])
+    weighted, plain = legendre(chip, zero)
     columns = exchange(columns, "lon", N_LON)
     spectra = lift(columns, matrices, (inverse, weighted, plain))
     spectra = exchange(spectra, ("lat", "lon"), N_DEV)

time: 263 us -> 268 us (1.019)
  other arithmetic: 16.7 us -> 22.7 us
  waiting for transfers between devices: 14.3 us -> 9.08 us
  local copies, waits for them, and re-layouts: 7.4 us -> 12.3 us
    all_to_all x1, waiting for transfers between devices: 14.3 us -> 9.08 us  [exchange(): pairs = lax.all_to_all(pairs, axes, split_axis=0, concat_axis=0, tiled=True)]
    unnamed x13 -> x27, local copies, waits for them, and re-layouts: 3.31 us -> 7.71 us
  transfers between devices with their start and end apart: 3 -> 3, of which waited for: 1 -> 1; matrix products, arithmetic and copies ran while one was open for 9% -> 12% of each run, Pallas kernels for 1% -> 1%
where the time goes in v5:
time: 268 us; the launch traced here: 267 us
  blocking collectives  190 us (71%)
  other arithmetic  22.7 us (8%)
  Pallas kernels  19.8 us (7%)
  starting transfers between devices  13 us (5%)
  local copies, waits for them, and re-layouts  12.3 us (5%)
  waiting for transfers between devices  9.08 us (3%)
    all_to_all x3, blocking collectives, exchange(): pairs = lax.all_to_all(pairs, axes, split_axis=0, concat_axis=0, tiled=True)  140 us
    all_to_all x2, blocking collectives, regroup(): lax.all_to_all(values, 'lon', split_axis=0, concat_axis=0, tiled=True)  50.1 us
    select_n x1, other arithmetic, lift_matrices(): return jnp.where(index < ITEMS * N_DEV, table, below)  10.2 us
    all_to_all x1, waiting for transfers between devices, exchange(): pairs = lax.all_to_all(pairs, axes, split_axis=0, concat_axis=0, tiled=True)  9.08 us
    unnamed x27, local copies, waits for them, and re-layouts  7.71 us
    pallas_call x1, Pallas kernels, lift(): pl.pallas_call(lift_kernel, out_shape=jax.ShapeDtypeStruct((N_DEV * PIECE...  6.95 us
    ppermute x1, starting transfers between devices, shards(): lax.ppermute(lax.dynamic_slice_in_dim(cube_cells, (1 - odd) * far, RIM, 0...  6.83 us
  transfers between devices with their start and end apart: 3, of which 1 were waited for; matrix products, arithmetic and copies ran while one was open for 12% of the time, Pallas kernels for 1%

profile of v5, /device:TPU:33, one launch (start us, length us, event | category | flops | bytes accessed | tf_op | source)
XLA Modules:
  0.0 267.4 jit_solution(10724735253966486031)
XLA Ops:
  0.0 1.2 constant_dynamic-slice_fusion
  1.2 1.9 collective-permute-start
  3.1 6.8 %collective-permute-start.1 = (bf16[24,80,128]{2,1,0:T(8,128)(2,1)S(1)}, bf16[24,80,128]{2,1,0:T(8,128)(2,1)S(1)}, u32[]{:S(2)}, u32[]{:S(2)}) collective-permute-start(bf16[24,80,128]{2,1,0:T(8,128)(2,1)S(1)} %get-tuple-element.13), channel_id=1, source_target_pairs={{0,1},{1,0},{2,3},{3,2},{4,5},{5,4},{6,7},{7,6},{8,9},{9,8},{10,11... | collective-permute-start | bytes 1474568 | tf_op jit(solution)/shard_map/ppermute | solution.py:434
  10.0 0.6 subtract_multiply_fusion
  10.5 0.7 fusion.50
  11.2 0.6 fusion.47
  11.8 0.6 fusion.48
  12.4 0.1 broadcast_multiply_fusion
  12.5 0.6 iota_compare_fusion
  13.1 0.7 add_remainder_fusion
  13.8 0.1 copy.10
  13.9 0.1 rem.200
  14.0 0.1 pad_add_fusion.offsets
  14.1 0.7 compare_select_fusion
  14.8 4.7 %multiply_convert_fusion.1.rest_0_.inverse = bf16[1440,768]{1,0:T(8,128)(2,1)} fusion(f32[768]{0:T(1024)S(1)} %fusion.33, f32[768]{0:T(1024)S(1)} %fusion.31, f32[1440]{0:T(1024)S(1)} %iota_convert_fusion), kind=kLoop, calls=%fused_computation.7 | loop fusion | flops 24330240 | bytes 2223744 | tf_op jit(solution)/shard_map/convert_element_type | solution.py:402
  19.5 0.1 divide_sqrt_fusion
  19.6 0.5 compare_select_fusion.3
  20.1 5.4 %copy.11.weight = bf16[45,1,4,90,128]{4,3,2,1,0:T(8,128)(2,1)} copy(bf16[45,1,4,90,128]{4,2,3,1,0:T(4,128)(2,1)} %param.8) | data formatting | bytes 8294400 | tf_op args[2]
  25.5 0.0 copy-done.11
  25.5 0.1 copy.12
  25.6 0.1 copy.13
  25.8 0.8 copy.14
  26.6 0.6 fusion.15
  27.2 0.6 fusion.17
  27.8 1.4 exponential_select_fusion
  29.2 0.0 collective-permute-done.across
  29.2 0.0 collective-permute-done.1.beside
  29.2 0.0 copy-done.2
  29.2 0.0 copy-start.1
  29.2 2.2 copy-done.1
  31.5 3.1 %remap.1 = (bf16[2880,128]{1,0:T(8,128)(2,1)}, f32[8,128]{1,0:T(8,128)S(1)}) custom-call(s32[181]{0:T(256)S(1)} %pad_add_fusion.offsets, bf16[24,80,128]{2,1,0:T(8,128)(2,1)S(1)} %collective-permute-done.across, bf16[48,80,128]{2,1,0:T(8,128)(2,1)S(1)} %copy-done.2, bf16[24,80,128]{2,1,0:T(8,128)(2,1)S(1)} %collective-permute-done.1.beside, ...), custom_call_target="tpu_custom_call" | custom-call | tf_op jit(solution)/shard_map/remap/pallas_call | solution.py:72
  34.6 0.6 slice.3
  35.2 4.4 %all-to-all-start = ((bf16[16,90,2,128]{3,2,1,0:T(2,128)(2,1)}), bf16[16,90,2,128]{3,2,1,0:T(2,128)(2,1)}, u32[]{:S(2)}, u32[]{:S(2)}) async-start(bf16[16,90,2,128]{3,2,1,0:T(2,128)(2,1)} %bitcast.1), calls=%async_computation | async-start | bytes 1474560 | tf_op jit(solution)/shard_map/all_to_all | solution.py:415
  39.5 0.0 copy-done.6
  39.5 0.0 copy-done.7
  39.5 0.0 copy-done.8
  39.6 0.0 copy-done.9
  39.6 0.0 copy-start.12
  39.6 0.0 copy-start.10
  39.6 0.0 copy-start.4
  39.6 0.0 copy-start.5
  39.6 10.2 %fusion.6.matrices = bf16[1104,1440]{1,0:T(8,128)(2,1)} fusion(bf16[80,256]{1,0:T(8,128)(2,1)S(1)} %copy-done.7, bf16[256,256]{1,0:T(8,128)(2,1)S(1)} %copy-done.6, f32[]{:T(128)} %bitcast.3, f32[1104]{0:T(1024)S(1)} %copy-done.9, f32[1104]{0:T(1024)S(1)} %copy-done.8, f32[1440]{0:T(1024)S(1)} %iota_convert_fusion, pred[1104]{0:T(1024)(128)(4,1)} %iota_compare_fusion), kind=kLoop, calls=%fused_computation.14 | loop fusion | flops 44513280 | bytes 3367252 | tf_op jit(solution)/shard_map/jit(_where)/select_n | solution.py:410
  49.8 0.5 broadcast_in_dim.39.rise
  50.3 0.5 broadcast_in_dim.40.fall
  50.8 0.5 broadcast_in_dim.41.start
  51.2 0.0 copy-done.12
  51.2 0.1 broadcast_in_dim.43.factor
  51.3 0.0 copy-done.10
  51.3 0.0 copy-done.4
  51.3 3.1 %legendre.1 = (bf16[3,384,768]{2,1,0:T(8,128)(2,1)S(1)}, bf16[3,768,384]{2,1,0:T(8,128)(2,1)S(1)}) custom-call(f32[384,8,128]{2,1,0:T(8,128)S(1)} %broadcast_in_dim.39.rise, f32[384,8,128]{2,1,0:T(8,128)S(1)} %broadcast_in_dim.40.fall, f32[384,8,128]{2,1,0:T(8,128)S(1)} %broadcast_in_dim.41.start, f32[8,768]{1,0:T(8,128)S(1)} %copy-done.5, ...), custom_call_target="tpu_custom_call" | custom-call | tf_op jit(solution)/shard_map/legendre/pallas_call | solution.py:217
  54.5 9.1 %all-to-all-done = bf16[16,90,2,128]{3,2,1,0:T(2,128)(2,1)} async-done(((bf16[16,90,2,128]{3,2,1,0:T(2,128)(2,1)}), bf16[16,90,2,128]{3,2,1,0:T(2,128)(2,1)}, u32[]{:S(2)}, u32[]{:S(2)}) %all-to-all-start) | async-done | bytes 737312 | tf_op jit(solution)/shard_map/all_to_all | solution.py:415
  63.5 7.0 %lift.1 = bf16[4608,128]{1,0:T(8,128)(2,1)S(1)} custom-call(bf16[2880,128]{1,0:T(8,128)(2,1)} %bitcast.2.cols, bf16[1104,1440]{1,0:T(8,128)(2,1)} %fusion.6.matrices, bf16[1440,768]{1,0:T(8,128)(2,1)} %multiply_convert_fusion.1.rest_0_.inverse, bf16[3,384,768]{2,1,0:T(8,128)(2,1)S(1)} %get-tuple-element.11.rest_1_.weighted, ...), custom_call_target="tpu_custom_call" | custom-call | tf_op jit(solution)/shard_map/lift/pallas_call | solution.py:128
  70.5 0.0 copy-start.3
  70.5 40.4 %all_to_all.30 = bf16[256,9,2,128]{3,2,1,0:T(2,128)(2,1)S(1)} all-to-all(bf16[256,9,2,128]{3,2,1,0:T(2,128)(2,1)S(1)} %bitcast.16), channel_id=1, replica_groups=mesh['lat'=16,'lon'=16] {'lat','lon'}, dimensions={0} | all-to-all | bytes 2359296 | tf_op jit(solution)/shard_map/all_to_all | solution.py:415
  111.0 0.8 analyse.1
  111.7 27.1 %all_to_all.31.pieces = bf16[16,72,256]{2,1,0:T(8,128)(2,1)S(1)} all-to-all(bf16[16,72,256]{2,1,0:T(8,128)(2,1)S(1)} %analyse.1), channel_id=1, replica_groups=mesh['lat'=16,'lon'=16] {'lon'}, dimensions={0} | all-to-all | bytes 1179648 | tf_op jit(solution)/shard_map/all_to_all | solution.py:420
  138.8 0.8 mix.1
  139.6 0.0 copy-start
  139.6 23.0 %all_to_all.32.pieces = bf16[16,72,256]{2,1,0:T(8,128)(2,1)S(1)} all-to-all(bf16[16,72,256]{2,1,0:T(8,128)(2,1)S(1)} %mix.1), channel_id=1, replica_groups=mesh['lat'=16,'lon'=16] {'lon'}, dimensions={0} | all-to-all | bytes 1179648 | tf_op jit(solution)/shard_map/all_to_all | solution.py:420
  162.6 0.8 synthesise.1
  163.5 38.0 %all_to_all.33 = bf16[256,9,2,128]{3,2,1,0:T(2,128)(2,1)S(1)} all-to-all(bf16[256,9,2,128]{3,2,1,0:T(2,128)(2,1)S(1)} %bitcast.15), channel_id=1, replica_groups=mesh['lat'=16,'lon'=16] {'lat','lon'}, dimensions={0} | all-to-all | bytes 2359296 | tf_op jit(solution)/shard_map/all_to_all | solution.py:415
  201.5 2.2 invert.1
  203.7 61.6 %all_to_all.34 = bf16[16,270,2,128]{3,2,1,0:T(2,128)(2,1)S(1)} all-to-all(bf16[16,270,2,128]{3,2,1,0:T(2,128)(2,1)S(1)} %bitcast.12), channel_id=1, replica_groups=mesh['lat'=16,'lon'=16] {'lon'}, dimensions={0} | all-to-all | bytes 4423680 | tf_op jit(solution)/shard_map/all_to_all | solution.py:415
  265.4 2.0 unpack.1
  (19 shorter events, 0.1 us)
Async XLA Ops:
  1.2 28.0 %collective-permute-start = (bf16[24,80,128]{2,1,0:T(8,128)(2,1)S(1)}, bf16[24,80,128]{2,1,0:T(8,128)(2,1)S(1)}, u32[]{:S(2)}, u32[]{:S(2)}) collective-permute-start(bf16[24,80,128]{2,1,0:T(8,128)(2,1)S(1)} %get-tuple-element.14), channel_id=1, source_target_pairs={{0,15},{1,2},{2,1},{3,4},{4,3},{5,6},{6,5},{7,8},{8,7},{9,10},{10,... | collective-permute-start | bytes 1474568 | tf_op jit(solution)/shard_map/ppermute | solution.py:429
  3.1 26.1 %collective-permute-start.1 = (bf16[24,80,128]{2,1,0:T(8,128)(2,1)S(1)}, bf16[24,80,128]{2,1,0:T(8,128)(2,1)S(1)}, u32[]{:S(2)}, u32[]{:S(2)}) collective-permute-start(bf16[24,80,128]{2,1,0:T(8,128)(2,1)S(1)} %get-tuple-element.13), channel_id=1, source_target_pairs={{0,1},{1,0},{2,3},{3,2},{4,5},{5,4},{6,7},{7,6},{8,9},{9,8},{10,11... | collective-permute-start | bytes 1474568 | tf_op jit(solution)/shard_map/ppermute | solution.py:434
  10.5 15.0 %copy-start.11 = (f32[8]{0:T(128)}, f32[8]{0:T(128)S(1)}, u32[]{:S(2)}) copy-start(f32[8]{0:T(128)S(1)} %add_convert_fusion) | copy-start | bytes 100
  20.1 9.1 %copy-start.2 = (bf16[48,80,128]{2,1,0:T(8,128)(2,1)S(1)}, bf16[48,80,128]{2,1,0:T(8,128)(2,1)}, u32[]{:S(2)}) copy-start(bf16[48,80,128]{2,1,0:T(8,128)(2,1)} %own.1) | copy-start | bytes 2949124
  29.2 2.3 copy-start.1
  31.5 8.1 %copy-start.6 = (bf16[256,256]{1,0:T(8,128)(2,1)S(1)}, bf16[256,256]{1,0:T(8,128)(2,1)}, u32[]{:S(2)}) copy-start(bf16[256,256]{1,0:T(8,128)(2,1)} %param.10) | copy-start | bytes 393220
  31.5 8.1 %copy-start.7 = (bf16[80,256]{1,0:T(8,128)(2,1)S(1)}, bf16[80,256]{1,0:T(8,128)(2,1)}, u32[]{:S(2)}) copy-start(bf16[80,256]{1,0:T(8,128)(2,1)} %param.9) | copy-start | bytes 122884
  31.5 8.1 %copy-start.8 = (f32[1104]{0:T(1024)S(1)}, f32[1104]{0:T(1024)}, u32[]{:S(2)}) copy-start(f32[1104]{0:T(1024)} %fusion.15) | copy-start | bytes 13252
  31.5 8.1 %copy-start.9 = (f32[1104]{0:T(1024)S(1)}, f32[1104]{0:T(1024)}, u32[]{:S(2)}) copy-start(f32[1104]{0:T(1024)} %fusion.17) | copy-start | bytes 13252
  35.2 28.4 %all-to-all-start = ((bf16[16,90,2,128]{3,2,1,0:T(2,128)(2,1)}), bf16[16,90,2,128]{3,2,1,0:T(2,128)(2,1)}, u32[]{:S(2)}, u32[]{:S(2)}) async-start(bf16[16,90,2,128]{3,2,1,0:T(2,128)(2,1)} %bitcast.1), calls=%async_computation | async-start | bytes 1474560 | tf_op jit(solution)/shard_map/all_to_all | solution.py:415
  39.6 11.7 %copy-start.12 = (f32[8]{0:T(128)S(1)}, f32[8]{0:T(128)}, u32[]{:S(2)}) copy-start(f32[8]{0:T(128)} %compare_select_fusion.3) | copy-start | bytes 100
  39.6 11.7 %copy-start.10 = (f32[768]{0:T(1024)S(1)}, f32[768]{0:T(1024)}, u32[]{:S(2)}) copy-start(f32[768]{0:T(1024)} %fusion.48) | copy-start | bytes 9220
  39.6 11.7 %copy-start.4 = (f32[8,768]{1,0:T(8,128)S(1)}, f32[8,768]{1,0:T(8,128)}, u32[]{:S(2)}) copy-start(f32[8,768]{1,0:T(8,128)} %get-tuple-element.15.restore) | copy-start | bytes 73732
  39.6 11.7 %copy-start.5 = (f32[8,768]{1,0:T(8,128)S(1)}, f32[8,768]{1,0:T(8,128)}, u32[]{:S(2)}) copy-start(f32[8,768]{1,0:T(8,128)} %get-tuple-element.16.initial) | copy-start | bytes 73732
  70.5 68.3 %copy-start.3 = (bf16[24,256,256]{2,1,0:T(8,128)(2,1)S(1)}, bf16[24,256,256]{2,1,0:T(8,128)(2,1)}, u32[]{:S(2)}) copy-start(bf16[24,256,256]{2,1,0:T(8,128)(2,1)} %spectral.1) | copy-start | bytes 9437188
  139.6 61.9 %copy-start = (bf16[1440,768]{1,0:T(8,128)(2,1)S(1)}, bf16[1440,768]{1,0:T(8,128)(2,1)}, u32[]{:S(2)}) copy-start(bf16[1440,768]{1,0:T(8,128)(2,1)} %multiply_convert_fusion.1.rest_0_.inverse) | copy-start | bytes 6635524

commit v6 on v4

--- a/solution.py
+++ b/solution.py
@@ -43,7 +43,7 @@
     return lax.dot_general(a, b, (dims, ((), ())), preferred_element_type=jnp.float32)
 
 
-REMAP_STEPS = 4
+REMAP_STEPS = 2
 STEP_GROUPS = N_LON // REMAP_STEPS
 GROUP_ROWS = 2 * LON_DEV
 
@@ -114,30 +114,23 @@
     )(offsets, across, own, beside, weight)
 
 
-def lift_kernel(cols, matrices, *rest):
-    out, packed, scratch, lifted, first, second, table, sems = rest[-8:]
+def lift_kernel(source, matrices, forward, *rest):
+    out, cols, packed, scratch, lifted, first, table, sems = rest[-8:]
+    fetch = pltpu.make_async_copy(source, cols, sems.at[0])
+    fetch.start()
+    copy = pltpu.make_async_copy(forward, table, sems.at[1])
+    copy.start()
     first[...] = jnp.zeros_like(first)
-    count = ITEMS * N_DEV
-    places = [first.at[row, row * CIN : (row + 1) * CIN] for row in range(ROWS)]
-    copies = [
-        pltpu.make_async_copy(matrices.at[count + C : count + C + CIN, :C], place, sems.at[row])
-        for row, place in enumerate(places)
-    ]
-    copies.append(
-        pltpu.make_async_copy(matrices.at[count : count + C, :C], second, sems.at[ROWS])
-    )
-    copies.append(pltpu.make_async_copy(matrices.at[:count], table, sems.at[ROWS + 1]))
-    for copy in copies:
-        copy.start()
+    for row in range(ROWS):
+        first[row, row * CIN : (row + 1) * CIN] = matrices[C:]
+    fetch.wait()
     packed[...] = cols[...].astype(jnp.float32)
     halves = [packed[pl.ds(h, NLON, stride=2), :] for h in range(2)]
     values = jnp.concatenate(halves, axis=1).astype(jnp.bfloat16)
-    for copy in copies[:-1]:
-        copy.wait()
     for row in range(ROWS):
         hidden = jax.nn.gelu(dot(values, first[row])).astype(jnp.bfloat16)
-        lifted[:, row * C : (row + 1) * C] = dot(hidden, second[...]).astype(jnp.bfloat16)
-    copies[-1].wait()
+        lifted[:, row * C : (row + 1) * C] = dot(hidden, matrices[:C]).astype(jnp.bfloat16)
+    copy.wait()
     for item in range(ITEMS):
         spectra = dot(table[item * N_DEV : (item + 1) * N_DEV], lifted[...])
         for piece in range(2 * ROWS):
@@ -147,24 +140,25 @@
     out[...] = scratch[...].astype(jnp.bfloat16)
 
 
-def lift(cols, matrices, tables):
+def lift(cols, matrices, forward, tables):
     return pl.pallas_call(
         lift_kernel,
         out_shape=jax.ShapeDtypeStruct((N_DEV * PIECES, 128), jnp.bfloat16),
-        in_specs=[whole()] + [pl.BlockSpec(memory_space=pl.ANY)] * (1 + len(tables)),
+        in_specs=[pl.BlockSpec(memory_space=pl.ANY), whole()]
+        + [pl.BlockSpec(memory_space=pl.ANY)] * (1 + len(tables)),
         out_specs=whole(),
         scratch_shapes=[
+            pltpu.VMEM((2 * NLON, 128), jnp.bfloat16),
             pltpu.VMEM((2 * NLON, 128), jnp.float32),
             pltpu.VMEM((N_DEV * PIECES, 128), jnp.float32),
             pltpu.VMEM((NLON, ROWS * C), jnp.bfloat16),
             pltpu.VMEM((ROWS, C, C), jnp.bfloat16),
-            pltpu.VMEM((C, C), jnp.bfloat16),
             pltpu.VMEM((ITEMS * N_DEV, NLON), jnp.bfloat16),
-            pltpu.SemaphoreType.DMA((ROWS + 2,)),
+            pltpu.SemaphoreType.DMA((2,)),
         ],
         compiler_params=params(48),
         name="lift",
-    )(cols, matrices, *tables)
+    )(cols, matrices, forward, *tables)
 
 
 def legendre_kernel(rise, fall, start, initial, restore, factor, cosine, quad, weighted, plain, table):
@@ -283,46 +277,28 @@
     )(pieces, weighted)
 
 
-MIX_STEPS = 4
-MIX_DEG = DEG // MIX_STEPS
-
-
 def mix_kernel(pieces, spectral, out, source, result):
-    step = pl.program_id(0)
     count = N_LON * ITEMS
-
-    @pl.when(step == 0)
-    def _():
-        values = pieces[...].astype(jnp.float32).reshape(count * DEG, C)
-        source[0] = values[:, :128]
-        source[1] = values[:, 128:]
-
-    for index in range(MIX_DEG):
-        degree = step * MIX_DEG + index
+    values = pieces[...].astype(jnp.float32).reshape(count * DEG, C)
+    source[0] = values[:, :128]
+    source[1] = values[:, 128:]
+    for degree in range(DEG):
         halves = [source[h, pl.ds(degree, count, stride=DEG), :] for h in range(2)]
         values = jnp.concatenate(halves, axis=1).astype(jnp.bfloat16)
-        mixed = dot(values, spectral[index])
+        mixed = dot(values, spectral[degree])
         for h in range(2):
             result[h, pl.ds(degree, count, stride=DEG), :] = mixed[:, h * 128 : (h + 1) * 128]
-
-    @pl.when(step == MIX_STEPS - 1)
-    def _():
-        for h in range(2):
-            values = result[h].reshape(N_LON, ITEMS * DEG, 128)
-            out[:, :, h * 128 : (h + 1) * 128] = values.astype(jnp.bfloat16)
+    for h in range(2):
+        values = result[h].reshape(N_LON, ITEMS * DEG, 128)
+        out[:, :, h * 128 : (h + 1) * 128] = values.astype(jnp.bfloat16)
 
 
 def mix(pieces, spectral):
-    shape = (N_LON, ITEMS * DEG, C)
     return pl.pallas_call(
         mix_kernel,
-        out_shape=jax.ShapeDtypeStruct(shape, jnp.bfloat16),
-        grid=(MIX_STEPS,),
-        in_specs=[
-            pl.BlockSpec(shape, lambda g: (0, 0, 0)),
-            pl.BlockSpec((MIX_DEG, C, C), lambda g: (g, 0, 0)),
-        ],
-        out_specs=pl.BlockSpec(shape, lambda g: (0, 0, 0)),
+        out_shape=jax.ShapeDtypeStruct((N_LON, ITEMS * DEG, C), jnp.bfloat16),
+        in_specs=[whole()] * 2,
+        out_specs=whole(),
         scratch_shapes=[pltpu.VMEM((2, N_LON * ITEMS * DEG, 128), jnp.float32)] * 2,
         compiler_params=params(40),
         name="mix",
@@ -417,9 +393,8 @@
     )(pieces)
 
 
-def fourier(item_axis, extra=0):
-    items = ITEMS * N_DEV + extra
-    shape = (items, 1) if item_axis == 0 else (1, items)
+def fourier(item_axis):
+    shape = (ITEMS * N_DEV, 1) if item_axis == 0 else (1, ITEMS * N_DEV)
     index = lax.broadcasted_iota(jnp.int32, shape, item_axis)
     device = index % N_DEV
     order = (index // N_DEV) * (L // ITEMS) + device // 2
@@ -437,14 +412,6 @@
     for term in (1.0 / 362880.0, -1.0 / 5040.0, 1.0 / 120.0, -1.0 / 6.0, 1.0):
         total = total * square + term
     return (total * angle).astype(jnp.bfloat16)
-
-
-def lift_matrices(lift_in, lift_out):
-    table = fourier(0, C + CIN)
-    rows, wide = table.shape[0], (0, NLON - C)
-    below = jnp.pad(lift_out, ((ITEMS * N_DEV, CIN), wide)) + jnp.pad(lift_in, ((rows - CIN, 0), wide))
-    index = lax.broadcasted_iota(jnp.int32, (rows, 1), 0)
-    return jnp.where(index < ITEMS * N_DEV, table, below)
 
 
 def exchange(values, axes, count):
@@ -477,12 +444,13 @@
     places = jnp.concatenate(
         [offsets.reshape(LAT_DEV * K), (odd * (RIM + SRC_DEV)).reshape(1).astype(jnp.int32)]
     )
-    matrices = lift_matrices(lift_in, lift_out)
+    forward = fourier(0)
+    matrices = jnp.concatenate([lift_out, lift_in], axis=0)
     inverse = fourier(1)
     weighted, plain = legendre(chip)
     columns = remap(places, across, cube_cells, beside, block_weight)
     columns = exchange(columns, "lon", N_LON)
-    spectra = lift(columns, matrices, (inverse, weighted, plain))
+    spectra = lift(columns, matrices, forward, (inverse, weighted, plain))
     spectra = exchange(spectra, ("lat", "lon"), N_DEV)
     analysis = regroup(analyse(spectra, weighted))
     mixed = regroup(mix(analysis, spectral))

time: 263 us -> 262 us (level)
    select_n x1 -> x0, other arithmetic: 7.57 us -> none  [lift_matrices(): return jnp.where(index < ITEMS * N_DEV, table, below)]
    convert_element_type x1 -> x2, other arithmetic: 4.71 us -> 9.59 us  [fourier(): return (total * angle).astype(jnp.bfloat16)]
  transfers between devices with their start and end apart: 3 -> 3, of which waited for: 1 -> 1; matrix products, arithmetic and copies ran while one was open for 9% -> 8% of each run, Pallas kernels for 1% -> 1%
where the time goes in v6:
time: 262 us; the launch traced here: 261 us
  blocking collectives  191 us (73%)
  Pallas kernels  18.4 us (7%)
  other arithmetic  15.8 us (6%)
  starting transfers between devices  15.4 us (6%)
  waiting for transfers between devices  12.4 us (5%)
  local copies, waits for them, and re-layouts  8.33 us (3%)
    all_to_all x3, blocking collectives, exchange(): pairs = lax.all_to_all(pairs, axes, split_axis=0, concat_axis=0, tiled=True)  141 us
    all_to_all x2, blocking collectives, regroup(): lax.all_to_all(values, 'lon', split_axis=0, concat_axis=0, tiled=True)  50.1 us
    all_to_all x1, waiting for transfers between devices, exchange(): pairs = lax.all_to_all(pairs, axes, split_axis=0, concat_axis=0, tiled=True)  12.4 us
    convert_element_type x2, other arithmetic, fourier(): return (total * angle).astype(jnp.bfloat16)  9.59 us
    ppermute x1, starting transfers between devices, shards(): lax.ppermute(lax.dynamic_slice_in_dim(cube_cells, (1 - odd) * far, RIM, 0...  6.83 us
    all_to_all x1, starting transfers between devices, exchange(): pairs = lax.all_to_all(pairs, axes, split_axis=0, concat_axis=0, tiled=True)  6.73 us
  transfers between devices with their start and end apart: 3, of which 1 were waited for; matrix products, arithmetic and copies ran while one was open for 8% of the time, Pallas kernels for 1%

profile of v6, /device:TPU:33, one launch (start us, length us, event | category | flops | bytes accessed | tf_op | source)
XLA Modules:
  0.0 261.3 jit_solution(2390248115389947431)
XLA Ops:
  0.0 1.2 constant_dynamic-slice_fusion
  1.2 1.9 collective-permute-start
  3.1 6.8 %collective-permute-start.1 = (bf16[24,80,128]{2,1,0:T(8,128)(2,1)S(1)}, bf16[24,80,128]{2,1,0:T(8,128)(2,1)S(1)}, u32[]{:S(2)}, u32[]{:S(2)}) collective-permute-start(bf16[24,80,128]{2,1,0:T(8,128)(2,1)S(1)} %get-tuple-element.9), channel_id=1, source_target_pairs={{0,1},{1,0},{2,3},{3,2},{4,5},{5,4},{6,7},{7,6},{8,9},{9,8},{10,11... | collective-permute-start | bytes 1474568 | tf_op jit(solution)/shard_map/ppermute | solution.py:438
  10.0 0.0 copy-start.10
  10.1 0.7 add_remainder_fusion
  10.8 0.1 copy.10
  10.9 0.1 rem.194
  11.0 0.6 and_select_fusion
  11.5 0.7 compare_select_fusion
  12.2 4.7 %multiply_convert_fusion.1.rest_0_.inverse = bf16[1440,768]{1,0:T(8,128)(2,1)} fusion(f32[768]{0:T(1024)S(1)} %fusion.15, f32[768]{0:T(1024)S(1)} %fusion.13, f32[1440]{0:T(1024)S(1)} %iota_convert_fusion), kind=kLoop, calls=%fused_computation.7 | loop fusion | flops 24330240 | bytes 2223744 | tf_op jit(solution)/shard_map/convert_element_type | solution.py:414
  16.9 0.1 divide_sqrt_fusion
  17.0 0.7 compare_select_fusion.3
  17.6 0.1 copy.12
  17.8 0.0 copy-done.10
  17.8 0.1 copy.13
  17.9 0.0 copy-start.1
  17.9 0.9 copy.14
  18.8 0.0 copy-start.9
  18.8 3.3 %copy.11.weight = bf16[45,1,4,90,128]{4,3,2,1,0:T(8,128)(2,1)S(1)} copy(bf16[45,1,4,90,128]{4,2,3,1,0:T(4,128)(2,1)} %param.8) | data formatting | bytes 8294400 | tf_op args[2]
  22.1 0.0 copy-done.9
  22.1 0.1 pad_add_fusion.offsets
  22.2 0.6 fusion.32
  22.9 0.6 fusion.30
  23.5 0.6 broadcast_multiply_fusion
  24.2 0.0 collective-permute-done.across
  24.2 0.0 copy-start.8
  24.2 0.0 collective-permute-done.1.beside
  24.2 0.0 copy-done.1
  24.2 3.4 %remap.1 = bf16[2880,128]{1,0:T(8,128)(2,1)} custom-call(s32[181]{0:T(256)S(1)} %pad_add_fusion.offsets, bf16[24,80,128]{2,1,0:T(8,128)(2,1)S(1)} %collective-permute-done.across, bf16[48,80,128]{2,1,0:T(8,128)(2,1)S(1)} %copy-done.1, bf16[24,80,128]{2,1,0:T(8,128)(2,1)S(1)} %collective-permute-done.1.beside, bf16[45,1,4,90,128]{4,3,2,1,0:T(8,128)(2,1)S(1)} %copy.11.weight), custom_call_target="tpu_custom_call" | custom-call | tf_op jit(solution)/shard_map/remap/pallas_call | solution.py:92
  27.6 0.0 copy-start.11
  27.6 6.7 %all-to-all-start = ((bf16[16,90,2,128]{3,2,1,0:T(2,128)(2,1)}), bf16[16,90,2,128]{3,2,1,0:T(2,128)(2,1)}, u32[]{:S(2)}, u32[]{:S(2)}) async-start(bf16[16,90,2,128]{3,2,1,0:T(2,128)(2,1)} %bitcast.1), calls=%async_computation | async-start | bytes 1474560 | tf_op jit(solution)/shard_map/all_to_all | solution.py:419
  34.3 0.0 copy-done.8
  34.3 0.8 exponential_select_fusion
  35.1 0.5 broadcast_in_dim.30.rise
  35.6 0.0 copy-start.4
  35.6 0.0 copy-start.5
  35.6 0.5 broadcast_in_dim.31.fall
  36.1 0.5 broadcast_in_dim.32.start
  36.5 0.0 copy-done.11
  36.5 0.1 broadcast_in_dim.34.factor
  36.6 0.0 copy-done.7
  36.6 0.0 copy-done.6
  36.6 3.1 %legendre.1 = (bf16[3,384,768]{2,1,0:T(8,128)(2,1)S(1)}, bf16[3,768,384]{2,1,0:T(8,128)(2,1)S(1)}) custom-call(f32[384,8,128]{2,1,0:T(8,128)S(1)} %broadcast_in_dim.30.rise, f32[384,8,128]{2,1,0:T(8,128)S(1)} %broadcast_in_dim.31.fall, f32[384,8,128]{2,1,0:T(8,128)S(1)} %broadcast_in_dim.32.start, f32[8,768]{1,0:T(8,128)S(1)} %get-tuple-element.12.initial, ...), custom_call_target="tpu_custom_call" | custom-call | tf_op jit(solution)/shard_map/legendre/pallas_call | solution.py:232
  39.8 0.0 copy-done.4
  39.8 0.0 copy-done.5
  39.8 0.7 pad_maximum_fusion.matrices
  40.5 4.9 %multiply_convert_fusion.forward = bf16[768,1440]{1,0:T(8,128)(2,1)} fusion(f32[768]{0:T(1024)S(1)} %fusion.15, f32[768]{0:T(1024)S(1)} %fusion.13, f32[1440]{0:T(1024)S(1)} %iota_convert_fusion), kind=kLoop, calls=%fused_computation | loop fusion | flops 24330240 | bytes 2223744 | tf_op jit(solution)/shard_map/convert_element_type | solution.py:414
  45.4 12.4 %all-to-all-done = bf16[16,90,2,128]{3,2,1,0:T(2,128)(2,1)} async-done(((bf16[16,90,2,128]{3,2,1,0:T(2,128)(2,1)}), bf16[16,90,2,128]{3,2,1,0:T(2,128)(2,1)}, u32[]{:S(2)}, u32[]{:S(2)}) %all-to-all-start) | async-done | bytes 737312 | tf_op jit(solution)/shard_map/all_to_all | solution.py:419
  57.7 0.9 copy-done.3
  58.7 5.2 %lift.1 = bf16[4608,128]{1,0:T(8,128)(2,1)S(1)} custom-call(bf16[2880,128]{1,0:T(8,128)(2,1)} %bitcast.2.source, bf16[336,256]{1,0:T(8,128)(2,1)S(1)} %copy-done.3, bf16[768,1440]{1,0:T(8,128)(2,1)} %multiply_convert_fusion.forward, bf16[1440,768]{1,0:T(8,128)(2,1)} %multiply_convert_fusion.1.rest_0_.inverse, ...), custom_call_target="tpu_custom_call" | custom-call | tf_op jit(solution)/shard_map/lift/pallas_call | solution.py:144
  63.9 0.0 copy-start.2
  63.9 40.3 %all_to_all.30 = bf16[256,9,2,128]{3,2,1,0:T(2,128)(2,1)S(1)} all-to-all(bf16[256,9,2,128]{3,2,1,0:T(2,128)(2,1)S(1)} %bitcast.15), channel_id=1, replica_groups=mesh['lat'=16,'lon'=16] {'lat','lon'}, dimensions={0} | all-to-all | bytes 2359296 | tf_op jit(solution)/shard_map/all_to_all | solution.py:419
  104.2 0.7 analyse.1
  105.0 27.1 %all_to_all.31.pieces = bf16[16,72,256]{2,1,0:T(8,128)(2,1)S(1)} all-to-all(bf16[16,72,256]{2,1,0:T(8,128)(2,1)S(1)} %analyse.1), channel_id=1, replica_groups=mesh['lat'=16,'lon'=16] {'lon'}, dimensions={0} | all-to-all | bytes 1179648 | tf_op jit(solution)/shard_map/all_to_all | solution.py:424
  132.1 0.0 copy-done.2
  132.1 0.8 mix.1
  132.8 0.0 copy-start
  132.9 23.0 %all_to_all.32.pieces = bf16[16,72,256]{2,1,0:T(8,128)(2,1)S(1)} all-to-all(bf16[16,72,256]{2,1,0:T(8,128)(2,1)S(1)} %mix.1), channel_id=1, replica_groups=mesh['lat'=16,'lon'=16] {'lon'}, dimensions={0} | all-to-all | bytes 1179648 | tf_op jit(solution)/shard_map/all_to_all | solution.py:424
  155.9 0.8 synthesise.1
  156.7 38.7 %all_to_all.33 = bf16[256,9,2,128]{3,2,1,0:T(2,128)(2,1)S(1)} all-to-all(bf16[256,9,2,128]{3,2,1,0:T(2,128)(2,1)S(1)} %bitcast.14), channel_id=1, replica_groups=mesh['lat'=16,'lon'=16] {'lat','lon'}, dimensions={0} | all-to-all | bytes 2359296 | tf_op jit(solution)/shard_map/all_to_all | solution.py:419
  195.4 0.0 copy-done
  195.4 2.2 invert.1
  197.7 61.6 %all_to_all.34 = bf16[16,270,2,128]{3,2,1,0:T(2,128)(2,1)S(1)} all-to-all(bf16[16,270,2,128]{3,2,1,0:T(2,128)(2,1)S(1)} %bitcast.11), channel_id=1, replica_groups=mesh['lat'=16,'lon'=16] {'lon'}, dimensions={0} | all-to-all | bytes 4423680 | tf_op jit(solution)/shard_map/all_to_all | solution.py:419
  259.3 2.0 unpack.1
  (14 shorter events, 0.1 us)
Async XLA Ops:
  1.2 22.9 %collective-permute-start = (bf16[24,80,128]{2,1,0:T(8,128)(2,1)S(1)}, bf16[24,80,128]{2,1,0:T(8,128)(2,1)S(1)}, u32[]{:S(2)}, u32[]{:S(2)}) collective-permute-start(bf16[24,80,128]{2,1,0:T(8,128)(2,1)S(1)} %get-tuple-element.10), channel_id=1, source_target_pairs={{0,15},{1,2},{2,1},{3,4},{4,3},{5,6},{6,5},{7,8},{8,7},{9,10},{10,... | collective-permute-start | bytes 1474568 | tf_op jit(solution)/shard_map/ppermute | solution.py:433
  3.1 21.1 %collective-permute-start.1 = (bf16[24,80,128]{2,1,0:T(8,128)(2,1)S(1)}, bf16[24,80,128]{2,1,0:T(8,128)(2,1)S(1)}, u32[]{:S(2)}, u32[]{:S(2)}) collective-permute-start(bf16[24,80,128]{2,1,0:T(8,128)(2,1)S(1)} %get-tuple-element.9), channel_id=1, source_target_pairs={{0,1},{1,0},{2,3},{3,2},{4,5},{5,4},{6,7},{7,6},{8,9},{9,8},{10,11... | collective-permute-start | bytes 1474568 | tf_op jit(solution)/shard_map/ppermute | solution.py:438
  10.0 7.8 %copy-start.10 = (f32[8]{0:T(128)}, f32[8]{0:T(128)S(1)}, u32[]{:S(2)}) copy-start(f32[8]{0:T(128)S(1)} %add_convert_fusion) | copy-start | bytes 100
  17.9 6.3 %copy-start.1 = (bf16[48,80,128]{2,1,0:T(8,128)(2,1)S(1)}, bf16[48,80,128]{2,1,0:T(8,128)(2,1)}, u32[]{:S(2)}) copy-start(bf16[48,80,128]{2,1,0:T(8,128)(2,1)} %own.1) | copy-start | bytes 2949124
  18.8 3.3 %copy-start.9 = (s32[180]{0:T(256)S(1)}, s32[180]{0:T(256)}, u32[]{:S(2)}) copy-start(s32[180]{0:T(256)} %and_select_fusion) | copy-start | bytes 2164
  24.2 10.2 %copy-start.8 = (f32[768]{0:T(1024)S(1)}, f32[768]{0:T(1024)}, u32[]{:S(2)}) copy-start(f32[768]{0:T(1024)} %fusion.32) | copy-start | bytes 9220
  27.6 9.0 %copy-start.11 = (f32[8]{0:T(128)S(1)}, f32[8]{0:T(128)}, u32[]{:S(2)}) copy-start(f32[8]{0:T(128)} %get-tuple-element.15) | copy-start | bytes 100
  27.6 9.0 %copy-start.7 = (f32[768]{0:T(1024)S(1)}, f32[768]{0:T(1024)}, u32[]{:S(2)}) copy-start(f32[768]{0:T(1024)} %fusion.30) | copy-start | bytes 9220
  27.6 9.0 %copy-start.6 = (f32[768]{0:T(1024)S(1)}, f32[768]{0:T(1024)}, u32[]{:S(2)}) copy-start(f32[768]{0:T(1024)} %broadcast_multiply_fusion) | copy-start | bytes 9220
  27.6 30.1 %all-to-all-start = ((bf16[16,90,2,128]{3,2,1,0:T(2,128)(2,1)}), bf16[16,90,2,128]{3,2,1,0:T(2,128)(2,1)}, u32[]{:S(2)}, u32[]{:S(2)}) async-start(bf16[16,90,2,128]{3,2,1,0:T(2,128)(2,1)} %bitcast.1), calls=%async_computation | async-start | bytes 1474560 | tf_op jit(solution)/shard_map/all_to_all | solution.py:419
  35.6 4.2 %copy-start.4 = (bf16[256,256]{1,0:T(8,128)(2,1)S(1)}, bf16[256,256]{1,0:T(8,128)(2,1)}, u32[]{:S(2)}) copy-start(bf16[256,256]{1,0:T(8,128)(2,1)} %param.10) | copy-start | bytes 393220
  35.6 4.2 %copy-start.5 = (bf16[80,256]{1,0:T(8,128)(2,1)S(1)}, bf16[80,256]{1,0:T(8,128)(2,1)}, u32[]{:S(2)}) copy-start(bf16[80,256]{1,0:T(8,128)(2,1)} %param.9) | copy-start | bytes 122884
  57.7 0.9 copy-start.3
  63.9 68.2 %copy-start.2 = (bf16[24,256,256]{2,1,0:T(8,128)(2,1)S(1)}, bf16[24,256,256]{2,1,0:T(8,128)(2,1)}, u32[]{:S(2)}) copy-start(bf16[24,256,256]{2,1,0:T(8,128)(2,1)} %spectral.1) | copy-start | bytes 9437188
  132.8 62.6 %copy-start = (bf16[1440,768]{1,0:T(8,128)(2,1)S(1)}, bf16[1440,768]{1,0:T(8,128)(2,1)}, u32[]{:S(2)}) copy-start(bf16[1440,768]{1,0:T(8,128)(2,1)} %multiply_convert_fusion.1.rest_0_.inverse) | copy-start | bytes 6635524

commit v7 on v6

--- a/solution.py
+++ b/solution.py
@@ -367,27 +367,38 @@
     )(pieces, inverse)
 
 
-UNPACK_GROUPS = 4
-
-
-def unpack_kernel(pieces, out, packed):
-    packed[...] = pieces[...].astype(jnp.float32)
-    for group in range(UNPACK_GROUPS):
-        for row in range(ROWS):
-            place = group * LON_DEV * TILES + row * 2
+UNPACK_PARTS = 5
+
+
+def unpack_kernel(pieces, out, packed, rows, sems):
+    count = GROUPS // UNPACK_PARTS
+    size = count * LON_DEV * TILES
+    copies = []
+    for part in range(UNPACK_PARTS):
+        packed[...] = pieces[part * size : (part + 1) * size].astype(jnp.float32)
+        for row in range(count * ROWS):
+            place = row // ROWS * LON_DEV * TILES + row % ROWS * 2
             halves = [packed[pl.ds(place + h, LON_DEV, stride=TILES), :] for h in range(2)]
-            out[group * ROWS + row] = jnp.concatenate(halves, axis=1).astype(jnp.bfloat16)
+            rows[part, row] = jnp.concatenate(halves, axis=1).astype(jnp.bfloat16)
+        block = pl.ds(part * count * ROWS, count * ROWS)
+        copies.append(pltpu.make_async_copy(rows.at[part], out.at[block], sems.at[part]))
+        copies[-1].start()
+    for copy in copies:
+        copy.wait()
 
 
 def unpack(pieces):
-    block = UNPACK_GROUPS * LON_DEV * TILES
+    count = GROUPS // UNPACK_PARTS
     return pl.pallas_call(
         unpack_kernel,
         out_shape=jax.ShapeDtypeStruct((LAT_DEV, LON_DEV, C), jnp.bfloat16),
-        grid=(N_LON // UNPACK_GROUPS,),
-        in_specs=[pl.BlockSpec((block, 128), lambda g: (g, 0))],
-        out_specs=pl.BlockSpec((UNPACK_GROUPS * ROWS, LON_DEV, C), lambda g: (g, 0, 0)),
-        scratch_shapes=[pltpu.VMEM((block, 128), jnp.float32)],
+        in_specs=[whole()],
+        out_specs=pl.BlockSpec(memory_space=pl.ANY),
+        scratch_shapes=[
+            pltpu.VMEM((count * LON_DEV * TILES, 128), jnp.float32),
+            pltpu.VMEM((UNPACK_PARTS, count * ROWS, LON_DEV, C), jnp.bfloat16),
+            pltpu.SemaphoreType.DMA((UNPACK_PARTS,)),
+        ],
         compiler_params=params(32),
         name="unpack",
     )(pieces)

time: 262 us -> 261 us (level)
  no operation moved by 1% of the time
where the time goes in v7:
time: 261 us
  blocking collectives  191 us (73%)
  Pallas kernels  17.9 us (7%)
  other arithmetic  15.8 us (6%)
  starting transfers between devices  15.4 us (6%)
  waiting for transfers between devices  12.4 us (5%)
  local copies, waits for them, and re-layouts  8.33 us (3%)
    all_to_all x3, blocking collectives, exchange(): pairs = lax.all_to_all(pairs, axes, split_axis=0, concat_axis=0, tiled=True)  141 us
    all_to_all x2, blocking collectives, regroup(): lax.all_to_all(values, 'lon', split_axis=0, concat_axis=0, tiled=True)  50.1 us
    all_to_all x1, waiting for transfers between devices, exchange(): pairs = lax.all_to_all(pairs, axes, split_axis=0, concat_axis=0, tiled=True)  12.4 us
    convert_element_type x2, other arithmetic, fourier(): return (total * angle).astype(jnp.bfloat16)  9.59 us
    ppermute x1, starting transfers between devices, shards(): lax.ppermute(lax.dynamic_slice_in_dim(cube_cells, (1 - odd) * far, RIM, 0...  6.83 us
    all_to_all x1, starting transfers between devices, exchange(): pairs = lax.all_to_all(pairs, axes, split_axis=0, concat_axis=0, tiled=True)  6.71 us
    pallas_call x1, Pallas kernels, lift(): pl.pallas_call(lift_kernel, out_shape=jax.ShapeDtypeStruct((N_DEV * PIECE...  5.23 us
  transfers between devices with their start and end apart: 3, of which 1 were waited for; matrix products, arithmetic and copies ran while one was open for 8% of the time, Pallas kernels for 1%

profile of v7, /device:TPU:33, one launch (start us, length us, event | category | flops | bytes accessed | tf_op | source)
XLA Modules:
  0.0 261.0 jit_solution(16171755323071831812)
XLA Ops:
  0.0 1.2 constant_dynamic-slice_fusion
  1.2 1.9 collective-permute-start
  3.1 6.8 %collective-permute-start.1 = (bf16[24,80,128]{2,1,0:T(8,128)(2,1)S(1)}, bf16[24,80,128]{2,1,0:T(8,128)(2,1)S(1)}, u32[]{:S(2)}, u32[]{:S(2)}) collective-permute-start(bf16[24,80,128]{2,1,0:T(8,128)(2,1)S(1)} %get-tuple-element.9), channel_id=1, source_target_pairs={{0,1},{1,0},{2,3},{3,2},{4,5},{5,4},{6,7},{7,6},{8,9},{9,8},{10,11... | collective-permute-start | bytes 1474568 | tf_op jit(solution)/shard_map/ppermute | solution.py:449
  10.0 0.0 copy-start.10
  10.1 0.7 add_remainder_fusion
  10.8 0.1 copy.10
  10.9 0.1 rem.194
  11.0 0.6 and_select_fusion
  11.5 0.7 compare_select_fusion
  12.2 4.7 %multiply_convert_fusion.1.rest_0_.inverse = bf16[1440,768]{1,0:T(8,128)(2,1)} fusion(f32[768]{0:T(1024)S(1)} %fusion.15, f32[768]{0:T(1024)S(1)} %fusion.13, f32[1440]{0:T(1024)S(1)} %iota_convert_fusion), kind=kLoop, calls=%fused_computation.7 | loop fusion | flops 24330240 | bytes 2223744 | tf_op jit(solution)/shard_map/convert_element_type | solution.py:425
  16.9 0.1 divide_sqrt_fusion
  17.0 0.7 compare_select_fusion.3
  17.6 0.1 copy.12
  17.8 0.0 copy-done.10
  17.8 0.1 copy.13
  17.9 0.0 copy-start.1
  17.9 0.9 copy.14
  18.8 0.0 copy-start.9
  18.8 3.3 %copy.11.weight = bf16[45,1,4,90,128]{4,3,2,1,0:T(8,128)(2,1)S(1)} copy(bf16[45,1,4,90,128]{4,2,3,1,0:T(4,128)(2,1)} %param.8) | data formatting | bytes 8294400 | tf_op args[2]
  22.1 0.0 copy-done.9
  22.1 0.1 pad_add_fusion.offsets
  22.2 0.6 fusion.32
  22.9 0.6 fusion.30
  23.5 0.6 broadcast_multiply_fusion
  24.2 0.0 collective-permute-done.across
  24.2 0.0 copy-start.8
  24.2 0.0 collective-permute-done.1.beside
  24.2 0.0 copy-done.1
  24.2 3.4 %remap.1 = bf16[2880,128]{1,0:T(8,128)(2,1)} custom-call(s32[181]{0:T(256)S(1)} %pad_add_fusion.offsets, bf16[24,80,128]{2,1,0:T(8,128)(2,1)S(1)} %collective-permute-done.across, bf16[48,80,128]{2,1,0:T(8,128)(2,1)S(1)} %copy-done.1, bf16[24,80,128]{2,1,0:T(8,128)(2,1)S(1)} %collective-permute-done.1.beside, bf16[45,1,4,90,128]{4,3,2,1,0:T(8,128)(2,1)S(1)} %copy.11.weight), custom_call_target="tpu_custom_call" | custom-call | tf_op jit(solution)/shard_map/remap/pallas_call | solution.py:92
  27.6 0.0 copy-start.11
  27.6 6.7 %all-to-all-start = ((bf16[16,90,2,128]{3,2,1,0:T(2,128)(2,1)}), bf16[16,90,2,128]{3,2,1,0:T(2,128)(2,1)}, u32[]{:S(2)}, u32[]{:S(2)}) async-start(bf16[16,90,2,128]{3,2,1,0:T(2,128)(2,1)} %bitcast.1), calls=%async_computation | async-start | bytes 1474560 | tf_op jit(solution)/shard_map/all_to_all | solution.py:430
  34.3 0.0 copy-done.8
  34.3 0.8 exponential_select_fusion
  35.1 0.5 broadcast_in_dim.30.rise
  35.6 0.0 copy-start.4
  35.6 0.0 copy-start.5
  35.6 0.5 broadcast_in_dim.31.fall
  36.1 0.5 broadcast_in_dim.32.start
  36.5 0.0 copy-done.11
  36.5 0.1 broadcast_in_dim.34.factor
  36.6 0.0 copy-done.7
  36.6 0.0 copy-done.6
  36.6 3.1 %legendre.1 = (bf16[3,384,768]{2,1,0:T(8,128)(2,1)S(1)}, bf16[3,768,384]{2,1,0:T(8,128)(2,1)S(1)}) custom-call(f32[384,8,128]{2,1,0:T(8,128)S(1)} %broadcast_in_dim.30.rise, f32[384,8,128]{2,1,0:T(8,128)S(1)} %broadcast_in_dim.31.fall, f32[384,8,128]{2,1,0:T(8,128)S(1)} %broadcast_in_dim.32.start, f32[8,768]{1,0:T(8,128)S(1)} %get-tuple-element.12.initial, ...), custom_call_target="tpu_custom_call" | custom-call | tf_op jit(solution)/shard_map/legendre/pallas_call | solution.py:232
  39.8 0.0 copy-done.4
  39.8 0.0 copy-done.5
  39.8 0.7 pad_maximum_fusion.matrices
  40.4 4.9 %multiply_convert_fusion.forward = bf16[768,1440]{1,0:T(8,128)(2,1)} fusion(f32[768]{0:T(1024)S(1)} %fusion.15, f32[768]{0:T(1024)S(1)} %fusion.13, f32[1440]{0:T(1024)S(1)} %iota_convert_fusion), kind=kLoop, calls=%fused_computation | loop fusion | flops 24330240 | bytes 2223744 | tf_op jit(solution)/shard_map/convert_element_type | solution.py:425
  45.4 12.4 %all-to-all-done = bf16[16,90,2,128]{3,2,1,0:T(2,128)(2,1)} async-done(((bf16[16,90,2,128]{3,2,1,0:T(2,128)(2,1)}), bf16[16,90,2,128]{3,2,1,0:T(2,128)(2,1)}, u32[]{:S(2)}, u32[]{:S(2)}) %all-to-all-start) | async-done | bytes 737312 | tf_op jit(solution)/shard_map/all_to_all | solution.py:430
  57.7 0.9 copy-done.3
  58.7 5.2 %lift.1 = bf16[4608,128]{1,0:T(8,128)(2,1)S(1)} custom-call(bf16[2880,128]{1,0:T(8,128)(2,1)} %bitcast.2.source, bf16[336,256]{1,0:T(8,128)(2,1)S(1)} %copy-done.3, bf16[768,1440]{1,0:T(8,128)(2,1)} %multiply_convert_fusion.forward, bf16[1440,768]{1,0:T(8,128)(2,1)} %multiply_convert_fusion.1.rest_0_.inverse, ...), custom_call_target="tpu_custom_call" | custom-call | tf_op jit(solution)/shard_map/lift/pallas_call | solution.py:144
  63.9 0.0 copy-start.2
  63.9 40.3 %all_to_all.30 = bf16[256,9,2,128]{3,2,1,0:T(2,128)(2,1)S(1)} all-to-all(bf16[256,9,2,128]{3,2,1,0:T(2,128)(2,1)S(1)} %bitcast.15), channel_id=1, replica_groups=mesh['lat'=16,'lon'=16] {'lat','lon'}, dimensions={0} | all-to-all | bytes 2359296 | tf_op jit(solution)/shard_map/all_to_all | solution.py:430
  104.2 0.7 analyse.1
  105.0 27.1 %all_to_all.31.pieces = bf16[16,72,256]{2,1,0:T(8,128)(2,1)S(1)} all-to-all(bf16[16,72,256]{2,1,0:T(8,128)(2,1)S(1)} %analyse.1), channel_id=1, replica_groups=mesh['lat'=16,'lon'=16] {'lon'}, dimensions={0} | all-to-all | bytes 1179648 | tf_op jit(solution)/shard_map/all_to_all | solution.py:435
  132.1 0.0 copy-done.2
  132.1 0.8 mix.1
  132.8 0.0 copy-start
  132.9 23.0 %all_to_all.32.pieces = bf16[16,72,256]{2,1,0:T(8,128)(2,1)S(1)} all-to-all(bf16[16,72,256]{2,1,0:T(8,128)(2,1)S(1)} %mix.1), channel_id=1, replica_groups=mesh['lat'=16,'lon'=16] {'lon'}, dimensions={0} | all-to-all | bytes 1179648 | tf_op jit(solution)/shard_map/all_to_all | solution.py:435
  155.9 0.8 synthesise.1
  156.7 38.7 %all_to_all.33 = bf16[256,9,2,128]{3,2,1,0:T(2,128)(2,1)S(1)} all-to-all(bf16[256,9,2,128]{3,2,1,0:T(2,128)(2,1)S(1)} %bitcast.14), channel_id=1, replica_groups=mesh['lat'=16,'lon'=16] {'lat','lon'}, dimensions={0} | all-to-all | bytes 2359296 | tf_op jit(solution)/shard_map/all_to_all | solution.py:430
  195.4 0.0 copy-done
  195.4 2.2 invert.1
  197.7 61.6 %all_to_all.34 = bf16[16,270,2,128]{3,2,1,0:T(2,128)(2,1)S(1)} all-to-all(bf16[16,270,2,128]{3,2,1,0:T(2,128)(2,1)S(1)} %bitcast.11), channel_id=1, replica_groups=mesh['lat'=16,'lon'=16] {'lon'}, dimensions={0} | all-to-all | bytes 4423680 | tf_op jit(solution)/shard_map/all_to_all | solution.py:430
  259.3 1.5 unpack.1
  (14 shorter events, 0.1 us)
Async XLA Ops:
  1.2 22.9 %collective-permute-start = (bf16[24,80,128]{2,1,0:T(8,128)(2,1)S(1)}, bf16[24,80,128]{2,1,0:T(8,128)(2,1)S(1)}, u32[]{:S(2)}, u32[]{:S(2)}) collective-permute-start(bf16[24,80,128]{2,1,0:T(8,128)(2,1)S(1)} %get-tuple-element.10), channel_id=1, source_target_pairs={{0,15},{1,2},{2,1},{3,4},{4,3},{5,6},{6,5},{7,8},{8,7},{9,10},{10,... | collective-permute-start | bytes 1474568 | tf_op jit(solution)/shard_map/ppermute | solution.py:444
  3.1 21.1 %collective-permute-start.1 = (bf16[24,80,128]{2,1,0:T(8,128)(2,1)S(1)}, bf16[24,80,128]{2,1,0:T(8,128)(2,1)S(1)}, u32[]{:S(2)}, u32[]{:S(2)}) collective-permute-start(bf16[24,80,128]{2,1,0:T(8,128)(2,1)S(1)} %get-tuple-element.9), channel_id=1, source_target_pairs={{0,1},{1,0},{2,3},{3,2},{4,5},{5,4},{6,7},{7,6},{8,9},{9,8},{10,11... | collective-permute-start | bytes 1474568 | tf_op jit(solution)/shard_map/ppermute | solution.py:449
  10.0 7.8 %copy-start.10 = (f32[8]{0:T(128)}, f32[8]{0:T(128)S(1)}, u32[]{:S(2)}) copy-start(f32[8]{0:T(128)S(1)} %add_convert_fusion) | copy-start | bytes 100
  17.9 6.3 %copy-start.1 = (bf16[48,80,128]{2,1,0:T(8,128)(2,1)S(1)}, bf16[48,80,128]{2,1,0:T(8,128)(2,1)}, u32[]{:S(2)}) copy-start(bf16[48,80,128]{2,1,0:T(8,128)(2,1)} %own.1) | copy-start | bytes 2949124
  18.8 3.3 %copy-start.9 = (s32[180]{0:T(256)S(1)}, s32[180]{0:T(256)}, u32[]{:S(2)}) copy-start(s32[180]{0:T(256)} %and_select_fusion) | copy-start | bytes 2164
  24.2 10.2 %copy-start.8 = (f32[768]{0:T(1024)S(1)}, f32[768]{0:T(1024)}, u32[]{:S(2)}) copy-start(f32[768]{0:T(1024)} %fusion.32) | copy-start | bytes 9220
  27.6 8.9 %copy-start.11 = (f32[8]{0:T(128)S(1)}, f32[8]{0:T(128)}, u32[]{:S(2)}) copy-start(f32[8]{0:T(128)} %get-tuple-element.15) | copy-start | bytes 100
  27.6 9.0 %copy-start.7 = (f32[768]{0:T(1024)S(1)}, f32[768]{0:T(1024)}, u32[]{:S(2)}) copy-start(f32[768]{0:T(1024)} %fusion.30) | copy-start | bytes 9220
  27.6 9.0 %copy-start.6 = (f32[768]{0:T(1024)S(1)}, f32[768]{0:T(1024)}, u32[]{:S(2)}) copy-start(f32[768]{0:T(1024)} %broadcast_multiply_fusion) | copy-start | bytes 9220
  27.6 30.1 %all-to-all-start = ((bf16[16,90,2,128]{3,2,1,0:T(2,128)(2,1)}), bf16[16,90,2,128]{3,2,1,0:T(2,128)(2,1)}, u32[]{:S(2)}, u32[]{:S(2)}) async-start(bf16[16,90,2,128]{3,2,1,0:T(2,128)(2,1)} %bitcast.1), calls=%async_computation | async-start | bytes 1474560 | tf_op jit(solution)/shard_map/all_to_all | solution.py:430
  35.6 4.2 %copy-start.4 = (bf16[256,256]{1,0:T(8,128)(2,1)S(1)}, bf16[256,256]{1,0:T(8,128)(2,1)}, u32[]{:S(2)}) copy-start(bf16[256,256]{1,0:T(8,128)(2,1)} %param.10) | copy-start | bytes 393220
  35.6 4.2 %copy-start.5 = (bf16[80,256]{1,0:T(8,128)(2,1)S(1)}, bf16[80,256]{1,0:T(8,128)(2,1)}, u32[]{:S(2)}) copy-start(bf16[80,256]{1,0:T(8,128)(2,1)} %param.9) | copy-start | bytes 122884
  57.7 0.9 copy-start.3
  63.9 68.2 %copy-start.2 = (bf16[24,256,256]{2,1,0:T(8,128)(2,1)S(1)}, bf16[24,256,256]{2,1,0:T(8,128)(2,1)}, u32[]{:S(2)}) copy-start(bf16[24,256,256]{2,1,0:T(8,128)(2,1)} %spectral.1) | copy-start | bytes 9437188
  132.8 62.6 %copy-start = (bf16[1440,768]{1,0:T(8,128)(2,1)S(1)}, bf16[1440,768]{1,0:T(8,128)(2,1)}, u32[]{:S(2)}) copy-start(bf16[1440,768]{1,0:T(8,128)(2,1)} %multiply_convert_fusion.1.rest_0_.inverse) | copy-start | bytes 6635524

commit v8 on v7

--- a/solution.py
+++ b/solution.py
@@ -27,6 +27,7 @@
 ITEMS = 3
 PIECES = 2 * ITEMS * ROWS
 DEG = L // N_LON
+LIFT_PAD = 2304
 LATS = ROWS * N_DEV
 MIB = 1024 * 1024
 
@@ -114,13 +115,16 @@
     )(offsets, across, own, beside, weight)
 
 
-def lift_kernel(source, matrices, forward, *rest):
-    out, cols, packed, scratch, lifted, first, table, sems = rest[-8:]
+def lift_kernel(source, weights, forward, *rest):
+    out, cols, packed, scratch, lifted, first, matrices, table, sems = rest[-9:]
+    small = pltpu.make_async_copy(weights.at[: C + CIN], matrices, sems.at[2])
+    small.start()
     fetch = pltpu.make_async_copy(source, cols, sems.at[0])
     fetch.start()
     copy = pltpu.make_async_copy(forward, table, sems.at[1])
     copy.start()
     first[...] = jnp.zeros_like(first)
+    small.wait()
     for row in range(ROWS):
         first[row, row * CIN : (row + 1) * CIN] = matrices[C:]
     fetch.wait()
@@ -144,8 +148,7 @@
     return pl.pallas_call(
         lift_kernel,
         out_shape=jax.ShapeDtypeStruct((N_DEV * PIECES, 128), jnp.bfloat16),
-        in_specs=[pl.BlockSpec(memory_space=pl.ANY), whole()]
-        + [pl.BlockSpec(memory_space=pl.ANY)] * (1 + len(tables)),
+        in_specs=[pl.BlockSpec(memory_space=pl.ANY)] * (3 + len(tables)),
         out_specs=whole(),
         scratch_shapes=[
             pltpu.VMEM((2 * NLON, 128), jnp.bfloat16),
@@ -153,8 +156,9 @@
             pltpu.VMEM((N_DEV * PIECES, 128), jnp.float32),
             pltpu.VMEM((NLON, ROWS * C), jnp.bfloat16),
             pltpu.VMEM((ROWS, C, C), jnp.bfloat16),
+            pltpu.VMEM((C + CIN, C), jnp.bfloat16),
             pltpu.VMEM((ITEMS * N_DEV, NLON), jnp.bfloat16),
-            pltpu.SemaphoreType.DMA((2,)),
+            pltpu.SemaphoreType.DMA((3,)),
         ],
         compiler_params=params(48),
         name="lift",
@@ -456,7 +460,7 @@
         [offsets.reshape(LAT_DEV * K), (odd * (RIM + SRC_DEV)).reshape(1).astype(jnp.int32)]
     )
     forward = fourier(0)
-    matrices = jnp.concatenate([lift_out, lift_in], axis=0)
+    matrices = jnp.pad(jnp.concatenate([lift_out, lift_in], axis=0), ((0, LIFT_PAD), (0, 0)))
     inverse = fourier(1)
     weighted, plain = legendre(chip)
     columns = remap(places, across, cube_cells, beside, block_weight)

time: 261 us -> 261 us (level)
  other arithmetic: 15.8 us -> 11 us
  starting transfers between devices: 15.4 us -> 19.6 us
    all_to_all x1, starting transfers between devices: 6.71 us -> 11 us  [exchange(): pairs = lax.all_to_all(pairs, axes, split_axis=0, concat_axis=0, tiled=True)]
  transfers between devices with their start and end apart: 3 -> 3, of which waited for: 1 -> 1; matrix products, arithmetic and copies ran while one was open for 8% -> 6% of each run, Pallas kernels for 1% -> 1%
where the time goes in v8:
time: 261 us
  blocking collectives  191 us (73%)
  starting transfers between devices  19.6 us (8%)
  Pallas kernels  18.1 us (7%)
  waiting for transfers between devices  12.5 us (5%)
  other arithmetic  11 us (4%)
  local copies, waits for them, and re-layouts  8.66 us (3%)
    all_to_all x3, blocking collectives, exchange(): pairs = lax.all_to_all(pairs, axes, split_axis=0, concat_axis=0, tiled=True)  141 us
    all_to_all x2, blocking collectives, regroup(): lax.all_to_all(values, 'lon', split_axis=0, concat_axis=0, tiled=True)  50.1 us
    all_to_all x1, waiting for transfers between devices, exchange(): pairs = lax.all_to_all(pairs, axes, split_axis=0, concat_axis=0, tiled=True)  12.5 us
    all_to_all x1, starting transfers between devices, exchange(): pairs = lax.all_to_all(pairs, axes, split_axis=0, concat_axis=0, tiled=True)  11 us
    convert_element_type x2, other arithmetic, fourier(): return (total * angle).astype(jnp.bfloat16)  9.63 us
    ppermute x1, starting transfers between devices, shards(): lax.ppermute(lax.dynamic_slice_in_dim(cube_cells, (1 - odd) * far, RIM, 0...  6.83 us
    pallas_call x1, Pallas kernels, lift(): pl.pallas_call(lift_kernel, out_shape=jax.ShapeDtypeStruct((N_DEV * PIECE...  5.43 us
  transfers between devices with their start and end apart: 3, of which 1 were waited for; matrix products, arithmetic and copies ran while one was open for 6% of the time, Pallas kernels for 1%

profile of v8, /device:TPU:33, one launch (start us, length us, event | category | flops | bytes accessed | tf_op | source)
XLA Modules:
  0.0 261.0 jit_solution(12049613576791091939)
XLA Ops:
  0.0 2.0 constant_dynamic-slice_fusion
  2.0 1.8 collective-permute-start
  3.8 6.8 %collective-permute-start.1 = (bf16[24,80,128]{2,1,0:T(8,128)(2,1)S(1)}, bf16[24,80,128]{2,1,0:T(8,128)(2,1)S(1)}, u32[]{:S(2)}, u32[]{:S(2)}) collective-permute-start(bf16[24,80,128]{2,1,0:T(8,128)(2,1)S(1)} %get-tuple-element.9), channel_id=1, source_target_pairs={{0,1},{1,0},{2,3},{3,2},{4,5},{5,4},{6,7},{7,6},{8,9},{9,8},{10,11... | collective-permute-start | bytes 1474568 | tf_op jit(solution)/shard_map/ppermute | solution.py:453
  10.7 0.1 compare_select_fusion.3
  10.8 0.7 add_remainder_fusion
  11.5 0.1 copy.10
  11.6 0.1 rem.194
  11.7 0.1 compare_select_fusion
  11.8 4.7 %multiply_convert_fusion.1.rest_0_.inverse = bf16[1440,768]{1,0:T(8,128)(2,1)} fusion(f32[768]{0:T(1024)S(1)} %fusion.18, f32[768]{0:T(1024)S(1)} %fusion.16, f32[1440]{0:T(1024)S(1)} %iota_convert_fusion), kind=kLoop, calls=%fused_computation.7 | loop fusion | flops 24330240 | bytes 2223744 | tf_op jit(solution)/shard_map/convert_element_type | solution.py:429
  16.5 0.1 divide_sqrt_fusion
  16.6 0.1 pad_add_fusion.offsets
  16.7 0.1 copy.12
  16.8 0.1 copy.13
  16.9 0.0 copy-start.3
  16.9 0.1 copy.14
  17.1 3.4 %copy.11.weight = bf16[45,1,4,90,128]{4,3,2,1,0:T(8,128)(2,1)S(1)} copy(bf16[45,1,4,90,128]{4,2,3,1,0:T(4,128)(2,1)} %param.8) | data formatting | bytes 8294400 | tf_op args[2]
  20.4 0.1 fusion.35
  20.5 0.1 fusion.33
  20.5 0.1 exponential_select_fusion
  20.6 0.0 collective-permute-done.across
  20.6 0.0 collective-permute-done.1.beside
  20.7 0.0 copy-done.3
  20.7 3.4 %remap.1 = bf16[2880,128]{1,0:T(8,128)(2,1)} custom-call(s32[181]{0:T(256)S(1)} %pad_add_fusion.offsets, bf16[24,80,128]{2,1,0:T(8,128)(2,1)S(1)} %collective-permute-done.across, bf16[48,80,128]{2,1,0:T(8,128)(2,1)S(1)} %copy-done.3, bf16[24,80,128]{2,1,0:T(8,128)(2,1)S(1)} %collective-permute-done.1.beside, bf16[45,1,4,90,128]{4,3,2,1,0:T(8,128)(2,1)S(1)} %copy.11.weight), custom_call_target="tpu_custom_call" | custom-call | tf_op jit(solution)/shard_map/remap/pallas_call | solution.py:93
  24.1 11.0 %all-to-all-start = ((bf16[16,90,2,128]{3,2,1,0:T(2,128)(2,1)}), bf16[16,90,2,128]{3,2,1,0:T(2,128)(2,1)}, u32[]{:S(2)}, u32[]{:S(2)}) async-start(bf16[16,90,2,128]{3,2,1,0:T(2,128)(2,1)} %bitcast.1), calls=%async_computation | async-start | bytes 1474560 | tf_op jit(solution)/shard_map/all_to_all | solution.py:434
  35.1 0.1 broadcast_multiply_fusion
  35.1 0.5 broadcast_in_dim.30.rise
  35.6 0.0 copy-start.5
  35.6 0.0 copy-start.6
  35.6 0.5 broadcast_in_dim.31.fall
  36.1 0.5 broadcast_in_dim.32.start
  36.6 0.1 broadcast_in_dim.34.factor
  36.6 3.1 %legendre.1 = (bf16[3,384,768]{2,1,0:T(8,128)(2,1)S(1)}, bf16[3,768,384]{2,1,0:T(8,128)(2,1)S(1)}) custom-call(f32[384,8,128]{2,1,0:T(8,128)S(1)} %broadcast_in_dim.30.rise, f32[384,8,128]{2,1,0:T(8,128)S(1)} %broadcast_in_dim.31.fall, f32[384,8,128]{2,1,0:T(8,128)S(1)} %broadcast_in_dim.32.start, f32[8,768]{1,0:T(8,128)S(1)} %get-tuple-element.12.initial, ...), custom_call_target="tpu_custom_call" | custom-call | tf_op jit(solution)/shard_map/legendre/pallas_call | solution.py:236
  39.8 0.0 copy-start.1
  39.8 1.2 copy-done.1
  41.0 0.0 copy-done.5
  41.0 0.0 copy-done.6
  41.0 0.1 fusion.8.weights
  41.1 5.0 %multiply_convert_fusion.forward = bf16[768,1440]{1,0:T(8,128)(2,1)} fusion(f32[768]{0:T(1024)S(1)} %fusion.18, f32[768]{0:T(1024)S(1)} %fusion.16, f32[1440]{0:T(1024)S(1)} %iota_convert_fusion), kind=kLoop, calls=%fused_computation | loop fusion | flops 24330240 | bytes 2223744 | tf_op jit(solution)/shard_map/convert_element_type | solution.py:429
  46.0 12.5 %all-to-all-done = bf16[16,90,2,128]{3,2,1,0:T(2,128)(2,1)} async-done(((bf16[16,90,2,128]{3,2,1,0:T(2,128)(2,1)}), bf16[16,90,2,128]{3,2,1,0:T(2,128)(2,1)}, u32[]{:S(2)}, u32[]{:S(2)}) %all-to-all-start) | async-done | bytes 737312 | tf_op jit(solution)/shard_map/all_to_all | solution.py:434
  58.5 5.4 %lift.1 = bf16[4608,128]{1,0:T(8,128)(2,1)S(1)} custom-call(bf16[2880,128]{1,0:T(8,128)(2,1)} %bitcast.2.source, bf16[2640,256]{1,0:T(8,128)(2,1)S(1)} %fusion.8.weights, bf16[768,1440]{1,0:T(8,128)(2,1)} %multiply_convert_fusion.forward, bf16[1440,768]{1,0:T(8,128)(2,1)} %multiply_convert_fusion.1.rest_0_.inverse, ...), custom_call_target="tpu_custom_call" | custom-call | tf_op jit(solution)/shard_map/lift/pallas_call | solution.py:148
  63.9 0.0 copy-start.4
  63.9 40.3 %all_to_all.30 = bf16[256,9,2,128]{3,2,1,0:T(2,128)(2,1)S(1)} all-to-all(bf16[256,9,2,128]{3,2,1,0:T(2,128)(2,1)S(1)} %bitcast.13), channel_id=1, replica_groups=mesh['lat'=16,'lon'=16] {'lat','lon'}, dimensions={0} | all-to-all | bytes 2359296 | tf_op jit(solution)/shard_map/all_to_all | solution.py:434
  104.3 0.0 copy-start.2
  104.3 0.8 analyse.1
  105.0 27.1 %all_to_all.31.pieces = bf16[16,72,256]{2,1,0:T(8,128)(2,1)S(1)} all-to-all(bf16[16,72,256]{2,1,0:T(8,128)(2,1)S(1)} %analyse.1), channel_id=1, replica_groups=mesh['lat'=16,'lon'=16] {'lon'}, dimensions={0} | all-to-all | bytes 1179648 | tf_op jit(solution)/shard_map/all_to_all | solution.py:439
  132.1 0.0 copy-done.4
  132.1 0.8 mix.1
  132.9 0.0 copy-start
  132.9 23.0 %all_to_all.32.pieces = bf16[16,72,256]{2,1,0:T(8,128)(2,1)S(1)} all-to-all(bf16[16,72,256]{2,1,0:T(8,128)(2,1)S(1)} %mix.1), channel_id=1, replica_groups=mesh['lat'=16,'lon'=16] {'lon'}, dimensions={0} | all-to-all | bytes 1179648 | tf_op jit(solution)/shard_map/all_to_all | solution.py:439
  155.9 0.0 copy-done.2
  155.9 0.8 synthesise.1
  156.8 38.7 %all_to_all.33 = bf16[256,9,2,128]{3,2,1,0:T(2,128)(2,1)S(1)} all-to-all(bf16[256,9,2,128]{3,2,1,0:T(2,128)(2,1)S(1)} %bitcast.15), channel_id=1, replica_groups=mesh['lat'=16,'lon'=16] {'lat','lon'}, dimensions={0} | all-to-all | bytes 2359296 | tf_op jit(solution)/shard_map/all_to_all | solution.py:434
  195.5 0.0 copy-done
  195.5 2.2 invert.1
  197.7 61.6 %all_to_all.34 = bf16[16,270,2,128]{3,2,1,0:T(2,128)(2,1)S(1)} all-to-all(bf16[16,270,2,128]{3,2,1,0:T(2,128)(2,1)S(1)} %bitcast.11), channel_id=1, replica_groups=mesh['lat'=16,'lon'=16] {'lon'}, dimensions={0} | all-to-all | bytes 4423680 | tf_op jit(solution)/shard_map/all_to_all | solution.py:434
  259.4 1.5 unpack.1
  (12 shorter events, 0.1 us)
Async XLA Ops:
  2.0 18.6 %collective-permute-start = (bf16[24,80,128]{2,1,0:T(8,128)(2,1)}, bf16[24,80,128]{2,1,0:T(8,128)(2,1)S(1)}, u32[]{:S(2)}, u32[]{:S(2)}) collective-permute-start(bf16[24,80,128]{2,1,0:T(8,128)(2,1)} %get-tuple-element.10), channel_id=1, source_target_pairs={{0,15},{1,2},{2,1},{3,4},{4,3},{5,6},{6,5},{7,8},{8,7},{9,10},{10,... | collective-permute-start | bytes 1474568 | tf_op jit(solution)/shard_map/ppermute | solution.py:448
  3.8 16.9 %collective-permute-start.1 = (bf16[24,80,128]{2,1,0:T(8,128)(2,1)S(1)}, bf16[24,80,128]{2,1,0:T(8,128)(2,1)S(1)}, u32[]{:S(2)}, u32[]{:S(2)}) collective-permute-start(bf16[24,80,128]{2,1,0:T(8,128)(2,1)S(1)} %get-tuple-element.9), channel_id=1, source_target_pairs={{0,1},{1,0},{2,3},{3,2},{4,5},{5,4},{6,7},{7,6},{8,9},{9,8},{10,11... | collective-permute-start | bytes 1474568 | tf_op jit(solution)/shard_map/ppermute | solution.py:453
  16.9 3.7 %copy-start.3 = (bf16[48,80,128]{2,1,0:T(8,128)(2,1)S(1)}, bf16[48,80,128]{2,1,0:T(8,128)(2,1)}, u32[]{:S(2)}) copy-start(bf16[48,80,128]{2,1,0:T(8,128)(2,1)} %own.1) | copy-start | bytes 2949124
  24.1 34.4 %all-to-all-start = ((bf16[16,90,2,128]{3,2,1,0:T(2,128)(2,1)}), bf16[16,90,2,128]{3,2,1,0:T(2,128)(2,1)}, u32[]{:S(2)}, u32[]{:S(2)}) async-start(bf16[16,90,2,128]{3,2,1,0:T(2,128)(2,1)} %bitcast.1), calls=%async_computation | async-start | bytes 1474560 | tf_op jit(solution)/shard_map/all_to_all | solution.py:434
  35.6 5.4 %copy-start.5 = (bf16[256,256]{1,0:T(8,128)(2,1)S(1)}, bf16[256,256]{1,0:T(8,128)(2,1)}, u32[]{:S(2)}) copy-start(bf16[256,256]{1,0:T(8,128)(2,1)} %param.10) | copy-start | bytes 393220
  35.6 5.4 %copy-start.6 = (bf16[80,256]{1,0:T(8,128)(2,1)S(1)}, bf16[80,256]{1,0:T(8,128)(2,1)}, u32[]{:S(2)}) copy-start(bf16[80,256]{1,0:T(8,128)(2,1)} %param.9) | copy-start | bytes 122884
  39.8 1.2 copy-start.1
  63.9 68.2 %copy-start.4 = (bf16[24,256,256]{2,1,0:T(8,128)(2,1)S(1)}, bf16[24,256,256]{2,1,0:T(8,128)(2,1)}, u32[]{:S(2)}) copy-start(bf16[24,256,256]{2,1,0:T(8,128)(2,1)} %spectral.1) | copy-start | bytes 9437188
  104.3 51.7 %copy-start.2 = (bf16[3,768,384]{2,1,0:T(8,128)(2,1)S(1)}, bf16[3,768,384]{2,1,0:T(8,128)(2,1)}, u32[]{:S(2)}) copy-start(bf16[3,768,384]{2,1,0:T(8,128)(2,1)} %copy-done.1) | copy-start | bytes 5308420
  132.9 62.6 %copy-start = (bf16[1440,768]{1,0:T(8,128)(2,1)S(1)}, bf16[1440,768]{1,0:T(8,128)(2,1)}, u32[]{:S(2)}) copy-start(bf16[1440,768]{1,0:T(8,128)(2,1)} %multiply_convert_fusion.1.rest_0_.inverse) | copy-start | bytes 6635524
